TPU v7x, 256 devices: a whole 4x4x8 slice. The times are simulated.
256 devices in a mesh: dp: 16 (over x, y_lo, core), mp: 16 (over z, y_hi).
Axes of the slice: x: 4, y: 4 (y_hi: 2, y_lo: 2; y = y_hi * 2 + y_lo), z: 8, core: 2. Of those that a mesh axis runs over, the one named last changes fastest.
Arguments:
- tokens: bfloat16 [4096, 6144], P('dp'), may hold values from -6 to 6
- w_qkv: bfloat16 [6144, 3, 4096], P('dp', None, 'mp'), as said below
- w_out: bfloat16 [6144, 4096], P('dp', 'mp'), may hold values from -0.09375 to 0.09375
- layer_norm_gain: float32 [6144], replicated, may hold values from 0.1 to 1.9
- query_gain: float32 [4096], P('mp'), may hold values from 0.1 to 1.9
- key_gain: float32 [4096], P('mp'), may hold values from 0.1 to 1.9
- cotangent: bfloat16 [4096, 6144], P('dp'), may hold values from -6 to 6
Outputs:
- branch: bfloat16 [4096, 6144], P('dp', 'mp')
- token_gradient: bfloat16 [4096, 6144], P('dp', 'mp')
- grad_qkv_weight: bfloat16 [6144, 3, 4096], P('dp', None, 'mp')
- grad_out_weight: bfloat16 [6144, 4096], P('dp', 'mp')
Inputs may be any that keep to these rules, and one draw needn't show every extreme that they name: `w_qkv`: entries are of order 6144^-0.5.
All inputs are finite; a program needn't handle non-finite values.
Results may differ from a plain program's by a relative error of at most 0.035.
Values may be sent and summed in bfloat16 or wider, within the bound.
No kernel may reach another device: no remote copies, remote signals or barrier semaphores. Data moves between devices by JAX's collectives and lax.ppermute only.
A program may use at most 128 MiB of HBM per device.

v0:
```python
import jax
import jax.numpy as jnp
from jax import lax
from jax.sharding import PartitionSpec as P

DH = 128


EPS = 1e-06


def head_stats(values, heads):
    shaped = values.reshape(values.shape[0], heads, -1)
    centered_input = shaped - jnp.mean(shaped, -1, keepdims=True)
    spread = lax.rsqrt(jnp.mean(centered_input * centered_input, -1, keepdims=True) + EPS)
    return (centered_input * spread, spread)


def head_back(grad, normed, spread, gain):
    scaled_input = grad * gain.reshape(normed.shape[1], -1)
    return (
        scaled_input
        - jnp.mean(scaled_input, -1, keepdims=True)
        - normed * jnp.mean(scaled_input * normed, -1, keepdims=True)
    ) * spread


def local(tokens, w_qkv, w_out, layer_norm_gain, query_gain, key_gain, cotangent):
    rows = tokens.shape[0]
    width = w_out.shape[1]
    heads = width // DH
    scale = DH ** (-0.5)
    features = tokens.astype(jnp.float32)
    model_width = features.shape[1]
    centered_input = features - jnp.mean(features, -1, keepdims=True)
    spread = lax.rsqrt(jnp.mean(centered_input * centered_input, -1, keepdims=True) + EPS)
    normed = centered_input * spread
    hidden_state = (normed * layer_norm_gain).astype(jnp.bfloat16)
    full_qkv = lax.all_gather(w_qkv, "dp", axis=0, tiled=True)
    projected = jnp.einsum(
        "td,dch->tch", hidden_state, full_qkv, preferred_element_type=jnp.float32
    )
    query_normed, query_spread = head_stats(projected[:, 0], heads)
    key_normed, key_spread = head_stats(projected[:, 1], heads)
    queries = (query_normed * query_gain.reshape(heads, DH)).astype(jnp.bfloat16)
    keys = (key_normed * key_gain.reshape(heads, DH)).astype(jnp.bfloat16)
    values = projected[:, 2].reshape(rows, heads, DH).astype(jnp.bfloat16)
    scores = jnp.einsum("qhd,khd->hqk", queries, keys, preferred_element_type=jnp.float32) * scale
    expd = jnp.exp(scores)
    probs = expd / jnp.sum(expd, -1, keepdims=True)
    pweights = probs.astype(jnp.bfloat16)
    attended = (
        jnp.einsum("hqk,khd->qhd", pweights, values, preferred_element_type=jnp.float32)
        .astype(jnp.bfloat16)
        .reshape(rows, width)
    )
    full_out = lax.all_gather(w_out, "dp", axis=0, tiled=True)
    branch_terms = jnp.einsum("th,dh->td", attended, full_out, preferred_element_type=jnp.float32)
    branch = lax.psum_scatter(
        branch_terms.astype(jnp.bfloat16), "mp", scatter_dimension=1, tiled=True
    )
    block = cotangent
    grad_out_weight = lax.psum_scatter(
        jnp.einsum("td,th->dh", block, attended, preferred_element_type=jnp.float32).astype(
            jnp.bfloat16
        ),
        "dp",
        scatter_dimension=0,
        tiled=True,
    )
    grad_att = (
        jnp.einsum("td,dh->th", cotangent, full_out, preferred_element_type=jnp.float32)
        .astype(jnp.bfloat16)
        .reshape(rows, heads, DH)
    )
    grad_probs = jnp.einsum("qhd,khd->hqk", grad_att, values, preferred_element_type=jnp.float32)
    delta = jnp.sum(probs * grad_probs, -1, keepdims=True)
    grad_scores = (probs * (grad_probs - delta) * scale).astype(jnp.bfloat16)
    grad_qn = jnp.einsum("hqk,khd->qhd", grad_scores, keys, preferred_element_type=jnp.float32)
    grad_kn = jnp.einsum("hqk,qhd->khd", grad_scores, queries, preferred_element_type=jnp.float32)
    grad_values = jnp.einsum("hqk,qhd->khd", pweights, grad_att, preferred_element_type=jnp.float32)
    grad_query = head_back(grad_qn, query_normed, query_spread, query_gain)
    grad_key = head_back(grad_kn, key_normed, key_spread, key_gain)
    grad_qkv = (
        jnp.stack([grad_query, grad_key, grad_values], 1)
        .reshape(rows, 3, width)
        .astype(jnp.bfloat16)
    )
    block = hidden_state
    grad_weight_sum = lax.psum_scatter(
        jnp.einsum("td,tch->dch", block, grad_qkv, preferred_element_type=jnp.float32).astype(
            jnp.bfloat16
        ),
        "dp",
        scatter_dimension=0,
        tiled=True,
    )
    hidden_terms = jnp.einsum("tch,dch->td", grad_qkv, full_qkv, preferred_element_type=jnp.float32)
    grad_hidden = lax.psum_scatter(
        hidden_terms.astype(jnp.bfloat16), "mp", scatter_dimension=1, tiled=True
    ).astype(jnp.float32)
    local_width = grad_hidden.shape[1]
    offset = lax.axis_index("mp") * local_width
    gain_local = lax.dynamic_slice_in_dim(layer_norm_gain, offset, local_width, 0)
    normed_local = lax.dynamic_slice_in_dim(normed, offset, local_width, 1)
    scaled_input = grad_hidden * gain_local
    totals = lax.psum((jnp.sum(scaled_input, -1), jnp.sum(scaled_input * normed_local, -1)), "mp")
    mean_grad = totals[0][:, None] / model_width
    mean_cross = totals[1][:, None] / model_width
    token_gradient = ((scaled_input - mean_grad - normed_local * mean_cross) * spread).astype(
        jnp.bfloat16
    )
    return (branch, token_gradient, grad_weight_sum, grad_out_weight)


def solution(mesh):
    return jax.shard_map(
        local,
        mesh=mesh,
        in_specs=(
            P("dp", None),
            P("dp", None, "mp"),
            P("dp", "mp"),
            P(),
            P("mp"),
            P("mp"),
            P("dp", None),
        ),
        out_specs=(P("dp", "mp"), P("dp", "mp"), P("dp", None, "mp"), P("dp", "mp")),
        check_vma=False,
    )
```

profile of v0, /device:TPU:16, one launch (start us, length us, event | category | flops | bytes accessed | tf_op | source)
XLA Modules:
  0.0 731.2 jit_solution(7465279633164921483)
XLA Ops:
  7.2 2.3 copy.26
  10.3 2.4 convert_reduce_fusion
  12.7 2.9 fusion.5
  15.6 57.1 %all-gather.3.cloned.1.call-done = bf16[6144,3,256]{0,2,1:T(8,128)(2,1)} async-done(((bf16[384,3,256]{0,2,1:T(8,128)(2,1)}), bf16[6144,3,256]{0,2,1:T(8,128)(2,1)}) %all-gather.3.cloned.1.call-update) | async-done | bytes 9437200 | tf_op jit(solution)/shard_map/all_gather | solution.py:39
  72.7 6.5 fusion.19
  86.5 27.2 %all-gather.5.cloned.1.call-done = bf16[6144,256]{1,0:T(8,128)(2,1)} async-done(((bf16[384,256]{1,0:T(8,128)(2,1)}), bf16[6144,256]{1,0:T(8,128)(2,1)}) %all-gather.5.cloned.1.call-update) | async-done | bytes 3145744 | tf_op jit(solution)/shard_map/all_gather | solution.py:57
  113.7 4.6 convolution_convert_fusion.2
  118.3 4.7 copy.52
  123.1 3.9 convolution_convert_fusion.5
  127.0 2.2 convolution_convert_fusion.3
  130.9 2.1 fusion.23
  135.0 3.3 fusion.39
  143.1 3.2 fusion.40
  149.6 8.2 %fusion.1 = bf16[256,6144]{1,0:T(8,128)(2,1)} fusion(bf16[6144,3,256]{0,2,1:T(8,128)(2,1)} %all-gather.3.cloned.1.call-done, bf16[256,1,256]{2,0,1:T(8,128)(2,1)} %copy.37, bf16[256,1,256]{2,0,1:T(8,128)(2,1)S(1)} %copy.36, bf16[256,1,256]{2,0,1:T(8,128)(2,1)} %copy.35), kind=kOutput, calls=%fused_computation.7 | convolution fusion | flops 2417885184 | bytes 12976128 | tf_op jit(solution)/shard_map/tch,dch->td/dot_general | solution.py:98
  157.8 4.7 copy.54
  162.7 2.7 fusion.4
  165.4 4.7 copy.56
  170.2 8.6 %convolution_convert_fusion = bf16[6144,3,256]{2,0,1:T(8,128)(2,1)} fusion(f32[6144]{0:T(1024)} %param.10, bf16[256,1,256]{2,0,1:T(8,128)(2,1)S(1)} %copy-done.3, bf16[256,1,256]{2,0,1:T(8,128)(2,1)S(1)} %copy-done.6, bf16[256,1,256]{2,0,1:T(8,128)(2,1)S(1)} %copy-done.4, bf16[256,6144]{1,0:T(8,128)(2,1)} %param.7, f32[256]{0:T(256)S(1)} %copy-done.8, ...), kind=kOutput, calls=%fused_computation.1 | convolution fusion | flops 2429681664 | bytes 13002752 | tf_op jit(solution)/shard_map/td,tch->dch/dot_general | solution.py:91
  179.7 5.7 fusion.2
  185.4 146.7 %reduce-scatter.13.cloned.1.call-done = bf16[384,256]{1,0:T(8,128)(2,1)} async-done(((bf16[6144,256]{1,0:T(8,128)(2,1)}), bf16[384,256]{1,0:T(8,128)(2,1)}) %reduce-scatter.13.cloned.1.call-update) | async-done | bytes 196624
  333.8 210.6 %reduce-scatter.15.cloned.1.call-done = bf16[384,256]{1,0:T(8,128)(2,1)} async-done(((bf16[6144,256]{1,0:T(8,128)(2,1)}), bf16[384,256]{1,0:T(8,128)(2,1)}) %reduce-scatter.15.cloned.1.call-update) | async-done | bytes 196624
  546.7 39.2 %all-reduce = (f32[256]{0:T(256)S(1)}, f32[256]{0:T(256)S(1)}) all-reduce(f32[256]{0:T(256)S(1)} %get-tuple-element.17, f32[256]{0:T(256)S(1)} %get-tuple-element.16), channel_id=1, replica_groups=mesh['dp'=16,'mp'=16] {'mp'}, use_global_device_ids=true, to_apply=%region_17.0 | all-reduce | flops 512 | bytes 4096 | tf_op jit(solution)/shard_map/psum | solution.py:107
  587.8 27.3 %reduce-scatter.17.cloned.1.call-done = bf16[384,256]{1,0:T(8,128)(2,1)} async-done(((bf16[6144,256]{1,0:T(8,128)(2,1)}), bf16[384,256]{1,0:T(8,128)(2,1)}) %reduce-scatter.17.cloned.1.call-update) | async-done | bytes 196624
  615.0 109.4 %reduce-scatter.11.cloned.1.call-done = bf16[384,3,256]{2,0,1:T(8,128)(2,1)} async-done(((bf16[6144,3,256]{2,0,1:T(8,128)(2,1)}), bf16[384,3,256]{2,0,1:T(8,128)(2,1)}) %reduce-scatter.11.cloned.1.call-update) | async-done | bytes 589840 | tf_op jit(solution)/shard_map/reduce_scatter | solution.py:90
  (72 shorter events, 26.9 us)
Async XLA Ops:
  7.2 116.0 %copy-start = (bf16[256,6144]{1,0:T(8,128)(2,1)S(1)}, bf16[256,6144]{1,0:T(8,128)(2,1)}, u32[]{:S(2)}) copy-start(bf16[256,6144]{1,0:T(8,128)(2,1)} %param.13) | copy-start | bytes 9437188
  7.2 65.5 %copy-start.13 = (f32[6144]{0:T(1024)S(1)}, f32[6144]{0:T(1024)}, u32[]{:S(2)}) copy-start(f32[6144]{0:T(1024)} %param.10) | copy-start | bytes 73732
  7.2 65.5 %all-gather.3.cloned.1.call-start = ((), (), s32[]{:S(2)}) async-start(), calls=%async_computation.4 | async-start | bytes 10027008 | tf_op jit(solution)/shard_map/all_gather | solution.py:39
  9.5 104.2 %all-gather.5.cloned.1.call-start = ((), (), s32[]{:S(2)}) async-start(), calls=%async_computation.5 | async-start | bytes 3342336 | tf_op jit(solution)/shard_map/all_gather | solution.py:57
  10.3 321.8 %reduce-scatter.13.cloned.1.call-start = ((), (), s32[]{:S(2)}) async-start(), calls=%async_computation.7 | async-start | bytes 3342336
  12.7 66.5 %copy-start.9 = (f32[256]{0:T(256)}, f32[256]{0:T(256)S(1)}, u32[]{:S(2)}) copy-start(f32[256]{0:T(256)S(1)} %broadcast_multiply_fusion.8) | copy-start | bytes 3076
  15.6 63.6 %copy-start.7 = (f32[256]{0:T(256)}, f32[256]{0:T(256)S(1)}, u32[]{:S(2)}) copy-start(f32[256]{0:T(256)S(1)} %add_rsqrt_fusion.2) | copy-start | bytes 3076
  15.6 67.1 %copy-start.11 = (f32[256]{0:T(256)S(1)}, f32[256]{0:T(256)}, u32[]{:S(2)}) copy-start(f32[256]{0:T(256)} %param.11) | copy-start | bytes 3076
  15.6 67.1 %copy-start.12 = (f32[256]{0:T(256)S(1)}, f32[256]{0:T(256)}, u32[]{:S(2)}) copy-start(f32[256]{0:T(256)} %param.12) | copy-start | bytes 3076
  83.9 1.1 copy-start.1
  83.9 1.1 copy-start.2
  123.1 421.4 %reduce-scatter.15.cloned.1.call-start = ((), (), s32[]{:S(2)}) async-start(), calls=%async_computation.8 | async-start | bytes 3342336
  149.6 8.2 %copy-start.5 = (bf16[256,1,256]{2,0,1:T(8,128)(2,1)}, bf16[256,1,256]{2,0,1:T(8,128)(2,1)S(1)}, u32[]{:S(2)}) copy-start(bf16[256,1,256]{2,0,1:T(8,128)(2,1)S(1)} %copy.36) | copy-start | bytes 393220
  162.5 452.6 %reduce-scatter.17.cloned.1.call-start = ((), (), s32[]{:S(2)}) async-start(), calls=%async_computation.9 | async-start | bytes 3342336
  165.4 4.8 copy-start.3
  165.4 4.8 copy-start.4
  165.4 4.8 copy-start.6
  165.4 4.8 copy-start.8
  165.4 4.8 copy-start.10
  170.1 554.3 %reduce-scatter.11.cloned.1.call-start = ((), (), s32[]{:S(2)}) async-start(), calls=%async_computation.6 | async-start | bytes 10027008 | tf_op jit(solution)/shard_map/reduce_scatter | solution.py:90
Sparse Core Ops, SparseCore 0:
  10.4 62.2 all-gather.2
  74.5 39.1 all-gather.4
  123.2 208.8 reduce-scatter.12
  336.4 207.9 reduce-scatter.14
  547.4 67.5 reduce-scatter.16
  618.0 106.3 reduce-scatter.10
where the time goes:
time: 736 us; the launch traced here: 731 us
  waiting for transfers between devices  579 us (79%)
  matrix products  49.8 us (7%)
  blocking collectives  39.2 us (5%)
  local copies, waits for them, and re-layouts  25.8 us (4%)
  other arithmetic  22.6 us (3%)
  between operations  14.4 us (2%)
    unnamed x9, waiting for transfers between devices  385 us
    reduce_scatter x1, waiting for transfers between devices, local(): lax.psum_scatter(jnp.einsum('td,tch->dch', block, grad_qkv, preferred_ele...  109 us
    all_gather x1, waiting for transfers between devices, local(): full_qkv = lax.all_gather(w_qkv, 'dp', axis=0, tiled=True)  57.1 us
    psum x1, blocking collectives, local(): lax.psum((jnp.sum(scaled_input, -1), jnp.sum(scaled_input * normed_local,...  39.2 us
    all_gather x1, waiting for transfers between devices, local(): full_out = lax.all_gather(w_out, 'dp', axis=0, tiled=True)  27.2 us
    unnamed x34, local copies, waits for them, and re-layouts  19.3 us
  transfers between devices with their start and end apart: 6, of which 6 were waited for; matrix products, arithmetic and copies ran while one was open for 12% of the time, Pallas kernels for 0%

commit v1 on v0

v1 whole, which is shorter than its diff:
```python
import jax
import jax.numpy as jnp
from jax import lax
from jax.experimental import pallas as pl
from jax.experimental.pallas import tpu as pltpu
from jax.sharding import Mesh, PartitionSpec as P

DH = 128
EPS = 1e-06
DP = ("x", "yl", "c")
MP = ("z", "yh")
NX, NYL, NC, NZ, NYH = 4, 2, 2, 8, 2
NDP, NMP = NX * NYL * NC, NZ * NYH
ROWS = 256
SL = 384
HW = 256
D = 6144
SUB = ROWS // NZ
STEP = 2
KSTEP = 4
VMEM = 52 * 1024 * 1024
BF = jnp.bfloat16
F32 = jnp.float32


def dot(a, b, ca, cb):
    return lax.dot_general(a, b, (((ca,), (cb,)), ((), ())), preferred_element_type=F32)


def params():
    return pltpu.CompilerParams(vmem_limit_bytes=VMEM)


def normalise(t):
    mean = jnp.mean(t, -1, keepdims=True)
    cen = t - mean
    rstd = lax.rsqrt(jnp.mean(cen * cen, -1, keepdims=True) + EPS)
    return cen * rstd, mean, rstd


def norm_kernel(tok_ref, gain_ref, hid_ref, mean_ref, rstd_ref):
    xhat, mean, rstd = normalise(tok_ref[...].astype(F32))
    hid_ref[...] = (xhat * gain_ref[...]).astype(BF)
    mean_ref[...] = mean
    rstd_ref[...] = rstd


def norm_call(tokens, gain):
    blk = 64
    return pl.pallas_call(
        norm_kernel,
        grid=(ROWS // blk,),
        in_specs=[
            pl.BlockSpec((blk, D), lambda i: (i, 0)),
            pl.BlockSpec((1, D), lambda i: (0, 0)),
        ],
        out_specs=[
            pl.BlockSpec((blk, D), lambda i: (i, 0)),
            pl.BlockSpec((blk, 1), lambda i: (i, 0)),
            pl.BlockSpec((blk, 1), lambda i: (i, 0)),
        ],
        out_shape=[
            jax.ShapeDtypeStruct((ROWS, D), BF),
            jax.ShapeDtypeStruct((ROWS, 1), F32),
            jax.ShapeDtypeStruct((ROWS, 1), F32),
        ],
        compiler_params=params(),
        cost_estimate=pl.CostEstimate(flops=2 * 10**7, bytes_accessed=2 * ROWS * D * 2, transcendentals=0),
    )(tokens, gain.reshape(1, D))


def rows_kernel(z_ref, tok_ref, cot_ref, gain_ref, out_ref):
    xhat, _, _ = normalise(tok_ref[...].astype(F32))
    hid = (xhat * gain_ref[...]).astype(BF)
    for i in range(NDP):
        out_ref[i, 0] = hid[:, i * SL : (i + 1) * SL]
        out_ref[i, 1] = cot_ref[:, i * SL : (i + 1) * SL]


def rows_call(z, tokens, cotangent, gain):
    return pl.pallas_call(
        rows_kernel,
        grid_spec=pltpu.PrefetchScalarGridSpec(
            num_scalar_prefetch=1,
            grid=(1,),
            in_specs=[
                pl.BlockSpec((SUB, D), lambda i, z: (z[0], 0)),
                pl.BlockSpec((SUB, D), lambda i, z: (z[0], 0)),
                pl.BlockSpec((1, D), lambda i, z: (0, 0)),
            ],
            out_specs=pl.BlockSpec((NDP, 2, SUB, SL), lambda i, z: (0, 0, 0, 0)),
        ),
        out_shape=jax.ShapeDtypeStruct((NDP, 2, SUB, SL), BF),
        compiler_params=params(),
        cost_estimate=pl.CostEstimate(flops=10**6, bytes_accessed=4 * SUB * D * 2, transcendentals=0),
    )(z, tokens, cotangent, gain.reshape(1, D))


def head_stats(u):
    cen = u - jnp.mean(u, -1, keepdims=True)
    s = lax.rsqrt(jnp.mean(cen * cen, -1, keepdims=True) + EPS)
    return cen * s, s


def head_back(g, n, s, gain):
    e = g * gain
    return (e - jnp.mean(e, -1, keepdims=True) - n * jnp.mean(e * n, -1, keepdims=True)) * s


def attn_kernel(hid_ref, cot_ref, w_ref, qg_ref, kg_ref, *rest):
    out_ref, acc, acc_g = rest[-3:]
    i = pl.program_id(0)

    @pl.when(i == 0)
    def _():
        acc[...] = jnp.zeros_like(acc)
        acc_g[...] = jnp.zeros_like(acc_g)

    h = hid_ref[...]
    for j in range(3):
        acc[j] += dot(h, w_ref[:, j].reshape(KSTEP * SL, HW), 1, 0)
    acc_g[...] += dot(cot_ref[...], w_ref[:, 3].reshape(KSTEP * SL, HW), 1, 0)

    @pl.when(i == pl.num_programs(0) - 1)
    def _():
        scale = DH ** (-0.5)
        for hd in range(HW // DH):
            sl = slice(hd * DH, (hd + 1) * DH)
            qg = qg_ref[:, sl]
            kg = kg_ref[:, sl]
            qn, qs = head_stats(acc[0, :, sl])
            kn, ks = head_stats(acc[1, :, sl])
            q = (qn * qg).astype(BF)
            k = (kn * kg).astype(BF)
            v = acc[2, :, sl].astype(BF)
            ga = acc_g[:, sl].astype(BF)
            e = jnp.exp(dot(q, k, 1, 1) * scale)
            p = e / jnp.sum(e, -1, keepdims=True)
            pw = p.astype(BF)
            att = dot(pw, v, 1, 0).astype(BF)
            gp = dot(ga, v, 1, 1)
            delta = jnp.sum(p * gp, -1, keepdims=True)
            gs = (p * (gp - delta) * scale).astype(BF)
            gq = head_back(dot(gs, k, 1, 0), qn, qs, qg)
            gk = head_back(dot(gs, q, 0, 0), kn, ks, kg)
            gv = dot(pw, ga, 0, 0)
            for j, val in enumerate((gq, gk, gv)):
                out_ref[:, j * HW + hd * DH : j * HW + (hd + 1) * DH] = val.astype(BF)
            out_ref[:, 3 * HW + hd * DH : 3 * HW + (hd + 1) * DH] = att


def attn_call(hid, cot, w, qg, kg, after):
    return pl.pallas_call(
        attn_kernel,
        grid=(NDP // KSTEP,),
        in_specs=[
            pl.BlockSpec((ROWS, KSTEP * SL), lambda i: (0, i)),
            pl.BlockSpec((ROWS, KSTEP * SL), lambda i: (0, i)),
            pl.BlockSpec((KSTEP, 4, SL, HW), lambda i: (i, 0, 0, 0)),
            pl.BlockSpec((1, HW), lambda i: (0, 0)),
            pl.BlockSpec((1, HW), lambda i: (0, 0)),
        ]
        + [pl.BlockSpec(memory_space=pl.ANY)] * len(after),
        out_specs=pl.BlockSpec((ROWS, 4 * HW), lambda i: (0, 0)),
        out_shape=jax.ShapeDtypeStruct((ROWS, 4 * HW), BF),
        scratch_shapes=[pltpu.VMEM((3, ROWS, HW), F32), pltpu.VMEM((ROWS, HW), F32)],
        compiler_params=params(),
        cost_estimate=pl.CostEstimate(
            flops=2 * ROWS * D * 4 * HW, bytes_accessed=20 * 10**6, transcendentals=ROWS * ROWS * 2
        ),
    )(hid, cot, w, qg.reshape(1, HW), kg.reshape(1, HW), *after)


def branch_kernel(g_ref, w_ref, out_ref):
    for s in range(STEP):
        out_ref[s] = dot(g_ref[...], w_ref[s, 0], 1, 1).astype(BF)


def branch_call(g, w):
    return pl.pallas_call(
        branch_kernel,
        grid=(NDP // STEP,),
        in_specs=[
            pl.BlockSpec((ROWS, HW), lambda i: (0, 3)),
            pl.BlockSpec((STEP, 1, SL, HW), lambda i: (i, 3, 0, 0)),
        ],
        out_specs=pl.BlockSpec((STEP, ROWS, SL), lambda i: (i, 0, 0)),
        out_shape=jax.ShapeDtypeStruct((NDP, ROWS, SL), BF),
        compiler_params=params(),
        cost_estimate=pl.CostEstimate(
            flops=2 * ROWS * D * HW, bytes_accessed=6 * 10**6, transcendentals=0
        ),
    )(g, w)


def back_kernel(g_ref, w_ref, hid_ref, gain_ref, *rest):
    hp_ref, sum_ref, s1, s2 = rest[-4:]
    i = pl.program_id(0)

    @pl.when(i == 0)
    def _():
        s1[...] = jnp.zeros_like(s1)
        s2[...] = jnp.zeros_like(s2)

    for s in range(STEP):
        t = dot(g_ref[:, :HW], w_ref[s, 0], 1, 1)
        t += dot(g_ref[:, HW : 2 * HW], w_ref[s, 1], 1, 1)
        t += dot(g_ref[:, 2 * HW :], w_ref[s, 2], 1, 1)
        hp_ref[s] = t.astype(BF)
        a = t * gain_ref[s]
        b = t * hid_ref[:, s * SL : (s + 1) * SL].astype(F32)
        for c in range(SL // 128):
            s1[...] += a[:, c * 128 : (c + 1) * 128]
            s2[...] += b[:, c * 128 : (c + 1) * 128]

    @pl.when(i == pl.num_programs(0) - 1)
    def _():
        sum_ref[:, 0:1] = jnp.sum(s1[...], -1, keepdims=True)
        sum_ref[:, 1:2] = jnp.sum(s2[...], -1, keepdims=True)


def back_call(g, w, hid, gain, after):
    return pl.pallas_call(
        back_kernel,
        grid=(NDP // STEP,),
        in_specs=[
            pl.BlockSpec((ROWS, 3 * HW), lambda i: (0, 0)),
            pl.BlockSpec((STEP, 3, SL, HW), lambda i: (i, 0, 0, 0)),
            pl.BlockSpec((ROWS, STEP * SL), lambda i: (0, i)),
            pl.BlockSpec((STEP, 1, SL), lambda i: (i, 0, 0)),
        ]
        + [pl.BlockSpec(memory_space=pl.ANY)] * len(after),
        out_specs=[
            pl.BlockSpec((STEP, ROWS, SL), lambda i: (i, 0, 0)),
            pl.BlockSpec((ROWS, 2), lambda i: (0, 0)),
        ],
        out_shape=[
            jax.ShapeDtypeStruct((NDP, ROWS, SL), BF),
            jax.ShapeDtypeStruct((ROWS, 2), F32),
        ],
        scratch_shapes=[pltpu.VMEM((ROWS, 128), F32), pltpu.VMEM((ROWS, 128), F32)],
        compiler_params=params(),
        cost_estimate=pl.CostEstimate(
            flops=2 * ROWS * D * 3 * HW, bytes_accessed=16 * 10**6, transcendentals=0
        ),
    )(g, w, hid, gain.reshape(NDP, 1, SL), *after)


def weight_kernel(z_ref, x_ref, g_ref, dw_ref, do_ref, acc, acc_o):
    i = pl.program_id(0)

    @pl.when(i == 0)
    def _():
        acc[...] = jnp.zeros_like(acc)
        acc_o[...] = jnp.zeros_like(acc_o)

    g = g_ref[...].reshape(NDP * SUB, 4 * HW)
    acc[...] += dot(x_ref[0, :, 0].reshape(NDP * SUB, SL), g[:, : 3 * HW], 0, 0)
    acc_o[...] += dot(x_ref[0, :, 1].reshape(NDP * SUB, SL), g[:, 3 * HW :], 0, 0)

    @pl.when(i == pl.num_programs(0) - 1)
    def _():
        for j in range(3):
            dw_ref[j] = acc[:, j * HW : (j + 1) * HW].astype(BF)
        do_ref[...] = acc_o[...].astype(BF)


def weight_call(z, x, g):
    return pl.pallas_call(
        weight_kernel,
        grid_spec=pltpu.PrefetchScalarGridSpec(
            num_scalar_prefetch=1,
            grid=(NZ,),
            in_specs=[
                pl.BlockSpec((1, NDP, 2, SUB, SL), lambda i, z: (i, 0, 0, 0, 0)),
                pl.BlockSpec((NDP, 1, SUB, 4 * HW), lambda i, z: (0, (z[0] + NZ - i) % NZ, 0, 0)),
            ],
            out_specs=[
                pl.BlockSpec((3, SL, HW), lambda i, z: (0, 0, 0)),
                pl.BlockSpec((SL, HW), lambda i, z: (0, 0)),
            ],
            scratch_shapes=[pltpu.VMEM((SL, 3 * HW), F32), pltpu.VMEM((SL, HW), F32)],
        ),
        out_shape=[
            jax.ShapeDtypeStruct((3, SL, HW), BF),
            jax.ShapeDtypeStruct((SL, HW), BF),
        ],
        compiler_params=params(),
        cost_estimate=pl.CostEstimate(
            flops=2 * ROWS * D * 4 * HW, bytes_accessed=16 * 10**6, transcendentals=0
        ),
    )(z, x, g.reshape(NDP, NZ, SUB, 4 * HW))


def shift(a, k):
    return lax.ppermute(a, "z", [(i, (i + k) % NZ) for i in range(NZ)])


def swap_yh(a):
    return lax.ppermute(a, "yh", [(0, 1), (1, 0)])


def ring_gather(own):
    half = NDP // 2
    r1, l1 = shift(own, 1), shift(own, -1)
    r2, l2 = shift(r1, 1), shift(l1, -1)
    r3, l3 = shift(r2, 1), shift(l2, -1)
    far = jnp.concatenate([shift(r3[:half], 1), shift(l3[half:], -1)], 0)
    return jnp.stack([own, r1, r2, r3, far, l3, l2, l1], 0), (r3, l3)


def ring_sum(a, z):
    a = a.reshape(NZ, NYH, ROWS, SL)

    def block(k):
        return lax.dynamic_index_in_dim(a, lax.rem(z + k + NZ, NZ), 0, keepdims=False)

    far = block(4)
    p = shift(far[0], 1)
    m = shift(far[1], -1)
    u, v = block(3), block(-3)
    p = shift(jnp.stack([u[0] + p, u[1]]), 1)
    m = shift(jnp.stack([v[0], v[1] + m]), -1)
    p, m = shift(block(2) + p, 1), shift(block(-2) + m, -1)
    p, m = shift(block(1) + p, 1), shift(block(-1) + m, -1)
    return block(0).astype(F32) + p.astype(F32) + m.astype(F32)


def all_sum(a):
    x = jnp.broadcast_to(a.T[None], (NMP, 2, ROWS))
    return jnp.sum(lax.all_to_all(x, MP, 0, 0, tiled=True), 0)


def across(part, yh):
    mine = lax.dynamic_index_in_dim(part, yh, 0, keepdims=False)
    other = lax.dynamic_index_in_dim(part, 1 - yh, 0, keepdims=False)
    return mine.astype(F32) + swap_yh(other.astype(BF)).astype(F32)


def local(tokens, w_qkv, w_out, layer_norm_gain, query_gain, key_gain, cotangent):
    z = lax.axis_index("z")
    yh = lax.axis_index("yh")
    zs = z.reshape(1).astype(jnp.int32)
    col = (z * NYH + yh) * SL

    w_own = jnp.concatenate([w_qkv.transpose(1, 0, 2), w_out[None]], 0)
    w = lax.all_gather(w_own, DP, axis=0)
    side = lax.psum_scatter(w_own, "c", scatter_dimension=0, tiled=True)

    rows = rows_call(zs, tokens, cotangent, layer_norm_gain)
    rows, early = ring_gather(lax.all_to_all(rows, DP, 0, 0, tiled=True))
    hid, mean, rstd = norm_call(tokens, layer_norm_gain)

    grads = attn_call(hid, cotangent, w, query_gain, key_gain, early + (side,))
    all_grads = lax.all_gather(grads, DP, axis=0)
    branch_terms = branch_call(grads, w)
    branch_part = lax.psum_scatter(
        branch_terms.reshape(NDP * ROWS, SL), "z", scatter_dimension=0, tiled=True
    ).reshape(NYH, ROWS, SL)
    hidden_terms, sums = back_call(grads, w, hid, layer_norm_gain, (rows,))
    sums = all_sum(sums) / D
    grad_hidden = across(ring_sum(hidden_terms, z), yh)
    branch = across(branch_part, yh).astype(BF)

    gain = lax.dynamic_slice_in_dim(layer_norm_gain, col, SL, 0)
    toks = lax.dynamic_slice_in_dim(tokens, col, SL, 1).astype(F32)
    xhat = (toks - mean) * rstd
    token_gradient = (
        (grad_hidden * gain - sums[0][:, None] - xhat * sums[1][:, None]) * rstd
    ).astype(BF)

    grad_w, grad_o = weight_call(zs, rows, all_grads)
    return (branch, token_gradient, grad_w.transpose(1, 0, 2), grad_o)


def solution(mesh):
    fine = Mesh(mesh.devices.reshape(NX, NYL, NC, NZ, NYH), DP + MP)
    return jax.shard_map(
        local,
        mesh=fine,
        in_specs=(
            P(DP, None),
            P(DP, None, MP),
            P(DP, MP),
            P(),
            P(MP),
            P(MP),
            P(DP, None),
        ),
        out_specs=(P(DP, MP), P(DP, MP), P(DP, None, MP), P(DP, MP)),
        check_vma=False,
    )
```

time: 736 us -> 252 us (0.34)
  waiting for transfers between devices: 579 us -> 108 us
  matrix products: 49.8 us -> 0 us
  Pallas kernels: 0 us -> 46 us
  starting transfers between devices: 0.42 us -> 38.2 us
  blocking collectives: 39.2 us -> 18.3 us
  local copies, waits for them, and re-layouts: 25.8 us -> 13 us
  other arithmetic: 22.6 us -> 11.6 us
    unnamed x9 -> x4, waiting for transfers between devices: 385 us -> 1.08 us
    reduce_scatter x1 -> x2, waiting for transfers between devices: 109 us -> 0.01 us  [the longest x1 0.01 us: local(): side = lax.psum_scatter(w_own, 'c', scatter_dimension=0, tiled=True)]
    ppermute x0 -> x18, waiting for transfers between devices: none -> 100 us  [the longest x16 95.4 us: shift(): return lax.ppermute(a, 'z', [(i, (i + k) % NZ) for i in range(NZ)])]
    all_gather x2, waiting for transfers between devices: 84.3 us -> 0.01 us  [the longest x1 0.01 us: local(): w = lax.all_gather(w_own, DP, axis=0)]
    dot_general x12 -> x0, matrix products: 47.7 us -> none  [the longest x1 8.64 us: local(): jnp.einsum('td,tch->dch', block, grad_qkv, preferred_element_type=jnp.flo...]
    pallas_call x0 -> x6, Pallas kernels: none -> 46 us  [the longest x1 10.8 us: attn_call(): pl.pallas_call(attn_kernel, grid=(NDP // KSTEP,), in_specs=[pl.BlockSpec(...]
    psum x1 -> x0, blocking collectives: 39.2 us -> none  [local(): lax.psum((jnp.sum(scaled_input, -1), jnp.sum(scaled_input * normed_local,...]
    ppermute x0 -> x18, starting transfers between devices: none -> 33.3 us  [the longest x16 29.6 us: shift(): return lax.ppermute(a, 'z', [(i, (i + k) % NZ) for i in range(NZ)])]
  transfers between devices with their start and end apart: 6 -> 23, of which waited for: 6 -> 13; matrix products, arithmetic and copies ran while one was open for 12% -> 7% of each run, Pallas kernels for 0% -> 7%
where the time goes in v1:
time: 252 us; the launch traced here: 251 us
  waiting for transfers between devices  108 us (43%)
  Pallas kernels  46 us (18%)
  starting transfers between devices  38.2 us (15%)
  blocking collectives  18.3 us (7%)
  between operations  15.8 us (6%)
  local copies, waits for them, and re-layouts  13 us (5%)
  other arithmetic  11.6 us (5%)
    ppermute x16, waiting for transfers between devices, shift(): return lax.ppermute(a, 'z', [(i, (i + k) % NZ) for i in range(NZ)])  95.4 us
    ppermute x16, starting transfers between devices, shift(): return lax.ppermute(a, 'z', [(i, (i + k) % NZ) for i in range(NZ)])  29.6 us
    all_to_all x1, blocking collectives, local(): rows, early = ring_gather(lax.all_to_all(rows, DP, 0, 0, tiled=True))  18.3 us
    pallas_call x1, Pallas kernels, attn_call(): pl.pallas_call(attn_kernel, grid=(NDP // KSTEP,), in_specs=[pl.BlockSpec(...  10.8 us
    pallas_call x1, Pallas kernels, back_call(): pl.pallas_call(back_kernel, grid=(NDP // STEP,), in_specs=[pl.BlockSpec((...  10.5 us
    pallas_call x1, Pallas kernels, weight_call(): pl.pallas_call(weight_kernel, grid_spec=pltpu.PrefetchScalarGridSpec(num_...  10.4 us
    unnamed x24, local copies, waits for them, and re-layouts  9.6 us
    all_to_all x1, waiting for transfers between devices, all_sum(): return jnp.sum(lax.all_to_all(x, MP, 0, 0, tiled=True), 0)  7.14 us
  transfers between devices with their start and end apart: 23, of which 13 were waited for; matrix products, arithmetic and copies ran while one was open for 7% of the time, Pallas kernels for 7%

profile of v1, /device:TPU:16, one launch (start us, length us, event | category | flops | bytes accessed | tf_op | source)
XLA Modules:
  0.0 251.2 jit_solution(5938110155651196887)
XLA Ops:
  13.1 18.3 %all_to_all.10 = bf16[16,2,32,384]{3,2,1,0:T(8,128)(2,1)S(1)} all-to-all(bf16[16,2,32,384]{3,2,1,0:T(8,128)(2,1)S(1)} %shard_map.103), channel_id=1, replica_groups=mesh['x'=4,'yl'=2,'c'=2,'z'=8,'yh'=2] {'x','yl','c'}, dimensions={0} | all-to-all | bytes 1572864 | tf_op jit(solution)/shard_map/all_to_all | solution.py:351
  33.3 5.4 %collective-permute-start.3 = (bf16[16,2,32,384]{3,2,1,0:T(8,128)(2,1)S(1)}, bf16[16,2,32,384]{3,2,1,0:T(8,128)(2,1)S(1)}, u32[]{:S(2)}, u32[]{:S(2)}) collective-permute-start(bf16[16,2,32,384]{3,2,1,0:T(8,128)(2,1)S(1)} %all_to_all.10), channel_id=1, source_target_pairs={{0,14},{2,0},{4,2},{6,4},{8,6},{10,8},{12,10},{14,12},{1,15},{3,1}... | collective-permute-start | bytes 2359304 | tf_op jit(solution)/shard_map/ppermute | solution.py:296
  38.7 17.5 %collective-permute-done = bf16[16,2,32,384]{3,2,1,0:T(8,128)(2,1)S(1)} collective-permute-done((bf16[16,2,32,384]{3,2,1,0:T(8,128)(2,1)S(1)}, bf16[16,2,32,384]{3,2,1,0:T(8,128)(2,1)S(1)}, u32[]{:S(2)}, u32[]{:S(2)}) %collective-permute-start) | collective-permute-done | bytes 786464 | tf_op jit(solution)/shard_map/ppermute | solution.py:296
  56.2 3.6 %collective-permute-start.4 = (bf16[16,2,32,384]{3,2,1,0:T(8,128)(2,1)S(1)}, bf16[16,2,32,384]{3,2,1,0:T(8,128)(2,1)}, u32[]{:S(2)}, u32[]{:S(2)}) collective-permute-start(bf16[16,2,32,384]{3,2,1,0:T(8,128)(2,1)S(1)} %collective-permute-done.3), channel_id=1, source_target_pairs={{0,14},{2,0},{4,2},{6,4},{8,6},{10,8},{12,10},{14,12},{1,15},{3,1}... | collective-permute-start | bytes 2359304 | tf_op jit(solution)/shard_map/ppermute | solution.py:296
  59.8 17.9 %collective-permute-done.1 = bf16[16,2,32,384]{3,2,1,0:T(8,128)(2,1)} collective-permute-done((bf16[16,2,32,384]{3,2,1,0:T(8,128)(2,1)S(1)}, bf16[16,2,32,384]{3,2,1,0:T(8,128)(2,1)}, u32[]{:S(2)}, u32[]{:S(2)}) %collective-permute-start.1) | collective-permute-done | bytes 786464 | tf_op jit(solution)/shard_map/ppermute | solution.py:296
  77.7 3.2 %collective-permute-start.5 = (bf16[16,2,32,384]{3,2,1,0:T(8,128)(2,1)}, bf16[16,2,32,384]{3,2,1,0:T(8,128)(2,1)S(1)}, u32[]{:S(2)}, u32[]{:S(2)}) collective-permute-start(bf16[16,2,32,384]{3,2,1,0:T(8,128)(2,1)} %collective-permute-done.4), channel_id=1, source_target_pairs={{0,14},{2,0},{4,2},{6,4},{8,6},{10,8},{12,10},{14,12},{1,15},{3,1}... | collective-permute-start | bytes 2359304 | tf_op jit(solution)/shard_map/ppermute | solution.py:296
  80.9 5.6 %shard_map.102 = (bf16[256,6144]{1,0:T(8,128)(2,1)}, f32[256,1]{1,0:T(8,128)S(1)}, f32[256,1]{1,0:T(8,128)S(1)}) custom-call(bf16[256,6144]{1,0:T(8,128)(2,1)} %tok_ref.3, f32[1,6144]{1,0:T(1,128)S(1)} %bitcast.89), custom_call_target="tpu_custom_call" | custom-call | flops 20000000 | bytes 6291456 | tf_op jit(solution)/shard_map/pallas_call | solution.py:50
  86.5 11.9 %collective-permute-done.2.rest_0_ = bf16[16,2,32,384]{3,2,1,0:T(8,128)(2,1)S(1)} collective-permute-done((bf16[16,2,32,384]{3,2,1,0:T(8,128)(2,1)}, bf16[16,2,32,384]{3,2,1,0:T(8,128)(2,1)S(1)}, u32[]{:S(2)}, u32[]{:S(2)}) %collective-permute-start.2) | collective-permute-done | bytes 786464 | tf_op jit(solution)/shard_map/ppermute | solution.py:296
  100.4 10.8 %shard_map.104.g_ref = bf16[256,1024]{1,0:T(8,128)(2,1)} custom-call(bf16[256,6144]{1,0:T(8,128)(2,1)} %get-tuple-element.11.hid_ref, bf16[256,6144]{1,0:T(8,128)(2,1)} %cot_ref.3, bf16[16,4,384,256]{3,2,1,0:T(8,128)(2,1)} %bitcast.94, f32[1,256]{1,0:T(1,128)S(1)} %bitcast.92, f32[1,256]{1,0:T(1,128)S(1)} %bitcast.93, ...), custom_call_target="tpu_custom_call" | custom-call | flops 3221225472 | bytes 20000000 | tf_op jit(solution)/shard_map/pallas_call | solution.py:153
  111.2 7.1 %shard_map.105 = bf16[16,256,384]{2,1,0:T(8,128)(2,1)} custom-call(bf16[256,1024]{1,0:T(8,128)(2,1)} %shard_map.104.g_ref, bf16[16,4,384,256]{3,2,1,0:T(8,128)(2,1)} %bitcast.95), custom_call_target="tpu_custom_call" | custom-call | flops 805306368 | bytes 6000000 | tf_op jit(solution)/shard_map/pallas_call | solution.py:180
  120.6 3.5 %collective-permute-start.8 = (bf16[8,2,32,384]{3,2,1,0:T(8,128)(2,1)S(1)}, bf16[8,2,32,384]{3,2,1,0:T(8,128)(2,1)S(1)}, u32[]{:S(2)}, u32[]{:S(2)}) collective-permute-start(bf16[8,2,32,384]{3,2,1,0:T(8,128)(2,1)S(1)} %slice.53), channel_id=1, source_target_pairs={{0,14},{2,0},{4,2},{6,4},{8,6},{10,8},{12,10},{14,12},{1,15},{3,1}... | collective-permute-start | bytes 1179656 | tf_op jit(solution)/shard_map/ppermute | solution.py:296
  125.5 6.4 %collective-permute-done.7 = bf16[8,2,32,384]{3,2,1,0:T(8,128)(2,1)S(1)} collective-permute-done((bf16[8,2,32,384]{3,2,1,0:T(8,128)(2,1)S(1)}, bf16[8,2,32,384]{3,2,1,0:T(8,128)(2,1)S(1)}, u32[]{:S(2)}, u32[]{:S(2)}) %collective-permute-start.7) | collective-permute-done | bytes 393248 | tf_op jit(solution)/shard_map/ppermute | solution.py:296
  131.9 5.2 %collective-permute-done.8 = bf16[8,2,32,384]{3,2,1,0:T(8,128)(2,1)S(1)} collective-permute-done((bf16[8,2,32,384]{3,2,1,0:T(8,128)(2,1)S(1)}, bf16[8,2,32,384]{3,2,1,0:T(8,128)(2,1)S(1)}, u32[]{:S(2)}, u32[]{:S(2)}) %collective-permute-start.8) | collective-permute-done | bytes 393248 | tf_op jit(solution)/shard_map/ppermute | solution.py:296
  141.5 10.5 %shard_map.106 = (bf16[16,256,384]{2,1,0:T(8,128)(2,1)}, f32[256,2]{1,0:T(8,128)S(1)}) custom-call(bf16[256,1024]{1,0:T(8,128)(2,1)} %shard_map.104.g_ref, bf16[16,4,384,256]{3,2,1,0:T(8,128)(2,1)} %bitcast.96, bf16[256,6144]{1,0:T(8,128)(2,1)} %get-tuple-element.11.hid_ref, f32[16,1,384]{2,1,0:T(1,128)S(1)} %bitcast.90, bf16[8,16,2,32,384]{4,3,2,1,0:T(8,128)(2,1)} %copy-done.5), custom_call_target="tpu_custom_call" | custom-call | flops 2415919104 | bytes 16000000 | tf_op jit(solution)/shard_map/pallas_call | solution.py:223
  153.3 3.8 %collective-permute-start.13 = (bf16[256,384]{1,0:T(8,128)(2,1)S(1)}, bf16[256,384]{1,0:T(8,128)(2,1)S(1)}, u32[]{:S(2)}, u32[]{:S(2)}) collective-permute-start(bf16[256,384]{1,0:T(8,128)(2,1)S(1)} %get-tuple-element.24), channel_id=1, source_target_pairs={{0,14},{2,0},{4,2},{6,4},{8,6},{10,8},{12,10},{14,12},{1,15},{3,1}... | collective-permute-start | bytes 589832 | tf_op jit(solution)/shard_map/ppermute | solution.py:296
  157.1 7.6 %collective-permute-done.13 = bf16[256,384]{1,0:T(8,128)(2,1)S(1)} collective-permute-done((bf16[256,384]{1,0:T(8,128)(2,1)S(1)}, bf16[256,384]{1,0:T(8,128)(2,1)S(1)}, u32[]{:S(2)}, u32[]{:S(2)}) %collective-permute-start.13) | collective-permute-done | bytes 196640 | tf_op jit(solution)/shard_map/ppermute | solution.py:296
  164.7 3.2 %collective-permute-done.9 = bf16[256,384]{1,0:T(8,128)(2,1)S(1)} collective-permute-done((bf16[256,384]{1,0:T(8,128)(2,1)S(1)}, bf16[256,384]{1,0:T(8,128)(2,1)S(1)}, u32[]{:S(2)}, u32[]{:S(2)}) %collective-permute-start.9) | collective-permute-done | bytes 196640 | tf_op jit(solution)/shard_map/ppermute | solution.py:296
  169.1 3.3 %collective-permute-start.14 = (bf16[2,256,384]{2,1,0:T(8,128)(2,1)S(1)}, bf16[2,256,384]{2,1,0:T(8,128)(2,1)S(1)}, u32[]{:S(2)}, u32[]{:S(2)}) collective-permute-start(bf16[2,256,384]{2,1,0:T(8,128)(2,1)S(1)} %pad_maximum_fusion.2), channel_id=1, source_target_pairs={{0,14},{2,0},{4,2},{6,4},{8,6},{10,8},{12,10},{14,12},{1,15},{3,1}... | collective-permute-start | bytes 1179656 | tf_op jit(solution)/shard_map/ppermute | solution.py:296
  172.4 7.7 %collective-permute-done.10 = bf16[2,256,384]{2,1,0:T(8,128)(2,1)S(1)} collective-permute-done((bf16[2,256,384]{2,1,0:T(8,128)(2,1)S(1)}, bf16[2,256,384]{2,1,0:T(8,128)(2,1)S(1)}, u32[]{:S(2)}, u32[]{:S(2)}) %collective-permute-start.10) | collective-permute-done | bytes 393248 | tf_op jit(solution)/shard_map/ppermute | solution.py:296
  181.3 11.9 %collective-permute-done.11 = bf16[2,256,384]{2,1,0:T(8,128)(2,1)S(1)} collective-permute-done((bf16[2,256,384]{2,1,0:T(8,128)(2,1)S(1)}, bf16[2,256,384]{2,1,0:T(8,128)(2,1)S(1)}, u32[]{:S(2)}, u32[]{:S(2)}) %collective-permute-start.11) | collective-permute-done | bytes 393248 | tf_op jit(solution)/shard_map/ppermute | solution.py:296
  196.5 6.2 %collective-permute-done.15 = bf16[2,256,384]{2,1,0:T(8,128)(2,1)S(1)} collective-permute-done((bf16[2,256,384]{2,1,0:T(8,128)(2,1)S(1)}, bf16[2,256,384]{2,1,0:T(8,128)(2,1)S(1)}, u32[]{:S(2)}, u32[]{:S(2)}) %collective-permute-start.15) | collective-permute-done | bytes 393248 | tf_op jit(solution)/shard_map/ppermute | solution.py:296
  207.0 4.8 %all-to-all-start.1 = ((f32[16,2,256]{2,1,0:T(2,128)}), f32[16,2,256]{2,1,0:T(2,128)S(1)}, u32[]{:S(2)}, u32[]{:S(2)}) async-start(f32[16,2,256]{2,1,0:T(2,128)} %broadcast_in_dim.5), calls=%async_computation.3 | async-start | bytes 65536 | tf_op jit(solution)/shard_map/all_to_all | solution.py:331
  212.1 7.1 %all-to-all-done.1 = f32[16,2,256]{2,1,0:T(2,128)S(1)} async-done(((f32[16,2,256]{2,1,0:T(2,128)}), f32[16,2,256]{2,1,0:T(2,128)S(1)}, u32[]{:S(2)}, u32[]{:S(2)}) %all-to-all-start.1) | async-done | bytes 32800 | tf_op jit(solution)/shard_map/all_to_all | solution.py:331
  233.4 10.4 %shard_map.107 = (bf16[3,384,256]{2,1,0:T(8,128)(2,1)}, bf16[384,256]{1,0:T(8,128)(2,1)}) custom-call(s32[1]{0:T(128)} %bitcast.6.z_ref, bf16[8,16,2,32,384]{4,3,2,1,0:T(8,128)(2,1)} %copy-done.5, bf16[16,8,32,1024]{3,2,1,0:T(8,128)(2,1)} %bitcast.98), custom_call_target="tpu_custom_call" | custom-call | flops 3221225472 | bytes 16000000 | tf_op jit(solution)/shard_map/pallas_call | solution.py:269
  (82 shorter events, 42.7 us)
Async XLA Ops:
  8.0 78.5 %reduce-scatter.3.cloned.1.call-start = ((), (), s32[]{:S(2)}) async-start(), calls=%async_computation.4 | async-start | bytes 1179648 | tf_op jit(solution)/shard_map/reduce_scatter | solution.py:348
  10.2 89.2 %copy-start.3 = (f32[256]{0:T(256)S(1)}, f32[256]{0:T(256)}, u32[]{:S(2)}) copy-start(f32[256]{0:T(256)} %param.11) | copy-start | bytes 3076
  10.2 88.2 %all-gather.5.cloned.1.call-start = ((), (), s32[]{:S(2)}) async-start(), calls=%async_computation.6 | async-start | bytes 13369344 | tf_op jit(solution)/shard_map/all_gather | solution.py:347
  10.8 212.7 %reduce-scatter.5.cloned.1.call-start = ((), (), s32[]{:S(2)}) async-start(), calls=%async_computation.5 | async-start | bytes 3538944 | tf_op jit(solution)/shard_map/reduce_scatter | solution.py:357
  31.4 24.8 %collective-permute-start = (bf16[16,2,32,384]{3,2,1,0:T(8,128)(2,1)S(1)}, bf16[16,2,32,384]{3,2,1,0:T(8,128)(2,1)S(1)}, u32[]{:S(2)}, u32[]{:S(2)}) collective-permute-start(bf16[16,2,32,384]{3,2,1,0:T(8,128)(2,1)S(1)} %all_to_all.10), channel_id=1, source_target_pairs={{0,2},{2,4},{4,6},{6,8},{8,10},{10,12},{12,14},{14,0},{1,3},{3,5},... | collective-permute-start | bytes 2359304 | tf_op jit(solution)/shard_map/ppermute | solution.py:296
  33.3 22.9 %collective-permute-start.3 = (bf16[16,2,32,384]{3,2,1,0:T(8,128)(2,1)S(1)}, bf16[16,2,32,384]{3,2,1,0:T(8,128)(2,1)S(1)}, u32[]{:S(2)}, u32[]{:S(2)}) collective-permute-start(bf16[16,2,32,384]{3,2,1,0:T(8,128)(2,1)S(1)} %all_to_all.10), channel_id=1, source_target_pairs={{0,14},{2,0},{4,2},{6,4},{8,6},{10,8},{12,10},{14,12},{1,15},{3,1}... | collective-permute-start | bytes 2359304 | tf_op jit(solution)/shard_map/ppermute | solution.py:296
  56.2 21.5 %collective-permute-start.1 = (bf16[16,2,32,384]{3,2,1,0:T(8,128)(2,1)S(1)}, bf16[16,2,32,384]{3,2,1,0:T(8,128)(2,1)}, u32[]{:S(2)}, u32[]{:S(2)}) collective-permute-start(bf16[16,2,32,384]{3,2,1,0:T(8,128)(2,1)S(1)} %collective-permute-done), channel_id=1, source_target_pairs={{0,2},{2,4},{4,6},{6,8},{8,10},{10,12},{12,14},{14,0},{1,3},{3,5},... | collective-permute-start | bytes 2359304 | tf_op jit(solution)/shard_map/ppermute | solution.py:296
  56.2 21.5 %collective-permute-start.4 = (bf16[16,2,32,384]{3,2,1,0:T(8,128)(2,1)S(1)}, bf16[16,2,32,384]{3,2,1,0:T(8,128)(2,1)}, u32[]{:S(2)}, u32[]{:S(2)}) collective-permute-start(bf16[16,2,32,384]{3,2,1,0:T(8,128)(2,1)S(1)} %collective-permute-done.3), channel_id=1, source_target_pairs={{0,14},{2,0},{4,2},{6,4},{8,6},{10,8},{12,10},{14,12},{1,15},{3,1}... | collective-permute-start | bytes 2359304 | tf_op jit(solution)/shard_map/ppermute | solution.py:296
  77.7 20.7 %collective-permute-start.2 = (bf16[16,2,32,384]{3,2,1,0:T(8,128)(2,1)}, bf16[16,2,32,384]{3,2,1,0:T(8,128)(2,1)S(1)}, u32[]{:S(2)}, u32[]{:S(2)}) collective-permute-start(bf16[16,2,32,384]{3,2,1,0:T(8,128)(2,1)} %collective-permute-done.1), channel_id=1, source_target_pairs={{0,2},{2,4},{4,6},{6,8},{8,10},{10,12},{12,14},{14,0},{1,3},{3,5},... | collective-permute-start | bytes 2359304 | tf_op jit(solution)/shard_map/ppermute | solution.py:296
  77.7 20.7 %collective-permute-start.5 = (bf16[16,2,32,384]{3,2,1,0:T(8,128)(2,1)}, bf16[16,2,32,384]{3,2,1,0:T(8,128)(2,1)S(1)}, u32[]{:S(2)}, u32[]{:S(2)}) collective-permute-start(bf16[16,2,32,384]{3,2,1,0:T(8,128)(2,1)} %collective-permute-done.4), channel_id=1, source_target_pairs={{0,14},{2,0},{4,2},{6,4},{8,6},{10,8},{12,10},{14,12},{1,15},{3,1}... | collective-permute-start | bytes 2359304 | tf_op jit(solution)/shard_map/ppermute | solution.py:296
  118.4 115.0 %all-gather.7.cloned.1.call-start = ((), (), s32[]{:S(2)}) async-start(), calls=%async_computation.7 | async-start | bytes 8912896 | tf_op jit(solution)/shard_map/all_gather | solution.py:355
  120.4 11.4 %collective-permute-start.7 = (bf16[8,2,32,384]{3,2,1,0:T(8,128)(2,1)S(1)}, bf16[8,2,32,384]{3,2,1,0:T(8,128)(2,1)S(1)}, u32[]{:S(2)}, u32[]{:S(2)}) collective-permute-start(bf16[8,2,32,384]{3,2,1,0:T(8,128)(2,1)S(1)} %slice.52), channel_id=1, source_target_pairs={{0,2},{2,4},{4,6},{6,8},{8,10},{10,12},{12,14},{14,0},{1,3},{3,5},... | collective-permute-start | bytes 1179656 | tf_op jit(solution)/shard_map/ppermute | solution.py:296
  120.6 16.5 %collective-permute-start.8 = (bf16[8,2,32,384]{3,2,1,0:T(8,128)(2,1)S(1)}, bf16[8,2,32,384]{3,2,1,0:T(8,128)(2,1)S(1)}, u32[]{:S(2)}, u32[]{:S(2)}) collective-permute-start(bf16[8,2,32,384]{3,2,1,0:T(8,128)(2,1)S(1)} %slice.53), channel_id=1, source_target_pairs={{0,14},{2,0},{4,2},{6,4},{8,6},{10,8},{12,10},{14,12},{1,15},{3,1}... | collective-permute-start | bytes 1179656 | tf_op jit(solution)/shard_map/ppermute | solution.py:296
  153.3 11.4 %collective-permute-start.13 = (bf16[256,384]{1,0:T(8,128)(2,1)S(1)}, bf16[256,384]{1,0:T(8,128)(2,1)S(1)}, u32[]{:S(2)}, u32[]{:S(2)}) collective-permute-start(bf16[256,384]{1,0:T(8,128)(2,1)S(1)} %get-tuple-element.24), channel_id=1, source_target_pairs={{0,14},{2,0},{4,2},{6,4},{8,6},{10,8},{12,10},{14,12},{1,15},{3,1}... | collective-permute-start | bytes 589832 | tf_op jit(solution)/shard_map/ppermute | solution.py:296
  157.1 10.7 %collective-permute-start.9 = (bf16[256,384]{1,0:T(8,128)(2,1)S(1)}, bf16[256,384]{1,0:T(8,128)(2,1)S(1)}, u32[]{:S(2)}, u32[]{:S(2)}) collective-permute-start(bf16[256,384]{1,0:T(8,128)(2,1)S(1)} %get-tuple-element.22), channel_id=1, source_target_pairs={{0,2},{2,4},{4,6},{6,8},{8,10},{10,12},{12,14},{14,0},{1,3},{3,5},... | collective-permute-start | bytes 589832 | tf_op jit(solution)/shard_map/ppermute | solution.py:296
  169.0 11.2 %collective-permute-start.10 = (bf16[2,256,384]{2,1,0:T(8,128)(2,1)S(1)}, bf16[2,256,384]{2,1,0:T(8,128)(2,1)S(1)}, u32[]{:S(2)}, u32[]{:S(2)}) collective-permute-start(bf16[2,256,384]{2,1,0:T(8,128)(2,1)S(1)} %pad_maximum_fusion.1), channel_id=1, source_target_pairs={{0,2},{2,4},{4,6},{6,8},{8,10},{10,12},{12,14},{14,0},{1,3},{3,5},... | collective-permute-start | bytes 1179656 | tf_op jit(solution)/shard_map/ppermute | solution.py:296
  169.1 12.2 %collective-permute-start.14 = (bf16[2,256,384]{2,1,0:T(8,128)(2,1)S(1)}, bf16[2,256,384]{2,1,0:T(8,128)(2,1)S(1)}, u32[]{:S(2)}, u32[]{:S(2)}) collective-permute-start(bf16[2,256,384]{2,1,0:T(8,128)(2,1)S(1)} %pad_maximum_fusion.2), channel_id=1, source_target_pairs={{0,14},{2,0},{4,2},{6,4},{8,6},{10,8},{12,10},{14,12},{1,15},{3,1}... | collective-permute-start | bytes 1179656 | tf_op jit(solution)/shard_map/ppermute | solution.py:296
  181.2 12.0 %collective-permute-start.11 = (bf16[2,256,384]{2,1,0:T(8,128)(2,1)S(1)}, bf16[2,256,384]{2,1,0:T(8,128)(2,1)S(1)}, u32[]{:S(2)}, u32[]{:S(2)}) collective-permute-start(bf16[2,256,384]{2,1,0:T(8,128)(2,1)S(1)} %bitcast_add_fusion.3), channel_id=1, source_target_pairs={{0,2},{2,4},{4,6},{6,8},{8,10},{10,12},{12,14},{14,0},{1,3},{3,5},... | collective-permute-start | bytes 1179656 | tf_op jit(solution)/shard_map/ppermute | solution.py:296
  194.4 8.3 %collective-permute-start.15 = (bf16[2,256,384]{2,1,0:T(8,128)(2,1)S(1)}, bf16[2,256,384]{2,1,0:T(8,128)(2,1)S(1)}, u32[]{:S(2)}, u32[]{:S(2)}) collective-permute-start(bf16[2,256,384]{2,1,0:T(8,128)(2,1)S(1)} %get-tuple-element.19), channel_id=1, source_target_pairs={{0,14},{2,0},{4,2},{6,4},{8,6},{10,8},{12,10},{14,12},{1,15},{3,1}... | collective-permute-start | bytes 1179656 | tf_op jit(solution)/shard_map/ppermute | solution.py:296
  194.5 24.8 %collective-permute-start.12 = (bf16[2,256,384]{2,1,0:T(8,128)(2,1)S(1)}, bf16[2,256,384]{2,1,0:T(8,128)(2,1)S(1)}, u32[]{:S(2)}, u32[]{:S(2)}) collective-permute-start(bf16[2,256,384]{2,1,0:T(8,128)(2,1)S(1)} %get-tuple-element.18), channel_id=1, source_target_pairs={{0,2},{2,4},{4,6},{6,8},{8,10},{10,12},{12,14},{14,0},{1,3},{3,5},... | collective-permute-start | bytes 1179656 | tf_op jit(solution)/shard_map/ppermute | solution.py:296
  203.8 15.6 %collective-permute-start.16 = (bf16[2,256,384]{2,1,0:T(8,128)(2,1)S(1)}, bf16[2,256,384]{2,1,0:T(8,128)(2,1)S(1)}, u32[]{:S(2)}, u32[]{:S(2)}) collective-permute-start(bf16[2,256,384]{2,1,0:T(8,128)(2,1)S(1)} %bitcast_add_fusion.2), channel_id=1, source_target_pairs={{0,14},{2,0},{4,2},{6,4},{8,6},{10,8},{12,10},{14,12},{1,15},{3,1}... | collective-permute-start | bytes 1179656 | tf_op jit(solution)/shard_map/ppermute | solution.py:296
  207.0 12.3 %all-to-all-start.1 = ((f32[16,2,256]{2,1,0:T(2,128)}), f32[16,2,256]{2,1,0:T(2,128)S(1)}, u32[]{:S(2)}, u32[]{:S(2)}) async-start(f32[16,2,256]{2,1,0:T(2,128)} %broadcast_in_dim.5), calls=%async_computation.3 | async-start | bytes 65536 | tf_op jit(solution)/shard_map/all_to_all | solution.py:331
  220.5 7.3 %collective-permute-start.17 = (bf16[256,384]{1,0:T(8,128)(2,1)S(1)}, bf16[256,384]{1,0:T(8,128)(2,1)S(1)}, u32[]{:S(2)}, u32[]{:S(2)}) collective-permute-start(bf16[256,384]{1,0:T(8,128)(2,1)S(1)} %fusion.8), channel_id=1, source_target_pairs={{0,1},{1,0},{2,3},{3,2},{4,5},{5,4},{6,7},{7,6},{8,9},{9,8},{10,11... | collective-permute-start | bytes 589832 | tf_op jit(solution)/shard_map/ppermute | solution.py:300
  224.5 7.3 %collective-permute-start.6 = (bf16[256,384]{1,0:T(8,128)(2,1)S(1)}, bf16[256,384]{1,0:T(8,128)(2,1)S(1)}, u32[]{:S(2)}, u32[]{:S(2)}) collective-permute-start(bf16[256,384]{1,0:T(8,128)(2,1)S(1)} %dynamic-slice_bitcast_fusion.6), channel_id=1, source_target_pairs={{0,1},{1,0},{2,3},{3,2},{4,5},{5,4},{6,7},{7,6},{8,9},{9,8},{10,11... | collective-permute-start | bytes 589832 | tf_op jit(solution)/shard_map/ppermute | solution.py:300
  (8 other events, 140.6 us)
Sparse Core Ops, SparseCore 0:
  11.3 16.3 reduce-scatter.2
  118.5 49.3 reduce-scatter.4
Sparse Core Ops, SparseCore 1:
  12.7 78.9 all-gather.4
  121.4 52.6 all-gather.6

commit v2 on v1

v2 whole, which is shorter than its diff:
```python
import jax
import jax.numpy as jnp
from jax import lax
from jax.experimental import pallas as pl
from jax.experimental.pallas import tpu as pltpu
from jax.sharding import Mesh, PartitionSpec as P

DH = 128
EPS = 1e-06
DP = ("x", "yl", "c")
MP = ("z", "yh")
NX, NYL, NC, NZ, NYH = 4, 2, 2, 8, 2
NDP, NMP = NX * NYL * NC, NZ * NYH
ROWS = 256
SL = 384
HW = 256
D = 6144
SUB = ROWS // NZ
EXT = ROWS + 16
STEP = 4
KSTEP = 4
COST = pl.CostEstimate(flops=1000, bytes_accessed=1000, transcendentals=0)
VMEM = 52 * 1024 * 1024
BF = jnp.bfloat16
F32 = jnp.float32


def dot(a, b, ca, cb):
    return lax.dot_general(a, b, (((ca,), (cb,)), ((), ())), preferred_element_type=F32)


def params():
    return pltpu.CompilerParams(vmem_limit_bytes=VMEM)


ANY = pl.BlockSpec(memory_space=pl.ANY)


def order(xs, after):
    n = len(xs)
    return pl.pallas_call(
        lambda *refs: None,
        in_specs=[ANY] * (n + len(after)),
        out_specs=[ANY] * n,
        out_shape=[jax.ShapeDtypeStruct(x.shape, x.dtype) for x in xs],
        input_output_aliases={i: i for i in range(n)},
        cost_estimate=COST,
    )(*xs, *after)


def normalise(t):
    mean = jnp.mean(t, -1, keepdims=True)
    cen = t - mean
    rstd = lax.rsqrt(jnp.mean(cen * cen, -1, keepdims=True) + EPS)
    return cen * rstd, mean, rstd


def norm_kernel(tok_ref, gain_ref, hid_ref, mean_ref, rstd_ref):
    i = pl.program_id(0)
    blk = tok_ref.shape[0]
    gain = gain_ref[...]
    xhat, mean, rstd = normalise(tok_ref[...].astype(F32))
    hid_ref[pl.ds(pl.multiple_of(i * blk, blk), blk), :] = (xhat * gain).astype(BF)
    mean_ref[...] = mean
    rstd_ref[...] = rstd

    @pl.when(i == pl.num_programs(0) - 1)
    def _():
        hi = gain.astype(BF).astype(F32)
        row = lax.broadcasted_iota(jnp.int32, (16, D), 0)
        extra = jnp.where(row == 0, hi, jnp.where(row == 1, gain - hi, 0.0))
        hid_ref[ROWS:, :] = extra.astype(BF)


def norm_call(tokens, gain):
    blk = 64
    return pl.pallas_call(
        norm_kernel,
        grid=(ROWS // blk,),
        in_specs=[
            pl.BlockSpec((blk, D), lambda i: (i, 0)),
            pl.BlockSpec((1, D), lambda i: (0, 0)),
        ],
        out_specs=[
            pl.BlockSpec((EXT, D), lambda i: (0, 0)),
            pl.BlockSpec((blk, 1), lambda i: (i, 0)),
            pl.BlockSpec((blk, 1), lambda i: (i, 0)),
        ],
        out_shape=[
            jax.ShapeDtypeStruct((EXT, D), BF),
            jax.ShapeDtypeStruct((ROWS, 1), F32),
            jax.ShapeDtypeStruct((ROWS, 1), F32),
        ],
        compiler_params=params(),
        cost_estimate=COST,
    )(tokens, gain.reshape(1, D))


def rows_kernel(z_ref, tok_ref, cot_ref, gain_ref, out_ref):
    xhat, _, _ = normalise(tok_ref[...].astype(F32))
    hid = (xhat * gain_ref[...]).astype(BF)
    for i in range(NDP):
        out_ref[i, 0] = hid[:, i * SL : (i + 1) * SL]
        out_ref[i, 1] = cot_ref[:, i * SL : (i + 1) * SL]


def rows_call(z, tokens, cotangent, gain):
    return pl.pallas_call(
        rows_kernel,
        grid_spec=pltpu.PrefetchScalarGridSpec(
            num_scalar_prefetch=1,
            grid=(1,),
            in_specs=[
                pl.BlockSpec((SUB, D), lambda i, z: (z[0], 0)),
                pl.BlockSpec((SUB, D), lambda i, z: (z[0], 0)),
                pl.BlockSpec((1, D), lambda i, z: (0, 0)),
            ],
            out_specs=pl.BlockSpec((NDP, 2, SUB, SL), lambda i, z: (0, 0, 0, 0)),
        ),
        out_shape=jax.ShapeDtypeStruct((NDP, 2, SUB, SL), BF),
        compiler_params=params(),
        cost_estimate=COST,
    )(z, tokens, cotangent, gain.reshape(1, D))


def head_stats(u):
    cen = u - jnp.mean(u, -1, keepdims=True)
    s = lax.rsqrt(jnp.mean(cen * cen, -1, keepdims=True) + EPS)
    return cen * s, s


def head_back(g, n, s, gain):
    e = g * gain
    return (e - jnp.mean(e, -1, keepdims=True) - n * jnp.mean(e * n, -1, keepdims=True)) * s


def proj_kernel(hid_ref, cot_ref, w_ref, *rest):
    out_ref = rest[-1]
    i = pl.program_id(0)
    cols = pl.ds(pl.multiple_of(i * KSTEP * SL, KSTEP * SL), KSTEP * SL)
    h = hid_ref[:, cols]
    c = cot_ref[:, cols]
    for j in range(4):
        rows = EXT if j < 3 else ROWS
        new = dot(h if j < 3 else c, w_ref[:, j].reshape(KSTEP * SL, HW), 1, 0)

        @pl.when(i == 0)
        def _():
            out_ref[:rows, j * HW : (j + 1) * HW] = new

        @pl.when(i > 0)
        def _():
            out_ref[:rows, j * HW : (j + 1) * HW] += new


def proj_call(hid, cot, w, after):
    return pl.pallas_call(
        proj_kernel,
        grid=(NDP // KSTEP,),
        in_specs=[pl.BlockSpec(memory_space=pltpu.VMEM)] * 2
        + [pl.BlockSpec((KSTEP, 4, SL, HW), lambda i: (i, 0, 0, 0))]
        + [ANY] * len(after),
        out_specs=pl.BlockSpec((EXT, 4 * HW), lambda i: (0, 0)),
        out_shape=jax.ShapeDtypeStruct((EXT, 4 * HW), F32),
        compiler_params=params(),
        cost_estimate=COST,
    )(hid, cot, w, *after)


def attn_kernel(acc_ref, qg_ref, kg_ref, *rest):
    out_ref, sum_ref = rest[-2:]
    scale = DH ** (-0.5)
    t1 = jnp.zeros((ROWS, DH), F32)
    t2 = jnp.zeros((ROWS, DH), F32)
    for hd in range(HW // DH):
        cols = [slice(j * HW + hd * DH, j * HW + (hd + 1) * DH) for j in range(4)]
        sl = cols[0]
        qg = qg_ref[:, sl]
        kg = kg_ref[:, sl]
        proj = [acc_ref[:ROWS, c] for c in cols]
        qn, qs = head_stats(proj[0])
        kn, ks = head_stats(proj[1])
        q = (qn * qg).astype(BF)
        k = (kn * kg).astype(BF)
        v = proj[2].astype(BF)
        ga = proj[3].astype(BF)
        e = jnp.exp(dot(q, k, 1, 1) * scale)
        p = e / jnp.sum(e, -1, keepdims=True)
        pw = p.astype(BF)
        out_ref[:, cols[3]] = dot(pw, v, 1, 0).astype(BF)
        gp = dot(ga, v, 1, 1)
        delta = jnp.sum(p * gp, -1, keepdims=True)
        gs = (p * (gp - delta) * scale).astype(BF)
        gq = head_back(dot(gs, k, 1, 0), qn, qs, qg)
        gk = head_back(dot(gs, q, 0, 0), kn, ks, kg)
        gv = dot(pw, ga, 0, 0)
        for j, val in enumerate((gq, gk, gv)):
            g = val.astype(BF)
            out_ref[:, cols[j]] = g
            g = g.astype(F32)
            t1 += g * (acc_ref[ROWS : ROWS + 1, cols[j]] + acc_ref[ROWS + 1 : ROWS + 2, cols[j]])
            t2 += g * proj[j]
    ones = jnp.ones((8, DH), F32)
    total = [
        lax.dot_general(
            ones, t, (((1,), (1,)), ((), ())), precision=lax.Precision.HIGHEST, preferred_element_type=F32
        )
        for t in (t1, t2)
    ]
    row = lax.broadcasted_iota(jnp.int32, (8, ROWS), 0)
    sum_ref[...] = jnp.where(row == 0, total[0], total[1])


def attn_call(acc, qg, kg, after):
    full = lambda shape: pl.BlockSpec(shape, lambda: (0, 0))
    return pl.pallas_call(
        attn_kernel,
        in_specs=[full((EXT, 4 * HW)), full((1, HW)), full((1, HW))]
        + [pl.BlockSpec(memory_space=pl.ANY)] * len(after),
        out_specs=[full((ROWS, 4 * HW)), full((8, ROWS))],
        out_shape=[
            jax.ShapeDtypeStruct((ROWS, 4 * HW), BF),
            jax.ShapeDtypeStruct((8, ROWS), F32),
        ],
        compiler_params=params(),
        cost_estimate=COST,
    )(acc, qg.reshape(1, HW), kg.reshape(1, HW), *after)


def back_kernel(g_ref, w_ref, out_ref):
    for s in range(STEP):
        t = dot(g_ref[:, :HW], w_ref[s, 0], 1, 1)
        t += dot(g_ref[:, HW : 2 * HW], w_ref[s, 1], 1, 1)
        t += dot(g_ref[:, 2 * HW : 3 * HW], w_ref[s, 2], 1, 1)
        out_ref[s, :ROWS] = t.astype(BF)
        out_ref[s, ROWS:] = dot(g_ref[:, 3 * HW :], w_ref[s, 3], 1, 1).astype(BF)


def back_call(g, w):
    return pl.pallas_call(
        back_kernel,
        grid=(NDP // STEP,),
        in_specs=[
            pl.BlockSpec((ROWS, 4 * HW), lambda i: (0, 0)),
            pl.BlockSpec((STEP, 4, SL, HW), lambda i: (i, 0, 0, 0)),
        ],
        out_specs=pl.BlockSpec((STEP, 2 * ROWS, SL), lambda i: (i, 0, 0)),
        out_shape=jax.ShapeDtypeStruct((NDP, 2 * ROWS, SL), BF),
        compiler_params=params(),
        cost_estimate=COST,
    )(g, w)


def weight_kernel(part, z_ref, *refs):
    x_refs, rest = refs[:NZ], refs[NZ:]
    g_refs = rest[:2]
    i = pl.program_id(0)
    half = NDP // 2
    n = half * SUB

    def total(step):
        new, new_o = 0.0, 0.0
        for k in (0, 1):
            for h in (0, 1):
                x = x_refs[2 * (2 * step + k) + h]
                g = g_refs[k][h * half : (h + 1) * half].reshape(n, 4 * HW)
                new = new + dot(x[:, 0].reshape(n, SL), g[:, : 3 * HW], 0, 0)
                new_o = new_o + dot(x[:, 1].reshape(n, SL), g[:, 3 * HW :], 0, 0)
        return new, new_o

    if part == 0:
        acc, acc_o = rest[2:4]

        @pl.when(i == 0)
        def _():
            acc[...], acc_o[...] = total(0)

        @pl.when(i == 1)
        def _():
            new, new_o = total(1)
            acc[...] += new
            acc_o[...] += new_o
    else:
        old, old_o, dw_ref, do_ref, acc, acc_o = rest[2:8]

        @pl.when(i == 0)
        def _():
            new, new_o = total(0)
            acc[...] = old[...] + new
            acc_o[...] = old_o[...] + new_o

        @pl.when(i == 1)
        def _():
            new, new_o = total(1)
            for j in range(3):
                sl = slice(j * HW, (j + 1) * HW)
                dw_ref[j] = (acc[:, sl] + new[:, sl]).astype(BF)
            do_ref[...] = (acc_o[...] + new_o).astype(BF)


def weight_call(part, scalars, xs, g, old):
    g = g.reshape(NDP, NZ, SUB, 4 * HW)
    shapes = [(SL, 3 * HW), (SL, HW)]
    outs = [(3, SL, HW), (SL, HW)]
    zero = lambda n: (lambda i, z: (0,) * n)
    spot = lambda k: (lambda i, z: (0, (z[0] + 2 * NZ - 4 * part - 2 * i - k) % NZ, 0, 0))
    out = outs if part else shapes
    return pl.pallas_call(
        lambda *refs: weight_kernel(part, *refs),
        grid_spec=pltpu.PrefetchScalarGridSpec(
            num_scalar_prefetch=1,
            grid=(2,),
            in_specs=[pl.BlockSpec(x.shape, zero(4)) for x in xs]
            + [pl.BlockSpec((NDP, 1, SUB, 4 * HW), spot(k)) for k in (0, 1)]
            + [pl.BlockSpec(x.shape, zero(2)) for x in old],
            out_specs=[pl.BlockSpec(x, zero(len(x))) for x in out],
            scratch_shapes=[pltpu.VMEM(x, F32) for x in shapes] if part else [],
        ),
        out_shape=[jax.ShapeDtypeStruct(x, BF if part else F32) for x in out],
        compiler_params=params(),
        cost_estimate=COST,
    )(scalars, *xs, g, g, *old)


def shift(a, k):
    return lax.ppermute(a, "z", [(i, (i + k) % NZ) for i in range(NZ)])


def swap_yh(a):
    return lax.ppermute(a, "yh", [(0, 1), (1, 0)])


def ring_gather(own, hid):
    half = NDP // 2
    a, b = own[:half], own[half:]
    ra, la, rb, lb = order((shift(a, 1), shift(a, -1), shift(b, 1), shift(b, -1)), (hid,))
    right, left = [(ra, rb)], [(la, lb)]
    for _ in range(2):
        right.append(tuple(shift(x, 1) for x in right[-1]))
        left.append(tuple(shift(x, -1) for x in left[-1]))
    far = shift(right[-1][0], 1), shift(left[-1][1], -1)
    return [(a, b)] + right + [far] + left[::-1]


def all_sum(a):
    x = jnp.broadcast_to(a[None], (NMP,) + a.shape)
    return jnp.sum(lax.all_to_all(x, MP, 0, 0, tiled=True), 0)


def final_kernel(s_ref, mine_ref, recv_ref, sum_ref, tok_ref, mean_ref, rstd_ref, gain_ref, *refs):
    branch_ref, token_ref = refs[-2:]
    t = mine_ref[0].astype(F32) + recv_ref[...].astype(F32)
    s = jnp.transpose(sum_ref[...]) * (1.0 / D)
    rstd = rstd_ref[...]
    xhat = (tok_ref[...].astype(F32) - mean_ref[...]) * rstd
    grad = t[:ROWS] * gain_ref[...] - s[:, 0:1] - xhat * s[:, 1:2]
    token_ref[...] = (grad * rstd).astype(BF)
    branch_ref[...] = t[ROWS:].astype(BF)


def final_call(scalars, part, recv, sums, tokens, mean, rstd, gain, after):
    fixed = lambda i, s: (0, 0)
    cols = lambda i, s: (0, s[2])
    out = jax.ShapeDtypeStruct((ROWS, SL), BF)
    return pl.pallas_call(
        final_kernel,
        grid_spec=pltpu.PrefetchScalarGridSpec(
            num_scalar_prefetch=1,
            grid=(1,),
            in_specs=[
                pl.BlockSpec((1, 2 * ROWS, SL), lambda i, s: (s[1], 0, 0)),
                pl.BlockSpec((2 * ROWS, SL), fixed),
                pl.BlockSpec((8, ROWS), fixed),
                pl.BlockSpec((ROWS, SL), cols),
                pl.BlockSpec((ROWS, 1), fixed),
                pl.BlockSpec((ROWS, 1), fixed),
                pl.BlockSpec((1, SL), cols),
            ]
            + [ANY] * len(after),
            out_specs=[pl.BlockSpec((ROWS, SL), fixed)] * 2,
        ),
        out_shape=[out, out],
        compiler_params=params(),
        cost_estimate=COST,
    )(scalars, part, recv, sums, tokens, mean, rstd, gain.reshape(1, D), *after)


def local(tokens, w_qkv, w_out, layer_norm_gain, query_gain, key_gain, cotangent):
    z = lax.axis_index("z")
    yh = lax.axis_index("yh")
    scalars = jnp.stack([z, yh, z * NYH + yh]).astype(jnp.int32)

    w_own = jnp.concatenate([w_qkv.transpose(1, 0, 2), w_out[None]], 0)
    w = lax.all_gather(w_own, DP, axis=0)
    side = lax.psum_scatter(w_own, "c", scatter_dimension=0, tiled=True)

    hid, mean, rstd = norm_call(tokens, layer_norm_gain)
    rows = rows_call(scalars, tokens, cotangent, layer_norm_gain)
    moved = ring_gather(lax.all_to_all(rows, DP, 0, 0, tiled=True), hid)

    acc = proj_call(hid, cotangent, w, moved[2] + moved[6] + (side,))
    grads, sums = attn_call(acc, query_gain, key_gain, moved[3] + moved[4] + moved[5])
    all_grads = lax.all_gather(grads, DP, axis=0)
    terms = back_call(grads, w)
    part = lax.psum_scatter(
        terms.reshape(NDP * 2 * ROWS, SL), "z", scatter_dimension=0, tiled=True
    ).reshape(NYH, 2 * ROWS, SL)
    sums = all_sum(sums)
    flat = [x for pair in moved for x in pair]
    partial = weight_call(0, scalars, flat[:NZ], all_grads, ())
    grad_w, grad_o = weight_call(1, scalars, flat[NZ:], all_grads, partial)
    (part,) = order((part,), (grad_w, sums))
    recv = swap_yh(lax.dynamic_index_in_dim(part, 1 - yh, 0, keepdims=False))
    branch, token_gradient = final_call(
        scalars, part, recv, sums, tokens, mean, rstd, layer_norm_gain, ()
    )
    return (branch, token_gradient, grad_w.transpose(1, 0, 2), grad_o)


def solution(mesh):
    fine = Mesh(mesh.devices.reshape(NX, NYL, NC, NZ, NYH), DP + MP)
    return jax.shard_map(
        local,
        mesh=fine,
        in_specs=(
            P(DP, None),
            P(DP, None, MP),
            P(DP, MP),
            P(),
            P(MP),
            P(MP),
            P(DP, None),
        ),
        out_specs=(P(DP, MP), P(DP, MP), P(DP, None, MP), P(DP, MP)),
        check_vma=False,
    )
```

time: 252 us -> 227 us (0.901)
  waiting for transfers between devices: 108 us -> 94 us
  other arithmetic: 11.6 us -> 2.84 us
  Pallas kernels: 46 us -> 50.8 us
  local copies, waits for them, and re-layouts: 13 us -> 8.54 us
    ppermute x16 -> x14, waiting for transfers between devices: 95.4 us -> 27.8 us  [shift(): return lax.ppermute(a, 'z', [(i, (i + k) % NZ) for i in range(NZ)])]
    all_gather x1, waiting for transfers between devices: 0.01 us -> 23.7 us  [local(): all_grads = lax.all_gather(grads, DP, axis=0)]
    reduce_scatter x1, waiting for transfers between devices: 0.01 us -> 19.9 us  [local(): lax.psum_scatter(terms.reshape(NDP * 2 * ROWS, SL), 'z', scatter_dimensio...]
    ppermute x2 -> x1, waiting for transfers between devices: 4.76 us -> 12.1 us  [swap_yh(): return lax.ppermute(a, 'yh', [(0, 1), (1, 0)])]
    add x4 -> x0, other arithmetic: 4.44 us -> none  [the longest x2 2.26 us: ring_sum(): p, m = (shift(block(1) + p, 1), shift(block(-1) + m, -1))]
    pallas_call x3 -> x7, Pallas kernels: 28.4 us -> 32.7 us  [the longest x1 14.5 us: proj_call(): pl.pallas_call(proj_kernel, grid=(NDP // KSTEP,), in_specs=[pl.BlockSpec(...]
    convert_element_type x2 -> x0, other arithmetic: 3.47 us -> none  [the longest x1 1.81 us: local(): token_gradient = ((grad_hidden * gain - sums[0][:, None] - xhat * sums[1]...]
    ppermute x2 -> x1, starting transfers between devices: 3.7 us -> 0.64 us  [swap_yh(): return lax.ppermute(a, 'yh', [(0, 1), (1, 0)])]
  transfers between devices with their start and end apart: 23 -> 20, of which waited for: 13 -> 10; matrix products, arithmetic and copies ran while one was open for 7% -> 1% of each run, Pallas kernels for 7% -> 20%
where the time goes in v2:
time: 227 us; the launch traced here: 226 us
  waiting for transfers between devices  94 us (41%)
  Pallas kernels  50.8 us (22%)
  starting transfers between devices  36 us (16%)
  blocking collectives  18.2 us (8%)
  between operations  15.7 us (7%)
  local copies, waits for them, and re-layouts  8.54 us (4%)
  other arithmetic  2.84 us (1%)
    ppermute x14, waiting for transfers between devices, shift(): return lax.ppermute(a, 'z', [(i, (i + k) % NZ) for i in range(NZ)])  27.8 us
    ppermute x14, starting transfers between devices, shift(): return lax.ppermute(a, 'z', [(i, (i + k) % NZ) for i in range(NZ)])  27.6 us
    all_gather x1, waiting for transfers between devices, local(): all_grads = lax.all_gather(grads, DP, axis=0)  23.7 us
    reduce_scatter x1, waiting for transfers between devices, local(): lax.psum_scatter(terms.reshape(NDP * 2 * ROWS, SL), 'z', scatter_dimensio...  19.9 us
    all_to_all x1, blocking collectives, local(): moved = ring_gather(lax.all_to_all(rows, DP, 0, 0, tiled=True), hid)  18.2 us
    pallas_call x1, Pallas kernels, proj_call(): pl.pallas_call(proj_kernel, grid=(NDP // KSTEP,), in_specs=[pl.BlockSpec(...  14.5 us
    ppermute x1, waiting for transfers between devices, swap_yh(): return lax.ppermute(a, 'yh', [(0, 1), (1, 0)])  12.1 us
    pallas_call x2, Pallas kernels, weight_call(): pl.pallas_call(lambda *refs: weight_kernel(part, *refs), grid_spec=pltpu....  11.8 us
  transfers between devices with their start and end apart: 20, of which 10 were waited for; matrix products, arithmetic and copies ran while one was open for 1% of the time, Pallas kernels for 20%

profile of v2, /device:TPU:16, one launch (start us, length us, event | category | flops | bytes accessed | tf_op | source)
XLA Modules:
  0.0 226.1 jit_solution(8588643890507768217)
XLA Ops:
  13.8 18.2 %all_to_all.10 = bf16[16,2,32,384]{3,2,1,0:T(8,128)(2,1)S(1)} all-to-all(bf16[16,2,32,384]{3,2,1,0:T(8,128)(2,1)S(1)} %shard_map.103), channel_id=1, replica_groups=mesh['x'=4,'yl'=2,'c'=2,'z'=8,'yh'=2] {'x','yl','c'}, dimensions={0} | all-to-all | bytes 1572864 | tf_op jit(solution)/shard_map/all_to_all | solution.py:399
  32.0 8.1 %collective-permute-start.3 = (bf16[8,2,32,384]{3,2,1,0:T(8,128)(2,1)S(1)}, bf16[8,2,32,384]{3,2,1,0:T(8,128)(2,1)S(1)}, u32[]{:S(2)}, u32[]{:S(2)}) collective-permute-start(bf16[8,2,32,384]{3,2,1,0:T(8,128)(2,1)S(1)} %get-tuple-element.34.refs_2_), channel_id=1, source_target_pairs={{0,14},{2,0},{4,2},{6,4},{8,6},{10,8},{12,10},{14,12},{1,15},{3,1}... | collective-permute-start | bytes 1179656 | tf_op jit(solution)/shard_map/ppermute | solution.py:326
  40.1 3.2 %collective-permute-start.1 = (bf16[8,2,32,384]{3,2,1,0:T(8,128)(2,1)S(1)}, bf16[8,2,32,384]{3,2,1,0:T(8,128)(2,1)S(1)}, u32[]{:S(2)}, u32[]{:S(2)}) collective-permute-start(bf16[8,2,32,384]{3,2,1,0:T(8,128)(2,1)S(1)} %get-tuple-element.35.refs_1_), channel_id=1, source_target_pairs={{0,14},{2,0},{4,2},{6,4},{8,6},{10,8},{12,10},{14,12},{1,15},{3,1}... | collective-permute-start | bytes 1179656 | tf_op jit(solution)/shard_map/ppermute | solution.py:326
  43.4 6.2 %shard_map.102 = (bf16[272,6144]{1,0:T(8,128)(2,1)}, f32[256,1]{1,0:T(8,128)S(1)}, f32[256,1]{1,0:T(8,128)S(1)}) custom-call(bf16[256,6144]{1,0:T(8,128)(2,1)} %tok_ref.5, f32[1,6144]{1,0:T(1,128)S(1)} %bitcast.17), custom_call_target="tpu_custom_call" | custom-call | flops 1000 | bytes 1000 | tf_op jit(solution)/shard_map/pallas_call | solution.py:77
  53.0 4.5 %collective-permute-done.1.refs_1_ = bf16[8,2,32,384]{3,2,1,0:T(8,128)(2,1)S(1)} collective-permute-done((bf16[8,2,32,384]{3,2,1,0:T(8,128)(2,1)S(1)}, bf16[8,2,32,384]{3,2,1,0:T(8,128)(2,1)S(1)}, u32[]{:S(2)}, u32[]{:S(2)}) %collective-permute-start.1) | collective-permute-done | bytes 393248 | tf_op jit(solution)/shard_map/ppermute | solution.py:326
  57.5 3.9 %collective-permute-done.refs_0_ = bf16[8,2,32,384]{3,2,1,0:T(8,128)(2,1)S(1)} collective-permute-done((bf16[8,2,32,384]{3,2,1,0:T(8,128)(2,1)S(1)}, bf16[8,2,32,384]{3,2,1,0:T(8,128)(2,1)S(1)}, u32[]{:S(2)}, u32[]{:S(2)}) %collective-permute-start) | collective-permute-done | bytes 393248 | tf_op jit(solution)/shard_map/ppermute | solution.py:326
  62.2 3.2 %collective-permute-start.7 = (bf16[8,2,32,384]{3,2,1,0:T(8,128)(2,1)}, bf16[8,2,32,384]{3,2,1,0:T(8,128)(2,1)S(1)}, u32[]{:S(2)}, u32[]{:S(2)}) collective-permute-start(bf16[8,2,32,384]{3,2,1,0:T(8,128)(2,1)} %get-tuple-element.23.refs_8_), channel_id=1, source_target_pairs={{0,14},{2,0},{4,2},{6,4},{8,6},{10,8},{12,10},{14,12},{1,15},{3,1}... | collective-permute-start | bytes 1179656 | tf_op jit(solution)/shard_map/ppermute | solution.py:326
  65.4 3.2 %collective-permute-start.6 = (bf16[8,2,32,384]{3,2,1,0:T(8,128)(2,1)}, bf16[8,2,32,384]{3,2,1,0:T(8,128)(2,1)}, u32[]{:S(2)}, u32[]{:S(2)}) collective-permute-start(bf16[8,2,32,384]{3,2,1,0:T(8,128)(2,1)} %get-tuple-element.22.refs_7_), channel_id=1, source_target_pairs={{0,14},{2,0},{4,2},{6,4},{8,6},{10,8},{12,10},{14,12},{1,15},{3,1}... | collective-permute-start | bytes 1179656 | tf_op jit(solution)/shard_map/ppermute | solution.py:326
  68.6 6.9 %collective-permute-done.4.rest_0_.refs_5_ = bf16[8,2,32,384]{3,2,1,0:T(8,128)(2,1)S(1)} collective-permute-done((bf16[8,2,32,384]{3,2,1,0:T(8,128)(2,1)}, bf16[8,2,32,384]{3,2,1,0:T(8,128)(2,1)S(1)}, u32[]{:S(2)}, u32[]{:S(2)}) %collective-permute-start.4) | collective-permute-done | bytes 393248 | tf_op jit(solution)/shard_map/ppermute | solution.py:326
  75.6 3.3 %collective-permute-start.11 = (bf16[8,2,32,384]{3,2,1,0:T(8,128)(2,1)S(1)}, bf16[8,2,32,384]{3,2,1,0:T(8,128)(2,1)S(1)}, u32[]{:S(2)}, u32[]{:S(2)}) collective-permute-start(bf16[8,2,32,384]{3,2,1,0:T(8,128)(2,1)S(1)} %collective-permute-done.7.rest_3_.refs_6_), channel_id=1, source_target_pairs={{0,14},{2,0},{4,2},{6,4},{8,6},{10,8},{12,10},{14,12},{1,15},{3,1}... | collective-permute-start | bytes 1179656 | tf_op jit(solution)/shard_map/ppermute | solution.py:326
  78.8 5.3 %collective-permute-done.5.rest_1_.refs_6_ = bf16[8,2,32,384]{3,2,1,0:T(8,128)(2,1)} collective-permute-done((bf16[8,2,32,384]{3,2,1,0:T(8,128)(2,1)}, bf16[8,2,32,384]{3,2,1,0:T(8,128)(2,1)}, u32[]{:S(2)}, u32[]{:S(2)}) %collective-permute-start.5) | collective-permute-done | bytes 393248 | tf_op jit(solution)/shard_map/ppermute | solution.py:326
  84.1 3.3 %collective-permute-start.13 = (bf16[8,2,32,384]{3,2,1,0:T(8,128)(2,1)}, bf16[8,2,32,384]{3,2,1,0:T(8,128)(2,1)S(1)}, u32[]{:S(2)}, u32[]{:S(2)}) collective-permute-start(bf16[8,2,32,384]{3,2,1,0:T(8,128)(2,1)} %collective-permute-done.6.rest_2_.refs_5_), channel_id=1, source_target_pairs={{0,14},{2,0},{4,2},{6,4},{8,6},{10,8},{12,10},{14,12},{1,15},{3,1}... | collective-permute-start | bytes 1179656 | tf_op jit(solution)/shard_map/ppermute | solution.py:326
  87.4 5.0 %collective-permute-done.8.rest_0_.refs_7_ = bf16[8,2,32,384]{3,2,1,0:T(8,128)(2,1)S(1)} collective-permute-done((bf16[8,2,32,384]{3,2,1,0:T(8,128)(2,1)S(1)}, bf16[8,2,32,384]{3,2,1,0:T(8,128)(2,1)S(1)}, u32[]{:S(2)}, u32[]{:S(2)}) %collective-permute-start.8) | collective-permute-done | bytes 393248 | tf_op jit(solution)/shard_map/ppermute | solution.py:326
  92.4 3.3 %collective-permute-start.12 = (bf16[8,2,32,384]{3,2,1,0:T(8,128)(2,1)S(1)}, bf16[8,2,32,384]{3,2,1,0:T(8,128)(2,1)S(1)}, u32[]{:S(2)}, u32[]{:S(2)}) collective-permute-start(bf16[8,2,32,384]{3,2,1,0:T(8,128)(2,1)S(1)} %collective-permute-done.11.rest_5_.refs_4_), channel_id=1, source_target_pairs={{0,14},{2,0},{4,2},{6,4},{8,6},{10,8},{12,10},{14,12},{1,15},{3,1}... | collective-permute-start | bytes 1179656 | tf_op jit(solution)/shard_map/ppermute | solution.py:326
  96.7 14.5 %shard_map.105.acc_ref = f32[272,1024]{1,0:T(8,128)} custom-call(bf16[272,6144]{1,0:T(8,128)(2,1)} %get-tuple-element.19.refs_4_.hid_ref, bf16[256,6144]{1,0:T(8,128)(2,1)} %cot_ref.3, bf16[16,4,384,256]{3,2,1,0:T(8,128)(2,1)} %bitcast.25, bf16[8,2,32,384]{3,2,1,0:T(8,128)(2,1)S(1)} %collective-permute-done.4.rest_0_.refs_5_, ...), custom_call_target="tpu_custom_call" | custom-call | flops 1000 | bytes 1000 | tf_op jit(solution)/shard_map/pallas_call | solution.py:157
  111.3 3.8 %shard_map.106 = (bf16[256,1024]{1,0:T(8,128)(2,1)}, f32[8,256]{1,0:T(8,128)S(1)}) custom-call(f32[272,1024]{1,0:T(8,128)} %shard_map.105.acc_ref, f32[1,256]{1,0:T(1,128)S(1)} %bitcast.19, f32[1,256]{1,0:T(1,128)S(1)} %bitcast.20, bf16[8,2,32,384]{3,2,1,0:T(8,128)(2,1)S(1)} %collective-permute-done.8.rest_0_.refs_7_, ...), custom_call_target="tpu_custom_call" | custom-call | flops 1000 | bytes 1000 | tf_op jit(solution)/shard_map/pallas_call | solution.py:216
  116.2 9.9 %shard_map.107 = bf16[16,512,384]{2,1,0:T(8,128)(2,1)} custom-call(bf16[256,1024]{1,0:T(8,128)(2,1)S(1)} %copy-done.1, bf16[16,4,384,256]{3,2,1,0:T(8,128)(2,1)} %bitcast.26), custom_call_target="tpu_custom_call" | custom-call | flops 1000 | bytes 1000 | tf_op jit(solution)/shard_map/pallas_call | solution.py:240
  126.8 7.5 %all-to-all-start.1 = ((f32[16,8,256]{2,1,0:T(8,128)}), f32[16,8,256]{2,1,0:T(8,128)S(1)}, u32[]{:S(2)}, u32[]{:S(2)}) async-start(f32[16,8,256]{2,1,0:T(8,128)} %broadcast_in_dim.10), calls=%async_computation.3 | async-start | bytes 262144 | tf_op jit(solution)/shard_map/all_to_all | solution.py:347
  134.4 10.1 %all-to-all-done.1 = f32[16,8,256]{2,1,0:T(8,128)S(1)} async-done(((f32[16,8,256]{2,1,0:T(8,128)}), f32[16,8,256]{2,1,0:T(8,128)S(1)}, u32[]{:S(2)}, u32[]{:S(2)}) %all-to-all-start.1) | async-done | bytes 131104 | tf_op jit(solution)/shard_map/all_to_all | solution.py:347
  145.1 23.7 %all-gather.7.cloned.1.call-done = bf16[4096,1024]{1,0:T(8,128)(2,1)} async-done(((bf16[256,1024]{1,0:T(8,128)(2,1)}), bf16[4096,1024]{1,0:T(8,128)(2,1)}) %all-gather.7.cloned.1.call-update) | async-done | bytes 8388624 | tf_op jit(solution)/shard_map/all_gather | solution.py:403
  168.7 5.8 %shard_map.108 = (f32[384,768]{1,0:T(8,128)}, f32[384,256]{1,0:T(8,128)S(1)}) custom-call(s32[3]{0:T(128)S(1)} %pad_add_fusion.z_ref.refs_0_.s_ref, bf16[8,2,32,384]{3,2,1,0:T(8,128)(2,1)S(1)} %copy-done.11, bf16[8,2,32,384]{3,2,1,0:T(8,128)(2,1)S(1)} %get-tuple-element.34.refs_2_, bf16[8,2,32,384]{3,2,1,0:T(8,128)(2,1)S(1)} %copy-done.9, ...), custom_call_target="tpu_custom_call" | custom-call | flops 1000 | bytes 1000 | tf_op jit(solution)/shard_map/pallas_call | solution.py:308
  175.3 6.0 %shard_map.109 = (bf16[3,384,256]{2,1,0:T(8,128)(2,1)}, bf16[384,256]{1,0:T(8,128)(2,1)}) custom-call(s32[3]{0:T(128)S(1)} %pad_add_fusion.z_ref.refs_0_.s_ref, bf16[8,2,32,384]{3,2,1,0:T(8,128)(2,1)S(1)} %collective-permute-done.10.rest_2_.refs_1_, bf16[8,2,32,384]{3,2,1,0:T(8,128)(2,1)S(1)} %collective-permute-done.12.rest_3_.refs_2_, ...), custom_call_target="tpu_custom_call" | custom-call | flops 1000 | bytes 1000 | tf_op jit(solution)/shard_map/pallas_call | solution.py:308
  181.3 19.9 %reduce-scatter.5.cloned.1.call-done = bf16[1024,384]{1,0:T(8,128)(2,1)} async-done(((bf16[8192,384]{1,0:T(8,128)(2,1)}), bf16[1024,384]{1,0:T(8,128)(2,1)}) %reduce-scatter.5.cloned.1.call-update) | async-done | bytes 786448 | tf_op jit(solution)/shard_map/reduce_scatter | solution.py:405
  202.9 12.1 %collective-permute-done.14.recv_ref = bf16[512,384]{1,0:T(8,128)(2,1)S(1)} collective-permute-done((bf16[512,384]{1,0:T(8,128)(2,1)S(1)}, bf16[512,384]{1,0:T(8,128)(2,1)S(1)}, u32[]{:S(2)}, u32[]{:S(2)}) %collective-permute-start.14) | collective-permute-done | bytes 393248 | tf_op jit(solution)/shard_map/ppermute | solution.py:330
  (91 shorter events, 19.6 us)
Async XLA Ops:
  8.0 87.7 %reduce-scatter.3.cloned.1.call-start = ((), (), s32[]{:S(2)}) async-start(), calls=%async_computation.4 | async-start | bytes 1179648 | tf_op jit(solution)/shard_map/reduce_scatter | solution.py:395
  10.2 85.5 %all-gather.5.cloned.1.call-start = ((), (), s32[]{:S(2)}) async-start(), calls=%async_computation.6 | async-start | bytes 13369344 | tf_op jit(solution)/shard_map/all_gather | solution.py:394
  10.8 157.9 %all-gather.7.cloned.1.call-start = ((), (), s32[]{:S(2)}) async-start(), calls=%async_computation.7 | async-start | bytes 8912896 | tf_op jit(solution)/shard_map/all_gather | solution.py:403
  32.0 18.8 %collective-permute-start.3 = (bf16[8,2,32,384]{3,2,1,0:T(8,128)(2,1)S(1)}, bf16[8,2,32,384]{3,2,1,0:T(8,128)(2,1)S(1)}, u32[]{:S(2)}, u32[]{:S(2)}) collective-permute-start(bf16[8,2,32,384]{3,2,1,0:T(8,128)(2,1)S(1)} %get-tuple-element.34.refs_2_), channel_id=1, source_target_pairs={{0,14},{2,0},{4,2},{6,4},{8,6},{10,8},{12,10},{14,12},{1,15},{3,1}... | collective-permute-start | bytes 1179656 | tf_op jit(solution)/shard_map/ppermute | solution.py:326
  40.1 12.9 %collective-permute-start.2 = (bf16[8,2,32,384]{3,2,1,0:T(8,128)(2,1)S(1)}, bf16[8,2,32,384]{3,2,1,0:T(8,128)(2,1)S(1)}, u32[]{:S(2)}, u32[]{:S(2)}) collective-permute-start(bf16[8,2,32,384]{3,2,1,0:T(8,128)(2,1)S(1)} %get-tuple-element.34.refs_2_), channel_id=1, source_target_pairs={{0,2},{2,4},{4,6},{6,8},{8,10},{10,12},{12,14},{14,0},{1,3},{3,5},... | collective-permute-start | bytes 1179656 | tf_op jit(solution)/shard_map/ppermute | solution.py:326
  40.1 17.4 %collective-permute-start.1 = (bf16[8,2,32,384]{3,2,1,0:T(8,128)(2,1)S(1)}, bf16[8,2,32,384]{3,2,1,0:T(8,128)(2,1)S(1)}, u32[]{:S(2)}, u32[]{:S(2)}) collective-permute-start(bf16[8,2,32,384]{3,2,1,0:T(8,128)(2,1)S(1)} %get-tuple-element.35.refs_1_), channel_id=1, source_target_pairs={{0,14},{2,0},{4,2},{6,4},{8,6},{10,8},{12,10},{14,12},{1,15},{3,1}... | collective-permute-start | bytes 1179656 | tf_op jit(solution)/shard_map/ppermute | solution.py:326
  43.4 18.0 %collective-permute-start = (bf16[8,2,32,384]{3,2,1,0:T(8,128)(2,1)S(1)}, bf16[8,2,32,384]{3,2,1,0:T(8,128)(2,1)S(1)}, u32[]{:S(2)}, u32[]{:S(2)}) collective-permute-start(bf16[8,2,32,384]{3,2,1,0:T(8,128)(2,1)S(1)} %get-tuple-element.35.refs_1_), channel_id=1, source_target_pairs={{0,2},{2,4},{4,6},{6,8},{8,10},{10,12},{12,14},{14,0},{1,3},{3,5},... | collective-permute-start | bytes 1179656 | tf_op jit(solution)/shard_map/ppermute | solution.py:326
  62.2 13.4 %collective-permute-start.4 = (bf16[8,2,32,384]{3,2,1,0:T(8,128)(2,1)}, bf16[8,2,32,384]{3,2,1,0:T(8,128)(2,1)S(1)}, u32[]{:S(2)}, u32[]{:S(2)}) collective-permute-start(bf16[8,2,32,384]{3,2,1,0:T(8,128)(2,1)} %get-tuple-element.20.refs_3_), channel_id=1, source_target_pairs={{0,2},{2,4},{4,6},{6,8},{8,10},{10,12},{12,14},{14,0},{1,3},{3,5},... | collective-permute-start | bytes 1179656 | tf_op jit(solution)/shard_map/ppermute | solution.py:326
  62.2 13.4 %collective-permute-start.7 = (bf16[8,2,32,384]{3,2,1,0:T(8,128)(2,1)}, bf16[8,2,32,384]{3,2,1,0:T(8,128)(2,1)S(1)}, u32[]{:S(2)}, u32[]{:S(2)}) collective-permute-start(bf16[8,2,32,384]{3,2,1,0:T(8,128)(2,1)} %get-tuple-element.23.refs_8_), channel_id=1, source_target_pairs={{0,14},{2,0},{4,2},{6,4},{8,6},{10,8},{12,10},{14,12},{1,15},{3,1}... | collective-permute-start | bytes 1179656 | tf_op jit(solution)/shard_map/ppermute | solution.py:326
  65.4 18.7 %collective-permute-start.5 = (bf16[8,2,32,384]{3,2,1,0:T(8,128)(2,1)}, bf16[8,2,32,384]{3,2,1,0:T(8,128)(2,1)}, u32[]{:S(2)}, u32[]{:S(2)}) collective-permute-start(bf16[8,2,32,384]{3,2,1,0:T(8,128)(2,1)} %get-tuple-element.21.refs_4_), channel_id=1, source_target_pairs={{0,2},{2,4},{4,6},{6,8},{8,10},{10,12},{12,14},{14,0},{1,3},{3,5},... | collective-permute-start | bytes 1179656 | tf_op jit(solution)/shard_map/ppermute | solution.py:326
  65.4 18.7 %collective-permute-start.6 = (bf16[8,2,32,384]{3,2,1,0:T(8,128)(2,1)}, bf16[8,2,32,384]{3,2,1,0:T(8,128)(2,1)}, u32[]{:S(2)}, u32[]{:S(2)}) collective-permute-start(bf16[8,2,32,384]{3,2,1,0:T(8,128)(2,1)} %get-tuple-element.22.refs_7_), channel_id=1, source_target_pairs={{0,14},{2,0},{4,2},{6,4},{8,6},{10,8},{12,10},{14,12},{1,15},{3,1}... | collective-permute-start | bytes 1179656 | tf_op jit(solution)/shard_map/ppermute | solution.py:326
  75.5 16.9 %collective-permute-start.8 = (bf16[8,2,32,384]{3,2,1,0:T(8,128)(2,1)S(1)}, bf16[8,2,32,384]{3,2,1,0:T(8,128)(2,1)S(1)}, u32[]{:S(2)}, u32[]{:S(2)}) collective-permute-start(bf16[8,2,32,384]{3,2,1,0:T(8,128)(2,1)S(1)} %collective-permute-done.4.rest_0_.refs_5_), channel_id=1, source_target_pairs={{0,2},{2,4},{4,6},{6,8},{8,10},{10,12},{12,14},{14,0},{1,3},{3,5},... | collective-permute-start | bytes 1179656 | tf_op jit(solution)/shard_map/ppermute | solution.py:326
  75.6 16.8 %collective-permute-start.11 = (bf16[8,2,32,384]{3,2,1,0:T(8,128)(2,1)S(1)}, bf16[8,2,32,384]{3,2,1,0:T(8,128)(2,1)S(1)}, u32[]{:S(2)}, u32[]{:S(2)}) collective-permute-start(bf16[8,2,32,384]{3,2,1,0:T(8,128)(2,1)S(1)} %collective-permute-done.7.rest_3_.refs_6_), channel_id=1, source_target_pairs={{0,14},{2,0},{4,2},{6,4},{8,6},{10,8},{12,10},{14,12},{1,15},{3,1}... | collective-permute-start | bytes 1179656 | tf_op jit(solution)/shard_map/ppermute | solution.py:326
  84.1 27.2 %collective-permute-start.9 = (bf16[8,2,32,384]{3,2,1,0:T(8,128)(2,1)}, bf16[8,2,32,384]{3,2,1,0:T(8,128)(2,1)S(1)}, u32[]{:S(2)}, u32[]{:S(2)}) collective-permute-start(bf16[8,2,32,384]{3,2,1,0:T(8,128)(2,1)} %collective-permute-done.5.rest_1_.refs_6_), channel_id=1, source_target_pairs={{0,2},{2,4},{4,6},{6,8},{8,10},{10,12},{12,14},{14,0},{1,3},{3,5},... | collective-permute-start | bytes 1179656 | tf_op jit(solution)/shard_map/ppermute | solution.py:326
  84.1 27.2 %collective-permute-start.13 = (bf16[8,2,32,384]{3,2,1,0:T(8,128)(2,1)}, bf16[8,2,32,384]{3,2,1,0:T(8,128)(2,1)S(1)}, u32[]{:S(2)}, u32[]{:S(2)}) collective-permute-start(bf16[8,2,32,384]{3,2,1,0:T(8,128)(2,1)} %collective-permute-done.6.rest_2_.refs_5_), channel_id=1, source_target_pairs={{0,14},{2,0},{4,2},{6,4},{8,6},{10,8},{12,10},{14,12},{1,15},{3,1}... | collective-permute-start | bytes 1179656 | tf_op jit(solution)/shard_map/ppermute | solution.py:326
  92.4 18.9 %collective-permute-start.10 = (bf16[8,2,32,384]{3,2,1,0:T(8,128)(2,1)S(1)}, bf16[8,2,32,384]{3,2,1,0:T(8,128)(2,1)S(1)}, u32[]{:S(2)}, u32[]{:S(2)}) collective-permute-start(bf16[8,2,32,384]{3,2,1,0:T(8,128)(2,1)S(1)} %collective-permute-done.8.rest_0_.refs_7_), channel_id=1, source_target_pairs={{0,2},{2,4},{4,6},{6,8},{8,10},{10,12},{12,14},{14,0},{1,3},{3,5},... | collective-permute-start | bytes 1179656 | tf_op jit(solution)/shard_map/ppermute | solution.py:326
  92.4 18.9 %collective-permute-start.12 = (bf16[8,2,32,384]{3,2,1,0:T(8,128)(2,1)S(1)}, bf16[8,2,32,384]{3,2,1,0:T(8,128)(2,1)S(1)}, u32[]{:S(2)}, u32[]{:S(2)}) collective-permute-start(bf16[8,2,32,384]{3,2,1,0:T(8,128)(2,1)S(1)} %collective-permute-done.11.rest_5_.refs_4_), channel_id=1, source_target_pairs={{0,14},{2,0},{4,2},{6,4},{8,6},{10,8},{12,10},{14,12},{1,15},{3,1}... | collective-permute-start | bytes 1179656 | tf_op jit(solution)/shard_map/ppermute | solution.py:326
  115.2 86.1 %reduce-scatter.5.cloned.1.call-start = ((), (), s32[]{:S(2)}) async-start(), calls=%async_computation.5 | async-start | bytes 7077888 | tf_op jit(solution)/shard_map/reduce_scatter | solution.py:405
  126.1 42.6 %copy-start.7 = (bf16[8,2,32,384]{3,2,1,0:T(8,128)(2,1)S(1)}, bf16[8,2,32,384]{3,2,1,0:T(8,128)(2,1)}, u32[]{:S(2)}) copy-start(bf16[8,2,32,384]{3,2,1,0:T(8,128)(2,1)} %get-tuple-element.21.refs_4_) | copy-start | bytes 1179652
  126.1 42.6 %copy-start.9 = (bf16[8,2,32,384]{3,2,1,0:T(8,128)(2,1)S(1)}, bf16[8,2,32,384]{3,2,1,0:T(8,128)(2,1)}, u32[]{:S(2)}) copy-start(bf16[8,2,32,384]{3,2,1,0:T(8,128)(2,1)} %get-tuple-element.20.refs_3_) | copy-start | bytes 1179652
  126.1 42.6 %copy-start.11 = (bf16[8,2,32,384]{3,2,1,0:T(8,128)(2,1)S(1)}, bf16[8,2,32,384]{3,2,1,0:T(8,128)(2,1)}, u32[]{:S(2)}) copy-start(bf16[8,2,32,384]{3,2,1,0:T(8,128)(2,1)} %copy-done.10) | copy-start | bytes 1179652
  126.8 17.6 %all-to-all-start.1 = ((f32[16,8,256]{2,1,0:T(8,128)}), f32[16,8,256]{2,1,0:T(8,128)S(1)}, u32[]{:S(2)}, u32[]{:S(2)}) async-start(f32[16,8,256]{2,1,0:T(8,128)} %broadcast_in_dim.10), calls=%async_computation.3 | async-start | bytes 262144 | tf_op jit(solution)/shard_map/all_to_all | solution.py:347
  175.3 39.7 %copy-start.22 = (f32[8,256]{1,0:T(8,128)S(1)}, f32[8,256]{1,0:T(8,128)}, u32[]{:S(2)}) copy-start(f32[8,256]{1,0:T(8,128)} %reduce_sum.9.refs_2_.sum_ref) | copy-start | bytes 24580
  202.2 12.7 %collective-permute-start.14 = (bf16[512,384]{1,0:T(8,128)(2,1)S(1)}, bf16[512,384]{1,0:T(8,128)(2,1)S(1)}, u32[]{:S(2)}, u32[]{:S(2)}) collective-permute-start(bf16[512,384]{1,0:T(8,128)(2,1)S(1)} %dynamic-slice_bitcast_fusion), channel_id=1, source_target_pairs={{0,1},{1,0},{2,3},{3,2},{4,5},{5,4},{6,7},{7,6},{8,9},{9,8},{10,11... | collective-permute-start | bytes 1179656 | tf_op jit(solution)/shard_map/ppermute | solution.py:330
  (23 other events, 337.8 us)
Sparse Core Ops, SparseCore 0:
  11.3 16.3 reduce-scatter.2
  126.3 74.8 reduce-scatter.4
Sparse Core Ops, SparseCore 1:
  12.7 79.2 all-gather.4
  115.2 53.4 all-gather.6

commit v3 on v2

--- a/solution.py
+++ b/solution.py
@@ -17,7 +17,6 @@
 D = 6144
 SUB = ROWS // NZ
 EXT = ROWS + 16
-STEP = 4
 KSTEP = 4
 COST = pl.CostEstimate(flops=1000, bytes_accessed=1000, transcendentals=0)
 VMEM = 52 * 1024 * 1024
@@ -132,39 +131,6 @@
 def head_back(g, n, s, gain):
     e = g * gain
     return (e - jnp.mean(e, -1, keepdims=True) - n * jnp.mean(e * n, -1, keepdims=True)) * s
-
-
-def proj_kernel(hid_ref, cot_ref, w_ref, *rest):
-    out_ref = rest[-1]
-    i = pl.program_id(0)
-    cols = pl.ds(pl.multiple_of(i * KSTEP * SL, KSTEP * SL), KSTEP * SL)
-    h = hid_ref[:, cols]
-    c = cot_ref[:, cols]
-    for j in range(4):
-        rows = EXT if j < 3 else ROWS
-        new = dot(h if j < 3 else c, w_ref[:, j].reshape(KSTEP * SL, HW), 1, 0)
-
-        @pl.when(i == 0)
-        def _():
-            out_ref[:rows, j * HW : (j + 1) * HW] = new
-
-        @pl.when(i > 0)
-        def _():
-            out_ref[:rows, j * HW : (j + 1) * HW] += new
-
-
-def proj_call(hid, cot, w, after):
-    return pl.pallas_call(
-        proj_kernel,
-        grid=(NDP // KSTEP,),
-        in_specs=[pl.BlockSpec(memory_space=pltpu.VMEM)] * 2
-        + [pl.BlockSpec((KSTEP, 4, SL, HW), lambda i: (i, 0, 0, 0))]
-        + [ANY] * len(after),
-        out_specs=pl.BlockSpec((EXT, 4 * HW), lambda i: (0, 0)),
-        out_shape=jax.ShapeDtypeStruct((EXT, 4 * HW), F32),
-        compiler_params=params(),
-        cost_estimate=COST,
-    )(hid, cot, w, *after)
 
 
 def attn_kernel(acc_ref, qg_ref, kg_ref, *rest):
@@ -211,44 +177,73 @@
     sum_ref[...] = jnp.where(row == 0, total[0], total[1])
 
 
-def attn_call(acc, qg, kg, after):
+def core_kernel(hid_in, cot_in, w_in, qg_ref, kg_ref, *rest):
+    g_ref, sum_ref, out_ref, hid, cot, w, acc, out, sems, out_sems = rest[-10:]
+    groups = NDP // KSTEP
+    loads = []
+    for i in range(groups):
+        cols = slice(i * KSTEP * SL, (i + 1) * KSTEP * SL)
+        span = slice(i * KSTEP, (i + 1) * KSTEP)
+        pairs = [
+            (hid_in.at[:, cols], hid.at[:, cols]),
+            (cot_in.at[:, cols], cot.at[:, cols]),
+            (w_in.at[span], w.at[span]),
+        ]
+        loads.append([pltpu.make_async_copy(a, b, sems.at[i, n]) for n, (a, b) in enumerate(pairs)])
+    for group in loads:
+        for copy in group:
+            copy.start()
+    for i, group in enumerate(loads):
+        for copy in group:
+            copy.wait()
+        cols = slice(i * KSTEP * SL, (i + 1) * KSTEP * SL)
+        for j in range(4):
+            rows = EXT if j < 3 else ROWS
+            src = hid if j < 3 else cot
+            wj = w[i * KSTEP : (i + 1) * KSTEP, j].reshape(KSTEP * SL, HW)
+            new = dot(src[:, cols], wj, 1, 0)
+            dst = slice(j * HW, (j + 1) * HW)
+            acc[:rows, dst] = new if i == 0 else acc[:rows, dst] + new
+    attn_kernel(acc, qg_ref, kg_ref, g_ref, sum_ref)
+    stores = []
+    for i in range(groups):
+        for s in range(i * KSTEP, (i + 1) * KSTEP):
+            t = 0.0
+            for j in range(3):
+                t = t + dot(g_ref[:, j * HW : (j + 1) * HW], w[s, j], 1, 1)
+            out[s, :ROWS] = t.astype(BF)
+            out[s, ROWS:] = dot(g_ref[:, 3 * HW :], w[s, 3], 1, 1).astype(BF)
+        span = slice(i * KSTEP, (i + 1) * KSTEP)
+        stores.append(pltpu.make_async_copy(out.at[span], out_ref.at[span], out_sems.at[i]))
+        stores[-1].start()
+    for copy in stores:
+        copy.wait()
+
+
+def core_call(hid, cot, w, qg, kg, after):
     full = lambda shape: pl.BlockSpec(shape, lambda: (0, 0))
-    return pl.pallas_call(
-        attn_kernel,
-        in_specs=[full((EXT, 4 * HW)), full((1, HW)), full((1, HW))]
-        + [pl.BlockSpec(memory_space=pl.ANY)] * len(after),
-        out_specs=[full((ROWS, 4 * HW)), full((8, ROWS))],
+    groups = NDP // KSTEP
+    return pl.pallas_call(
+        core_kernel,
+        in_specs=[ANY] * 3 + [full((1, HW)), full((1, HW))] + [ANY] * len(after),
+        out_specs=[full((ROWS, 4 * HW)), full((8, ROWS)), ANY],
         out_shape=[
             jax.ShapeDtypeStruct((ROWS, 4 * HW), BF),
             jax.ShapeDtypeStruct((8, ROWS), F32),
+            jax.ShapeDtypeStruct((NDP, 2 * ROWS, SL), BF),
+        ],
+        scratch_shapes=[
+            pltpu.VMEM((EXT, D), BF),
+            pltpu.VMEM((ROWS, D), BF),
+            pltpu.VMEM((NDP, 4, SL, HW), BF),
+            pltpu.VMEM((EXT, 4 * HW), F32),
+            pltpu.VMEM((NDP, 2 * ROWS, SL), BF),
+            pltpu.SemaphoreType.DMA((groups, 3)),
+            pltpu.SemaphoreType.DMA((groups,)),
         ],
         compiler_params=params(),
         cost_estimate=COST,
-    )(acc, qg.reshape(1, HW), kg.reshape(1, HW), *after)
-
-
-def back_kernel(g_ref, w_ref, out_ref):
-    for s in range(STEP):
-        t = dot(g_ref[:, :HW], w_ref[s, 0], 1, 1)
-        t += dot(g_ref[:, HW : 2 * HW], w_ref[s, 1], 1, 1)
-        t += dot(g_ref[:, 2 * HW : 3 * HW], w_ref[s, 2], 1, 1)
-        out_ref[s, :ROWS] = t.astype(BF)
-        out_ref[s, ROWS:] = dot(g_ref[:, 3 * HW :], w_ref[s, 3], 1, 1).astype(BF)
-
-
-def back_call(g, w):
-    return pl.pallas_call(
-        back_kernel,
-        grid=(NDP // STEP,),
-        in_specs=[
-            pl.BlockSpec((ROWS, 4 * HW), lambda i: (0, 0)),
-            pl.BlockSpec((STEP, 4, SL, HW), lambda i: (i, 0, 0, 0)),
-        ],
-        out_specs=pl.BlockSpec((STEP, 2 * ROWS, SL), lambda i: (i, 0, 0)),
-        out_shape=jax.ShapeDtypeStruct((NDP, 2 * ROWS, SL), BF),
-        compiler_params=params(),
-        cost_estimate=COST,
-    )(g, w)
+    )(hid, cot, w, qg.reshape(1, HW), kg.reshape(1, HW), *after)
 
 
 def weight_kernel(part, z_ref, *refs):
@@ -333,13 +328,12 @@
 def ring_gather(own, hid):
     half = NDP // 2
     a, b = own[:half], own[half:]
-    ra, la, rb, lb = order((shift(a, 1), shift(a, -1), shift(b, 1), shift(b, -1)), (hid,))
-    right, left = [(ra, rb)], [(la, lb)]
+    ra, la = order((shift(a, 1), shift(a, -1)), (hid,))
+    right, left = [(ra, shift(b, 1))], [(la, shift(b, -1))]
     for _ in range(2):
         right.append(tuple(shift(x, 1) for x in right[-1]))
         left.append(tuple(shift(x, -1) for x in left[-1]))
-    far = shift(right[-1][0], 1), shift(left[-1][1], -1)
-    return [(a, b)] + right + [far] + left[::-1]
+    return [(a, b)] + right + left[::-1]
 
 
 def all_sum(a):
@@ -398,15 +392,18 @@
     rows = rows_call(scalars, tokens, cotangent, layer_norm_gain)
     moved = ring_gather(lax.all_to_all(rows, DP, 0, 0, tiled=True), hid)
 
-    acc = proj_call(hid, cotangent, w, moved[2] + moved[6] + (side,))
-    grads, sums = attn_call(acc, query_gain, key_gain, moved[3] + moved[4] + moved[5])
+    (ra, rb), (la, lb) = moved[3], moved[4]
+    grads, sums, terms = core_call(
+        hid, cotangent, w, query_gain, key_gain, moved[3] + moved[4] + (side,)
+    )
     all_grads = lax.all_gather(grads, DP, axis=0)
-    terms = back_call(grads, w)
     part = lax.psum_scatter(
         terms.reshape(NDP * 2 * ROWS, SL), "z", scatter_dimension=0, tiled=True
     ).reshape(NYH, 2 * ROWS, SL)
     sums = all_sum(sums)
-    flat = [x for pair in moved for x in pair]
+    ra, lb = order((ra, lb), (terms,))
+    flat = [x for pair in moved[:3] for x in pair] + [ra, rb]
+    flat += [shift(ra, 1), shift(lb, -1), la, lb] + [x for pair in moved[5:] for x in pair]
     partial = weight_call(0, scalars, flat[:NZ], all_grads, ())
     grad_w, grad_o = weight_call(1, scalars, flat[NZ:], all_grads, partial)
     (part,) = order((part,), (grad_w, sums))

time: 227 us -> 217 us (0.956)
  Pallas kernels: 50.8 us -> 38.1 us
  waiting for transfers between devices: 94 us -> 96.3 us
    pallas_call x3 -> x1, Pallas kernels: 28.2 us -> 15.6 us  [core_call(): pl.pallas_call(core_kernel, in_specs=[ANY] * 3 + [full((1, HW)), full((1,...]
    all_gather x1, waiting for transfers between devices: 23.7 us -> 31.1 us  [local(): all_grads = lax.all_gather(grads, DP, axis=0)]
    reduce_scatter x1, waiting for transfers between devices: 19.9 us -> 12.5 us  [local(): lax.psum_scatter(terms.reshape(NDP * 2 * ROWS, SL), 'z', scatter_dimensio...]
    unnamed x54 -> x42, local copies, waits for them, and re-layouts: 6.76 us -> 6.59 us
  transfers between devices with their start and end apart: 20 -> 20, of which waited for: 10 -> 12; matrix products, arithmetic and copies ran while one was open for 1% -> 1% of each run, Pallas kernels for 20% -> 9%
where the time goes in v3:
time: 217 us; the launch traced here: 216 us
  waiting for transfers between devices  96.3 us (44%)
  Pallas kernels  38.1 us (18%)
  starting transfers between devices  37 us (17%)
  blocking collectives  18.2 us (8%)
  between operations  15.7 us (7%)
  local copies, waits for them, and re-layouts  8.37 us (4%)
  other arithmetic  2.82 us (1%)
    all_gather x1, waiting for transfers between devices, local(): all_grads = lax.all_gather(grads, DP, axis=0)  31.1 us
    ppermute x14, waiting for transfers between devices, shift(): return lax.ppermute(a, 'z', [(i, (i + k) % NZ) for i in range(NZ)])  29.8 us
    ppermute x14, starting transfers between devices, shift(): return lax.ppermute(a, 'z', [(i, (i + k) % NZ) for i in range(NZ)])  28.2 us
    all_to_all x1, blocking collectives, local(): moved = ring_gather(lax.all_to_all(rows, DP, 0, 0, tiled=True), hid)  18.2 us
    pallas_call x1, Pallas kernels, core_call(): pl.pallas_call(core_kernel, in_specs=[ANY] * 3 + [full((1, HW)), full((1,...  15.6 us
    reduce_scatter x1, waiting for transfers between devices, local(): lax.psum_scatter(terms.reshape(NDP * 2 * ROWS, SL), 'z', scatter_dimensio...  12.5 us
    ppermute x1, waiting for transfers between devices, swap_yh(): return lax.ppermute(a, 'yh', [(0, 1), (1, 0)])  12.1 us
    pallas_call x2, Pallas kernels, weight_call(): pl.pallas_call(lambda *refs: weight_kernel(part, *refs), grid_spec=pltpu....  11.7 us
  transfers between devices with their start and end apart: 20, of which 12 were waited for; matrix products, arithmetic and copies ran while one was open for 1% of the time, Pallas kernels for 9%

profile of v3, /device:TPU:16, one launch (start us, length us, event | category | flops | bytes accessed | tf_op | source)
XLA Modules:
  0.0 216.5 jit_solution(5215347039703097238)
XLA Ops:
  13.7 18.2 %all_to_all.10 = bf16[16,2,32,384]{3,2,1,0:T(8,128)(2,1)S(1)} all-to-all(bf16[16,2,32,384]{3,2,1,0:T(8,128)(2,1)S(1)} %shard_map.103), channel_id=1, replica_groups=mesh['x'=4,'yl'=2,'c'=2,'z'=8,'yh'=2] {'x','yl','c'}, dimensions={0} | all-to-all | bytes 1572864 | tf_op jit(solution)/shard_map/all_to_all | solution.py:393
  32.0 8.1 %collective-permute-start.9 = (bf16[8,2,32,384]{3,2,1,0:T(8,128)(2,1)S(1)}, bf16[8,2,32,384]{3,2,1,0:T(8,128)(2,1)S(1)}, u32[]{:S(2)}, u32[]{:S(2)}) collective-permute-start(bf16[8,2,32,384]{3,2,1,0:T(8,128)(2,1)S(1)} %get-tuple-element.36.refs_2_), channel_id=1, source_target_pairs={{0,14},{2,0},{4,2},{6,4},{8,6},{10,8},{12,10},{14,12},{1,15},{3,1}... | collective-permute-start | bytes 1179656 | tf_op jit(solution)/shard_map/ppermute | solution.py:321
  40.1 3.2 %collective-permute-start.1 = (bf16[8,2,32,384]{3,2,1,0:T(8,128)(2,1)S(1)}, bf16[8,2,32,384]{3,2,1,0:T(8,128)(2,1)S(1)}, u32[]{:S(2)}, u32[]{:S(2)}) collective-permute-start(bf16[8,2,32,384]{3,2,1,0:T(8,128)(2,1)S(1)} %get-tuple-element.37.refs_1_), channel_id=1, source_target_pairs={{0,14},{2,0},{4,2},{6,4},{8,6},{10,8},{12,10},{14,12},{1,15},{3,1}... | collective-permute-start | bytes 1179656 | tf_op jit(solution)/shard_map/ppermute | solution.py:321
  43.4 6.2 %shard_map.102 = (bf16[272,6144]{1,0:T(8,128)(2,1)}, f32[256,1]{1,0:T(8,128)S(1)}, f32[256,1]{1,0:T(8,128)S(1)}) custom-call(bf16[256,6144]{1,0:T(8,128)(2,1)} %tok_ref.5, f32[1,6144]{1,0:T(1,128)S(1)} %bitcast.17), custom_call_target="tpu_custom_call" | custom-call | flops 1000 | bytes 1000 | tf_op jit(solution)/shard_map/pallas_call | solution.py:76
  50.9 3.2 %collective-permute-start.10 = (bf16[8,2,32,384]{3,2,1,0:T(8,128)(2,1)S(1)}, bf16[8,2,32,384]{3,2,1,0:T(8,128)(2,1)}, u32[]{:S(2)}, u32[]{:S(2)}) collective-permute-start(bf16[8,2,32,384]{3,2,1,0:T(8,128)(2,1)S(1)} %collective-permute-done.9.refs_8_), channel_id=1, source_target_pairs={{0,14},{2,0},{4,2},{6,4},{8,6},{10,8},{12,10},{14,12},{1,15},{3,1}... | collective-permute-start | bytes 1179656 | tf_op jit(solution)/shard_map/ppermute | solution.py:321
  54.2 3.3 %collective-permute-done.1.refs_1_ = bf16[8,2,32,384]{3,2,1,0:T(8,128)(2,1)S(1)} collective-permute-done((bf16[8,2,32,384]{3,2,1,0:T(8,128)(2,1)S(1)}, bf16[8,2,32,384]{3,2,1,0:T(8,128)(2,1)S(1)}, u32[]{:S(2)}, u32[]{:S(2)}) %collective-permute-start.1) | collective-permute-done | bytes 393248 | tf_op jit(solution)/shard_map/ppermute | solution.py:321
  57.5 3.9 %collective-permute-done.refs_0_ = bf16[8,2,32,384]{3,2,1,0:T(8,128)(2,1)S(1)} collective-permute-done((bf16[8,2,32,384]{3,2,1,0:T(8,128)(2,1)S(1)}, bf16[8,2,32,384]{3,2,1,0:T(8,128)(2,1)S(1)}, u32[]{:S(2)}, u32[]{:S(2)}) %collective-permute-start) | collective-permute-done | bytes 393248 | tf_op jit(solution)/shard_map/ppermute | solution.py:321
  62.2 3.2 %collective-permute-start.7 = (bf16[8,2,32,384]{3,2,1,0:T(8,128)(2,1)}, bf16[8,2,32,384]{3,2,1,0:T(8,128)(2,1)S(1)}, u32[]{:S(2)}, u32[]{:S(2)}) collective-permute-start(bf16[8,2,32,384]{3,2,1,0:T(8,128)(2,1)} %get-tuple-element.22.refs_7_), channel_id=1, source_target_pairs={{0,14},{2,0},{4,2},{6,4},{8,6},{10,8},{12,10},{14,12},{1,15},{3,1}... | collective-permute-start | bytes 1179656 | tf_op jit(solution)/shard_map/ppermute | solution.py:321
  65.9 3.8 %collective-permute-start.11 = (bf16[8,2,32,384]{3,2,1,0:T(8,128)(2,1)}, bf16[8,2,32,384]{3,2,1,0:T(8,128)(2,1)S(1)}, u32[]{:S(2)}, u32[]{:S(2)}) collective-permute-start(bf16[8,2,32,384]{3,2,1,0:T(8,128)(2,1)} %collective-permute-done.10.refs_6_), channel_id=1, source_target_pairs={{0,14},{2,0},{4,2},{6,4},{8,6},{10,8},{12,10},{14,12},{1,15},{3,1}... | collective-permute-start | bytes 1179656 | tf_op jit(solution)/shard_map/ppermute | solution.py:321
  69.9 8.3 %collective-permute-done.2.refs_5_ = bf16[8,2,32,384]{3,2,1,0:T(8,128)(2,1)S(1)} collective-permute-done((bf16[8,2,32,384]{3,2,1,0:T(8,128)(2,1)}, bf16[8,2,32,384]{3,2,1,0:T(8,128)(2,1)S(1)}, u32[]{:S(2)}, u32[]{:S(2)}) %collective-permute-start.2) | collective-permute-done | bytes 393248 | tf_op jit(solution)/shard_map/ppermute | solution.py:321
  78.3 3.2 %collective-permute-start.8 = (bf16[8,2,32,384]{3,2,1,0:T(8,128)(2,1)S(1)}, bf16[8,2,32,384]{3,2,1,0:T(8,128)(2,1)S(1)}, u32[]{:S(2)}, u32[]{:S(2)}) collective-permute-start(bf16[8,2,32,384]{3,2,1,0:T(8,128)(2,1)S(1)} %collective-permute-done.7.refs_5_), channel_id=1, source_target_pairs={{0,14},{2,0},{4,2},{6,4},{8,6},{10,8},{12,10},{14,12},{1,15},{3,1}... | collective-permute-start | bytes 1179656 | tf_op jit(solution)/shard_map/ppermute | solution.py:321
  81.5 2.2 %collective-permute-done.11.rest_3_.refs_1_ = bf16[8,2,32,384]{3,2,1,0:T(8,128)(2,1)S(1)} collective-permute-done((bf16[8,2,32,384]{3,2,1,0:T(8,128)(2,1)}, bf16[8,2,32,384]{3,2,1,0:T(8,128)(2,1)S(1)}, u32[]{:S(2)}, u32[]{:S(2)}) %collective-permute-start.11) | collective-permute-done | bytes 393248 | tf_op jit(solution)/shard_map/ppermute | solution.py:321
  83.7 2.9 %collective-permute-done.6.rest_1_.refs_8_ = bf16[8,2,32,384]{3,2,1,0:T(8,128)(2,1)S(1)} collective-permute-done((bf16[8,2,32,384]{3,2,1,0:T(8,128)(2,1)}, bf16[8,2,32,384]{3,2,1,0:T(8,128)(2,1)S(1)}, u32[]{:S(2)}, u32[]{:S(2)}) %collective-permute-start.6) | collective-permute-done | bytes 393248 | tf_op jit(solution)/shard_map/ppermute | solution.py:321
  86.7 8.4 %collective-permute-done.3.rest_0_.refs_0_ = bf16[8,2,32,384]{3,2,1,0:T(8,128)(2,1)S(1)} collective-permute-done((bf16[8,2,32,384]{3,2,1,0:T(8,128)(2,1)S(1)}, bf16[8,2,32,384]{3,2,1,0:T(8,128)(2,1)S(1)}, u32[]{:S(2)}, u32[]{:S(2)}) %collective-permute-start.3) | collective-permute-done | bytes 393248 | tf_op jit(solution)/shard_map/ppermute | solution.py:321
  96.9 15.6 %shard_map.105 = (bf16[256,1024]{1,0:T(8,128)(2,1)}, f32[8,256]{1,0:T(8,128)S(1)}, bf16[16,512,384]{2,1,0:T(8,128)(2,1)}) custom-call(bf16[272,6144]{1,0:T(8,128)(2,1)} %get-tuple-element.20.refs_2_.hid_in, bf16[256,6144]{1,0:T(8,128)(2,1)} %cot_in.1, bf16[16,4,384,256]{3,2,1,0:T(8,128)(2,1)} %bitcast.26, f32[1,256]{1,0:T(1,128)S(1)} %bitcast.19, ...), custom_call_target="tpu_custom_call" | custom-call | flops 1000 | bytes 1000 | tf_op jit(solution)/shard_map/pallas_call | solution.py:226
  113.4 3.2 %collective-permute-start.13 = (bf16[8,2,32,384]{3,2,1,0:T(8,128)(2,1)}, bf16[8,2,32,384]{3,2,1,0:T(8,128)(2,1)S(1)}, u32[]{:S(2)}, u32[]{:S(2)}) collective-permute-start(bf16[8,2,32,384]{3,2,1,0:T(8,128)(2,1)} %get-tuple-element.25.refs_4_), channel_id=1, source_target_pairs={{0,14},{2,0},{4,2},{6,4},{8,6},{10,8},{12,10},{14,12},{1,15},{3,1}... | collective-permute-start | bytes 1179656 | tf_op jit(solution)/shard_map/ppermute | solution.py:321
  117.3 8.0 %all-to-all-start.1 = ((f32[16,8,256]{2,1,0:T(8,128)}), f32[16,8,256]{2,1,0:T(8,128)S(1)}, u32[]{:S(2)}, u32[]{:S(2)}) async-start(f32[16,8,256]{2,1,0:T(8,128)} %broadcast_in_dim.10), calls=%async_computation.3 | async-start | bytes 262144 | tf_op jit(solution)/shard_map/all_to_all | solution.py:341
  125.3 9.6 %all-to-all-done.1 = f32[16,8,256]{2,1,0:T(8,128)S(1)} async-done(((f32[16,8,256]{2,1,0:T(8,128)}), f32[16,8,256]{2,1,0:T(8,128)S(1)}, u32[]{:S(2)}, u32[]{:S(2)}) %all-to-all-start.1) | async-done | bytes 131104 | tf_op jit(solution)/shard_map/all_to_all | solution.py:341
  135.5 31.1 %all-gather.7.cloned.1.call-done = bf16[4096,1024]{1,0:T(8,128)(2,1)} async-done(((bf16[256,1024]{1,0:T(8,128)(2,1)}), bf16[4096,1024]{1,0:T(8,128)(2,1)}) %all-gather.7.cloned.1.call-update) | async-done | bytes 8388624 | tf_op jit(solution)/shard_map/all_gather | solution.py:399
  166.6 5.7 %shard_map.107 = (f32[384,768]{1,0:T(8,128)}, f32[384,256]{1,0:T(8,128)S(1)}) custom-call(s32[3]{0:T(128)S(1)} %pad_add_fusion.z_ref.refs_0_.s_ref, bf16[8,2,32,384]{3,2,1,0:T(8,128)(2,1)S(1)} %get-tuple-element.37.refs_1_, bf16[8,2,32,384]{3,2,1,0:T(8,128)(2,1)S(1)} %get-tuple-element.36.refs_2_, bf16[8,2,32,384]{3,2,1,0:T(8,128)(2,1)S(1)} %copy-done.6, ...), custom_call_target="tpu_custom_call" | custom-call | flops 1000 | bytes 1000 | tf_op jit(solution)/shard_map/pallas_call | solution.py:303
  173.1 6.0 %shard_map.108 = (bf16[3,384,256]{2,1,0:T(8,128)(2,1)}, bf16[384,256]{1,0:T(8,128)(2,1)}) custom-call(s32[3]{0:T(128)S(1)} %pad_add_fusion.z_ref.refs_0_.s_ref, bf16[8,2,32,384]{3,2,1,0:T(8,128)(2,1)S(1)} %collective-permute-done.12.refs_1_, bf16[8,2,32,384]{3,2,1,0:T(8,128)(2,1)S(1)} %collective-permute-done.13.refs_2_, ...), custom_call_target="tpu_custom_call" | custom-call | flops 1000 | bytes 1000 | tf_op jit(solution)/shard_map/pallas_call | solution.py:303
  179.1 12.5 %reduce-scatter.5.cloned.1.call-done = bf16[1024,384]{1,0:T(8,128)(2,1)} async-done(((bf16[8192,384]{1,0:T(8,128)(2,1)}), bf16[1024,384]{1,0:T(8,128)(2,1)}) %reduce-scatter.5.cloned.1.call-update) | async-done | bytes 786448 | tf_op jit(solution)/shard_map/reduce_scatter | solution.py:400
  193.3 12.1 %collective-permute-done.14.recv_ref = bf16[512,384]{1,0:T(8,128)(2,1)S(1)} collective-permute-done((bf16[512,384]{1,0:T(8,128)(2,1)S(1)}, bf16[512,384]{1,0:T(8,128)(2,1)S(1)}, u32[]{:S(2)}, u32[]{:S(2)}) %collective-permute-start.14) | collective-permute-done | bytes 393248 | tf_op jit(solution)/shard_map/ppermute | solution.py:325
  206.5 2.6 %shard_map.110 = (bf16[256,384]{1,0:T(8,128)(2,1)}, bf16[256,384]{1,0:T(8,128)(2,1)}) custom-call(s32[3]{0:T(128)S(1)} %pad_add_fusion.z_ref.refs_0_.s_ref, bf16[2,512,384]{2,1,0:T(8,128)(2,1)S(1)} %copy-done, bf16[512,384]{1,0:T(8,128)(2,1)S(1)} %collective-permute-done.14.recv_ref, f32[8,256]{1,0:T(8,128)S(1)} %copy-done.15, bf16[256,6144]{1,0:T(8,128)(2,1)} %tok_ref.5, ...), custom_call_target="tpu_custom_call" | custom-call | flops 1000 | bytes 1000 | tf_op jit(solution)/shard_map/pallas_call | solution.py:359
  (78 shorter events, 16.1 us)
Async XLA Ops:
  8.0 73.5 %reduce-scatter.3.cloned.1.call-start = ((), (), s32[]{:S(2)}) async-start(), calls=%async_computation.4 | async-start | bytes 1179648 | tf_op jit(solution)/shard_map/reduce_scatter | solution.py:389
  10.2 84.9 %all-gather.5.cloned.1.call-start = ((), (), s32[]{:S(2)}) async-start(), calls=%async_computation.6 | async-start | bytes 13369344 | tf_op jit(solution)/shard_map/all_gather | solution.py:388
  10.8 155.8 %all-gather.7.cloned.1.call-start = ((), (), s32[]{:S(2)}) async-start(), calls=%async_computation.7 | async-start | bytes 8912896 | tf_op jit(solution)/shard_map/all_gather | solution.py:399
  32.0 18.9 %collective-permute-start.9 = (bf16[8,2,32,384]{3,2,1,0:T(8,128)(2,1)S(1)}, bf16[8,2,32,384]{3,2,1,0:T(8,128)(2,1)S(1)}, u32[]{:S(2)}, u32[]{:S(2)}) collective-permute-start(bf16[8,2,32,384]{3,2,1,0:T(8,128)(2,1)S(1)} %get-tuple-element.36.refs_2_), channel_id=1, source_target_pairs={{0,14},{2,0},{4,2},{6,4},{8,6},{10,8},{12,10},{14,12},{1,15},{3,1}... | collective-permute-start | bytes 1179656 | tf_op jit(solution)/shard_map/ppermute | solution.py:321
  40.1 14.0 %collective-permute-start.4 = (bf16[8,2,32,384]{3,2,1,0:T(8,128)(2,1)S(1)}, bf16[8,2,32,384]{3,2,1,0:T(8,128)(2,1)S(1)}, u32[]{:S(2)}, u32[]{:S(2)}) collective-permute-start(bf16[8,2,32,384]{3,2,1,0:T(8,128)(2,1)S(1)} %get-tuple-element.36.refs_2_), channel_id=1, source_target_pairs={{0,2},{2,4},{4,6},{6,8},{8,10},{10,12},{12,14},{14,0},{1,3},{3,5},... | collective-permute-start | bytes 1179656 | tf_op jit(solution)/shard_map/ppermute | solution.py:321
  40.1 55.0 %copy-start.16 = (f32[256]{0:T(256)S(1)}, f32[256]{0:T(256)}, u32[]{:S(2)}) copy-start(f32[256]{0:T(256)} %param.11) | copy-start | bytes 3076
  40.1 17.4 %collective-permute-start.1 = (bf16[8,2,32,384]{3,2,1,0:T(8,128)(2,1)S(1)}, bf16[8,2,32,384]{3,2,1,0:T(8,128)(2,1)S(1)}, u32[]{:S(2)}, u32[]{:S(2)}) collective-permute-start(bf16[8,2,32,384]{3,2,1,0:T(8,128)(2,1)S(1)} %get-tuple-element.37.refs_1_), channel_id=1, source_target_pairs={{0,14},{2,0},{4,2},{6,4},{8,6},{10,8},{12,10},{14,12},{1,15},{3,1}... | collective-permute-start | bytes 1179656 | tf_op jit(solution)/shard_map/ppermute | solution.py:321
  43.4 18.0 %collective-permute-start = (bf16[8,2,32,384]{3,2,1,0:T(8,128)(2,1)S(1)}, bf16[8,2,32,384]{3,2,1,0:T(8,128)(2,1)S(1)}, u32[]{:S(2)}, u32[]{:S(2)}) collective-permute-start(bf16[8,2,32,384]{3,2,1,0:T(8,128)(2,1)S(1)} %get-tuple-element.37.refs_1_), channel_id=1, source_target_pairs={{0,2},{2,4},{4,6},{6,8},{8,10},{10,12},{12,14},{14,0},{1,3},{3,5},... | collective-permute-start | bytes 1179656 | tf_op jit(solution)/shard_map/ppermute | solution.py:321
  50.9 15.0 %collective-permute-start.10 = (bf16[8,2,32,384]{3,2,1,0:T(8,128)(2,1)S(1)}, bf16[8,2,32,384]{3,2,1,0:T(8,128)(2,1)}, u32[]{:S(2)}, u32[]{:S(2)}) collective-permute-start(bf16[8,2,32,384]{3,2,1,0:T(8,128)(2,1)S(1)} %collective-permute-done.9.refs_8_), channel_id=1, source_target_pairs={{0,14},{2,0},{4,2},{6,4},{8,6},{10,8},{12,10},{14,12},{1,15},{3,1}... | collective-permute-start | bytes 1179656 | tf_op jit(solution)/shard_map/ppermute | solution.py:321
  54.2 15.8 %collective-permute-start.5 = (bf16[8,2,32,384]{3,2,1,0:T(8,128)(2,1)S(1)}, bf16[8,2,32,384]{3,2,1,0:T(8,128)(2,1)}, u32[]{:S(2)}, u32[]{:S(2)}) collective-permute-start(bf16[8,2,32,384]{3,2,1,0:T(8,128)(2,1)S(1)} %collective-permute-done.4.refs_4_), channel_id=1, source_target_pairs={{0,2},{2,4},{4,6},{6,8},{8,10},{10,12},{12,14},{14,0},{1,3},{3,5},... | collective-permute-start | bytes 1179656 | tf_op jit(solution)/shard_map/ppermute | solution.py:321
  62.2 16.1 %collective-permute-start.2 = (bf16[8,2,32,384]{3,2,1,0:T(8,128)(2,1)}, bf16[8,2,32,384]{3,2,1,0:T(8,128)(2,1)S(1)}, u32[]{:S(2)}, u32[]{:S(2)}) collective-permute-start(bf16[8,2,32,384]{3,2,1,0:T(8,128)(2,1)} %get-tuple-element.21.refs_3_), channel_id=1, source_target_pairs={{0,2},{2,4},{4,6},{6,8},{8,10},{10,12},{12,14},{14,0},{1,3},{3,5},... | collective-permute-start | bytes 1179656 | tf_op jit(solution)/shard_map/ppermute | solution.py:321
  62.2 16.1 %collective-permute-start.7 = (bf16[8,2,32,384]{3,2,1,0:T(8,128)(2,1)}, bf16[8,2,32,384]{3,2,1,0:T(8,128)(2,1)S(1)}, u32[]{:S(2)}, u32[]{:S(2)}) collective-permute-start(bf16[8,2,32,384]{3,2,1,0:T(8,128)(2,1)} %get-tuple-element.22.refs_7_), channel_id=1, source_target_pairs={{0,14},{2,0},{4,2},{6,4},{8,6},{10,8},{12,10},{14,12},{1,15},{3,1}... | collective-permute-start | bytes 1179656 | tf_op jit(solution)/shard_map/ppermute | solution.py:321
  65.9 17.8 %collective-permute-start.11 = (bf16[8,2,32,384]{3,2,1,0:T(8,128)(2,1)}, bf16[8,2,32,384]{3,2,1,0:T(8,128)(2,1)S(1)}, u32[]{:S(2)}, u32[]{:S(2)}) collective-permute-start(bf16[8,2,32,384]{3,2,1,0:T(8,128)(2,1)} %collective-permute-done.10.refs_6_), channel_id=1, source_target_pairs={{0,14},{2,0},{4,2},{6,4},{8,6},{10,8},{12,10},{14,12},{1,15},{3,1}... | collective-permute-start | bytes 1179656 | tf_op jit(solution)/shard_map/ppermute | solution.py:321
  69.9 16.7 %collective-permute-start.6 = (bf16[8,2,32,384]{3,2,1,0:T(8,128)(2,1)}, bf16[8,2,32,384]{3,2,1,0:T(8,128)(2,1)S(1)}, u32[]{:S(2)}, u32[]{:S(2)}) collective-permute-start(bf16[8,2,32,384]{3,2,1,0:T(8,128)(2,1)} %collective-permute-done.5.refs_6_), channel_id=1, source_target_pairs={{0,2},{2,4},{4,6},{6,8},{8,10},{10,12},{12,14},{14,0},{1,3},{3,5},... | collective-permute-start | bytes 1179656 | tf_op jit(solution)/shard_map/ppermute | solution.py:321
  78.3 16.9 %collective-permute-start.3 = (bf16[8,2,32,384]{3,2,1,0:T(8,128)(2,1)S(1)}, bf16[8,2,32,384]{3,2,1,0:T(8,128)(2,1)S(1)}, u32[]{:S(2)}, u32[]{:S(2)}) collective-permute-start(bf16[8,2,32,384]{3,2,1,0:T(8,128)(2,1)S(1)} %collective-permute-done.2.refs_5_), channel_id=1, source_target_pairs={{0,2},{2,4},{4,6},{6,8},{8,10},{10,12},{12,14},{14,0},{1,3},{3,5},... | collective-permute-start | bytes 1179656 | tf_op jit(solution)/shard_map/ppermute | solution.py:321
  78.3 16.8 %collective-permute-start.8 = (bf16[8,2,32,384]{3,2,1,0:T(8,128)(2,1)S(1)}, bf16[8,2,32,384]{3,2,1,0:T(8,128)(2,1)S(1)}, u32[]{:S(2)}, u32[]{:S(2)}) collective-permute-start(bf16[8,2,32,384]{3,2,1,0:T(8,128)(2,1)S(1)} %collective-permute-done.7.refs_5_), channel_id=1, source_target_pairs={{0,14},{2,0},{4,2},{6,4},{8,6},{10,8},{12,10},{14,12},{1,15},{3,1}... | collective-permute-start | bytes 1179656 | tf_op jit(solution)/shard_map/ppermute | solution.py:321
  112.6 79.0 %reduce-scatter.5.cloned.1.call-start = ((), (), s32[]{:S(2)}) async-start(), calls=%async_computation.5 | async-start | bytes 7077888 | tf_op jit(solution)/shard_map/reduce_scatter | solution.py:400
  113.3 53.2 %copy-start.6 = (bf16[8,2,32,384]{3,2,1,0:T(8,128)(2,1)S(1)}, bf16[8,2,32,384]{3,2,1,0:T(8,128)(2,1)}, u32[]{:S(2)}) copy-start(bf16[8,2,32,384]{3,2,1,0:T(8,128)(2,1)} %get-tuple-element.21.refs_3_) | copy-start | bytes 1179652
  113.4 59.7 %collective-permute-start.12 = (bf16[8,2,32,384]{3,2,1,0:T(8,128)(2,1)}, bf16[8,2,32,384]{3,2,1,0:T(8,128)(2,1)S(1)}, u32[]{:S(2)}, u32[]{:S(2)}) collective-permute-start(bf16[8,2,32,384]{3,2,1,0:T(8,128)(2,1)} %get-tuple-element.24.refs_7_), channel_id=1, source_target_pairs={{0,2},{2,4},{4,6},{6,8},{8,10},{10,12},{12,14},{14,0},{1,3},{3,5},... | collective-permute-start | bytes 1179656 | tf_op jit(solution)/shard_map/ppermute | solution.py:321
  113.4 59.6 %collective-permute-start.13 = (bf16[8,2,32,384]{3,2,1,0:T(8,128)(2,1)}, bf16[8,2,32,384]{3,2,1,0:T(8,128)(2,1)S(1)}, u32[]{:S(2)}, u32[]{:S(2)}) collective-permute-start(bf16[8,2,32,384]{3,2,1,0:T(8,128)(2,1)} %get-tuple-element.25.refs_4_), channel_id=1, source_target_pairs={{0,14},{2,0},{4,2},{6,4},{8,6},{10,8},{12,10},{14,12},{1,15},{3,1}... | collective-permute-start | bytes 1179656 | tf_op jit(solution)/shard_map/ppermute | solution.py:321
  117.3 17.6 %all-to-all-start.1 = ((f32[16,8,256]{2,1,0:T(8,128)}), f32[16,8,256]{2,1,0:T(8,128)S(1)}, u32[]{:S(2)}, u32[]{:S(2)}) async-start(f32[16,8,256]{2,1,0:T(8,128)} %broadcast_in_dim.10), calls=%async_computation.3 | async-start | bytes 262144 | tf_op jit(solution)/shard_map/all_to_all | solution.py:341
  173.1 32.3 %copy-start.10 = (f32[6144]{0:T(1024)S(1)}, f32[6144]{0:T(1024)}, u32[]{:S(2)}) copy-start(f32[6144]{0:T(1024)} %param.10) | copy-start | bytes 73732
  173.1 32.3 %copy-start.12 = (f32[256,1]{1,0:T(8,128)S(1)}, f32[256,1]{1,0:T(8,128)}, u32[]{:S(2)}) copy-start(f32[256,1]{1,0:T(8,128)} %copy-done.11) | copy-start | bytes 3076
  192.6 12.7 %collective-permute-start.14 = (bf16[512,384]{1,0:T(8,128)(2,1)S(1)}, bf16[512,384]{1,0:T(8,128)(2,1)S(1)}, u32[]{:S(2)}, u32[]{:S(2)}) collective-permute-start(bf16[512,384]{1,0:T(8,128)(2,1)S(1)} %dynamic-slice_bitcast_fusion), channel_id=1, source_target_pairs={{0,1},{1,0},{2,3},{3,2},{4,5},{5,4},{6,7},{7,6},{8,9},{9,8},{10,11... | collective-permute-start | bytes 1179656 | tf_op jit(solution)/shard_map/ppermute | solution.py:325
  (17 other events, 189.3 us)
Sparse Core Ops, SparseCore 0:
  11.3 16.3 reduce-scatter.2
  116.1 75.3 reduce-scatter.4
Sparse Core Ops, SparseCore 1:
  12.7 79.2 all-gather.4
  112.7 53.9 all-gather.6

commit v4 on v3

--- a/solution.py
+++ b/solution.py
@@ -394,16 +394,17 @@
 
     (ra, rb), (la, lb) = moved[3], moved[4]
     grads, sums, terms = core_call(
-        hid, cotangent, w, query_gain, key_gain, moved[3] + moved[4] + (side,)
+        hid, cotangent, w, query_gain, key_gain, moved[2] + moved[5] + (ra, lb, side)
     )
+    far = shift(ra, 1), shift(lb, -1)
+    terms, grads, sums = order((terms, grads, sums), far + (rb, la))
     all_grads = lax.all_gather(grads, DP, axis=0)
     part = lax.psum_scatter(
         terms.reshape(NDP * 2 * ROWS, SL), "z", scatter_dimension=0, tiled=True
     ).reshape(NYH, 2 * ROWS, SL)
     sums = all_sum(sums)
-    ra, lb = order((ra, lb), (terms,))
     flat = [x for pair in moved[:3] for x in pair] + [ra, rb]
-    flat += [shift(ra, 1), shift(lb, -1), la, lb] + [x for pair in moved[5:] for x in pair]
+    flat += [*far, la, lb] + [x for pair in moved[5:] for x in pair]
     partial = weight_call(0, scalars, flat[:NZ], all_grads, ())
     grad_w, grad_o = weight_call(1, scalars, flat[NZ:], all_grads, partial)
     (part,) = order((part,), (grad_w, sums))

time: 217 us -> 215 us (level)
  waiting for transfers between devices: 96.3 us -> 92.7 us
    ppermute x14, waiting for transfers between devices: 29.8 us -> 24.8 us  [shift(): return lax.ppermute(a, 'z', [(i, (i + k) % NZ) for i in range(NZ)])]
    all_gather x1, waiting for transfers between devices: 31.1 us -> 34.9 us  [local(): all_grads = lax.all_gather(grads, DP, axis=0)]
    all_to_all x1, starting transfers between devices: 7.97 us -> 11.3 us  [all_sum(): return jnp.sum(lax.all_to_all(x, MP, 0, 0, tiled=True), 0)]
    ppermute x14, starting transfers between devices: 28.2 us -> 25.7 us  [shift(): return lax.ppermute(a, 'z', [(i, (i + k) % NZ) for i in range(NZ)])]
    unnamed x42 -> x54, local copies, waits for them, and re-layouts: 6.59 us -> 7.17 us
  transfers between devices with their start and end apart: 20 -> 20, of which waited for: 12 -> 10; matrix products, arithmetic and copies ran while one was open for 1% -> 1% of each run, Pallas kernels for 9% -> 17%
where the time goes in v4:
time: 215 us; the launch traced here: 214 us
  waiting for transfers between devices  92.7 us (43%)
  Pallas kernels  38.3 us (18%)
  starting transfers between devices  37.8 us (18%)
  blocking collectives  18.1 us (8%)
  between operations  15.7 us (7%)
  local copies, waits for them, and re-layouts  8.95 us (4%)
  other arithmetic  2.81 us (1%)
    all_gather x1, waiting for transfers between devices, local(): all_grads = lax.all_gather(grads, DP, axis=0)  34.9 us
    ppermute x14, starting transfers between devices, shift(): return lax.ppermute(a, 'z', [(i, (i + k) % NZ) for i in range(NZ)])  25.7 us
    ppermute x14, waiting for transfers between devices, shift(): return lax.ppermute(a, 'z', [(i, (i + k) % NZ) for i in range(NZ)])  24.8 us
    all_to_all x1, blocking collectives, local(): moved = ring_gather(lax.all_to_all(rows, DP, 0, 0, tiled=True), hid)  18.1 us
    pallas_call x1, Pallas kernels, core_call(): pl.pallas_call(core_kernel, in_specs=[ANY] * 3 + [full((1, HW)), full((1,...  15.6 us
    ppermute x1, waiting for transfers between devices, swap_yh(): return lax.ppermute(a, 'yh', [(0, 1), (1, 0)])  11.9 us
    pallas_call x2, Pallas kernels, weight_call(): pl.pallas_call(lambda *refs: weight_kernel(part, *refs), grid_spec=pltpu....  11.8 us
    all_to_all x1, starting transfers between devices, all_sum(): return jnp.sum(lax.all_to_all(x, MP, 0, 0, tiled=True), 0)  11.3 us
  transfers between devices with their start and end apart: 20, of which 10 were waited for; matrix products, arithmetic and copies ran while one was open for 1% of the time, Pallas kernels for 17%

profile of v4, /device:TPU:16, one launch (start us, length us, event | category | flops | bytes accessed | tf_op | source)
XLA Modules:
  0.0 214.5 jit_solution(17623616000344762206)
XLA Ops:
  8.0 2.1 pad_maximum_fusion
  11.6 2.1 shard_map.103
  13.8 18.1 %all_to_all.10 = bf16[16,2,32,384]{3,2,1,0:T(8,128)(2,1)S(1)} all-to-all(bf16[16,2,32,384]{3,2,1,0:T(8,128)(2,1)S(1)} %shard_map.103), channel_id=1, replica_groups=mesh['x'=4,'yl'=2,'c'=2,'z'=8,'yh'=2] {'x','yl','c'}, dimensions={0} | all-to-all | bytes 1572864 | tf_op jit(solution)/shard_map/all_to_all | solution.py:393
  32.0 2.0 collective-permute-start
  34.0 6.2 %collective-permute-start.1 = (bf16[8,2,32,384]{3,2,1,0:T(8,128)(2,1)S(1)}, bf16[8,2,32,384]{3,2,1,0:T(8,128)(2,1)S(1)}, u32[]{:S(2)}, u32[]{:S(2)}) collective-permute-start(bf16[8,2,32,384]{3,2,1,0:T(8,128)(2,1)S(1)} %get-tuple-element.39.refs_1_), channel_id=1, source_target_pairs={{0,14},{2,0},{4,2},{6,4},{8,6},{10,8},{12,10},{14,12},{1,15},{3,1}... | collective-permute-start | bytes 1179656 | tf_op jit(solution)/shard_map/ppermute | solution.py:321
  40.2 1.9 collective-permute-start.6
  42.2 6.3 %shard_map.102 = (bf16[272,6144]{1,0:T(8,128)(2,1)}, f32[256,1]{1,0:T(8,128)S(1)}, f32[256,1]{1,0:T(8,128)S(1)}) custom-call(bf16[256,6144]{1,0:T(8,128)(2,1)} %tok_ref.5, f32[1,6144]{1,0:T(1,128)S(1)} %bitcast.17), custom_call_target="tpu_custom_call" | custom-call | flops 1000 | bytes 1000 | tf_op jit(solution)/shard_map/pallas_call | solution.py:76
  50.7 6.9 %collective-permute-done.6.refs_8_ = bf16[8,2,32,384]{3,2,1,0:T(8,128)(2,1)} collective-permute-done((bf16[8,2,32,384]{3,2,1,0:T(8,128)(2,1)S(1)}, bf16[8,2,32,384]{3,2,1,0:T(8,128)(2,1)}, u32[]{:S(2)}, u32[]{:S(2)}) %collective-permute-start.6) | collective-permute-done | bytes 393248 | tf_op jit(solution)/shard_map/ppermute | solution.py:321
  57.6 3.8 %collective-permute-start.7 = (bf16[8,2,32,384]{3,2,1,0:T(8,128)(2,1)}, bf16[8,2,32,384]{3,2,1,0:T(8,128)(2,1)S(1)}, u32[]{:S(2)}, u32[]{:S(2)}) collective-permute-start(bf16[8,2,32,384]{3,2,1,0:T(8,128)(2,1)} %collective-permute-done.6.refs_8_), channel_id=1, source_target_pairs={{0,14},{2,0},{4,2},{6,4},{8,6},{10,8},{12,10},{14,12},{1,15},{3,1}... | collective-permute-start | bytes 1179656 | tf_op jit(solution)/shard_map/ppermute | solution.py:321
  64.2 7.2 %collective-permute-done.2.rest_0_.refs_5_ = bf16[8,2,32,384]{3,2,1,0:T(8,128)(2,1)S(1)} collective-permute-done((bf16[8,2,32,384]{3,2,1,0:T(8,128)(2,1)}, bf16[8,2,32,384]{3,2,1,0:T(8,128)(2,1)S(1)}, u32[]{:S(2)}, u32[]{:S(2)}) %collective-permute-start.2) | collective-permute-done | bytes 393248 | tf_op jit(solution)/shard_map/ppermute | solution.py:321
  71.5 3.3 %collective-permute-start.9 = (bf16[8,2,32,384]{3,2,1,0:T(8,128)(2,1)S(1)}, bf16[8,2,32,384]{3,2,1,0:T(8,128)(2,1)}, u32[]{:S(2)}, u32[]{:S(2)}) collective-permute-start(bf16[8,2,32,384]{3,2,1,0:T(8,128)(2,1)S(1)} %collective-permute-done.7.rest_3_.refs_6_), channel_id=1, source_target_pairs={{0,14},{2,0},{4,2},{6,4},{8,6},{10,8},{12,10},{14,12},{1,15},{3,1}... | collective-permute-start | bytes 1179656 | tf_op jit(solution)/shard_map/ppermute | solution.py:321
  74.8 4.8 %collective-permute-done.5.rest_2_.refs_5_ = bf16[8,2,32,384]{3,2,1,0:T(8,128)(2,1)S(1)} collective-permute-done((bf16[8,2,32,384]{3,2,1,0:T(8,128)(2,1)}, bf16[8,2,32,384]{3,2,1,0:T(8,128)(2,1)S(1)}, u32[]{:S(2)}, u32[]{:S(2)}) %collective-permute-start.5) | collective-permute-done | bytes 393248 | tf_op jit(solution)/shard_map/ppermute | solution.py:321
  79.6 3.6 %collective-permute-start.13 = (bf16[8,2,32,384]{3,2,1,0:T(8,128)(2,1)S(1)}, bf16[8,2,32,384]{3,2,1,0:T(8,128)(2,1)S(1)}, u32[]{:S(2)}, u32[]{:S(2)}) collective-permute-start(bf16[8,2,32,384]{3,2,1,0:T(8,128)(2,1)S(1)} %collective-permute-done.5.rest_2_.refs_5_), channel_id=1, source_target_pairs={{0,14},{2,0},{4,2},{6,4},{8,6},{10,8},{12,10},{14,12},{1,15},{3,1}... | collective-permute-start | bytes 1179656 | tf_op jit(solution)/shard_map/ppermute | solution.py:321
  83.2 5.2 %collective-permute-done.8.rest_4_.refs_7_ = bf16[8,2,32,384]{3,2,1,0:T(8,128)(2,1)} collective-permute-done((bf16[8,2,32,384]{3,2,1,0:T(8,128)(2,1)S(1)}, bf16[8,2,32,384]{3,2,1,0:T(8,128)(2,1)}, u32[]{:S(2)}, u32[]{:S(2)}) %collective-permute-start.8) | collective-permute-done | bytes 393248 | tf_op jit(solution)/shard_map/ppermute | solution.py:321
  88.4 3.3 %collective-permute-start.11 = (bf16[8,2,32,384]{3,2,1,0:T(8,128)(2,1)}, bf16[8,2,32,384]{3,2,1,0:T(8,128)(2,1)S(1)}, u32[]{:S(2)}, u32[]{:S(2)}) collective-permute-start(bf16[8,2,32,384]{3,2,1,0:T(8,128)(2,1)} %collective-permute-done.9.rest_5_.refs_4_), channel_id=1, source_target_pairs={{0,14},{2,0},{4,2},{6,4},{8,6},{10,8},{12,10},{14,12},{1,15},{3,1}... | collective-permute-start | bytes 1179656 | tf_op jit(solution)/shard_map/ppermute | solution.py:321
  92.0 15.6 %shard_map.105 = (bf16[256,1024]{1,0:T(8,128)(2,1)}, f32[8,256]{1,0:T(8,128)S(1)}, bf16[16,512,384]{2,1,0:T(8,128)(2,1)}) custom-call(bf16[272,6144]{1,0:T(8,128)(2,1)} %get-tuple-element.21.refs_2_.hid_in, bf16[256,6144]{1,0:T(8,128)(2,1)} %cot_in.1, bf16[16,4,384,256]{3,2,1,0:T(8,128)(2,1)} %bitcast.26, f32[1,256]{1,0:T(1,128)S(1)} %bitcast.19, ...), custom_call_target="tpu_custom_call" | custom-call | flops 1000 | bytes 1000 | tf_op jit(solution)/shard_map/pallas_call | solution.py:226
  110.6 11.3 %all-to-all-start.1 = ((f32[16,8,256]{2,1,0:T(8,128)}), f32[16,8,256]{2,1,0:T(8,128)S(1)}, u32[]{:S(2)}, u32[]{:S(2)}) async-start(f32[16,8,256]{2,1,0:T(8,128)} %broadcast_in_dim.10), calls=%async_computation.3 | async-start | bytes 262144 | tf_op jit(solution)/shard_map/all_to_all | solution.py:341
  121.9 9.0 %all-to-all-done.1 = f32[16,8,256]{2,1,0:T(8,128)S(1)} async-done(((f32[16,8,256]{2,1,0:T(8,128)}), f32[16,8,256]{2,1,0:T(8,128)S(1)}, u32[]{:S(2)}, u32[]{:S(2)}) %all-to-all-start.1) | async-done | bytes 131104 | tf_op jit(solution)/shard_map/all_to_all | solution.py:341
  131.5 34.9 %all-gather.7.cloned.1.call-done = bf16[4096,1024]{1,0:T(8,128)(2,1)} async-done(((bf16[256,1024]{1,0:T(8,128)(2,1)}), bf16[4096,1024]{1,0:T(8,128)(2,1)}) %all-gather.7.cloned.1.call-update) | async-done | bytes 8388624 | tf_op jit(solution)/shard_map/all_gather | solution.py:401
  166.5 5.7 %shard_map.107 = (f32[384,768]{1,0:T(8,128)}, f32[384,256]{1,0:T(8,128)S(1)}) custom-call(s32[3]{0:T(128)S(1)} %pad_add_fusion.z_ref.refs_0_.s_ref, bf16[8,2,32,384]{3,2,1,0:T(8,128)(2,1)S(1)} %get-tuple-element.39.refs_1_, bf16[8,2,32,384]{3,2,1,0:T(8,128)(2,1)S(1)} %get-tuple-element.38.refs_2_, bf16[8,2,32,384]{3,2,1,0:T(8,128)(2,1)S(1)} %copy-done.11, ...), custom_call_target="tpu_custom_call" | custom-call | flops 1000 | bytes 1000 | tf_op jit(solution)/shard_map/pallas_call | solution.py:303
  172.9 6.1 %shard_map.108 = (bf16[3,384,256]{2,1,0:T(8,128)(2,1)}, bf16[384,256]{1,0:T(8,128)(2,1)}) custom-call(s32[3]{0:T(128)S(1)} %pad_add_fusion.z_ref.refs_0_.s_ref, bf16[8,2,32,384]{3,2,1,0:T(8,128)(2,1)S(1)} %copy-done.4, bf16[8,2,32,384]{3,2,1,0:T(8,128)(2,1)S(1)} %copy-done.6, bf16[8,2,32,384]{3,2,1,0:T(8,128)(2,1)S(1)} %copy-done.2, ...), custom_call_target="tpu_custom_call" | custom-call | flops 1000 | bytes 1000 | tf_op jit(solution)/shard_map/pallas_call | solution.py:303
  179.0 10.7 %reduce-scatter.5.cloned.1.call-done = bf16[1024,384]{1,0:T(8,128)(2,1)} async-done(((bf16[8192,384]{1,0:T(8,128)(2,1)}), bf16[1024,384]{1,0:T(8,128)(2,1)}) %reduce-scatter.5.cloned.1.call-update) | async-done | bytes 786448 | tf_op jit(solution)/shard_map/reduce_scatter | solution.py:402
  191.4 11.9 %collective-permute-done.14.recv_ref = bf16[512,384]{1,0:T(8,128)(2,1)S(1)} collective-permute-done((bf16[512,384]{1,0:T(8,128)(2,1)S(1)}, bf16[512,384]{1,0:T(8,128)(2,1)S(1)}, u32[]{:S(2)}, u32[]{:S(2)}) %collective-permute-start.14) | collective-permute-done | bytes 393248 | tf_op jit(solution)/shard_map/ppermute | solution.py:325
  204.5 2.6 %shard_map.110 = (bf16[256,384]{1,0:T(8,128)(2,1)}, bf16[256,384]{1,0:T(8,128)(2,1)}) custom-call(s32[3]{0:T(128)S(1)} %pad_add_fusion.z_ref.refs_0_.s_ref, bf16[2,512,384]{2,1,0:T(8,128)(2,1)S(1)} %copy-done, bf16[512,384]{1,0:T(8,128)(2,1)S(1)} %collective-permute-done.14.recv_ref, f32[8,256]{1,0:T(8,128)S(1)} %copy-done.21, bf16[256,6144]{1,0:T(8,128)(2,1)} %tok_ref.5, ...), custom_call_target="tpu_custom_call" | custom-call | flops 1000 | bytes 1000 | tf_op jit(solution)/shard_map/pallas_call | solution.py:359
  (90 shorter events, 14.0 us)
Async XLA Ops:
  8.0 83.7 %reduce-scatter.3.cloned.1.call-start = ((), (), s32[]{:S(2)}) async-start(), calls=%async_computation.4 | async-start | bytes 1179648 | tf_op jit(solution)/shard_map/reduce_scatter | solution.py:389
  10.2 81.8 %all-gather.5.cloned.1.call-start = ((), (), s32[]{:S(2)}) async-start(), calls=%async_computation.6 | async-start | bytes 13369344 | tf_op jit(solution)/shard_map/all_gather | solution.py:388
  10.8 155.7 %all-gather.7.cloned.1.call-start = ((), (), s32[]{:S(2)}) async-start(), calls=%async_computation.7 | async-start | bytes 8912896 | tf_op jit(solution)/shard_map/all_gather | solution.py:401
  13.7 78.2 %copy-start.24 = (f32[256]{0:T(256)S(1)}, f32[256]{0:T(256)}, u32[]{:S(2)}) copy-start(f32[256]{0:T(256)} %param.11) | copy-start | bytes 3076
  13.7 78.2 %copy-start.25 = (f32[256]{0:T(256)S(1)}, f32[256]{0:T(256)}, u32[]{:S(2)}) copy-start(f32[256]{0:T(256)} %param.12) | copy-start | bytes 3076
  32.0 17.8 %collective-permute-start = (bf16[8,2,32,384]{3,2,1,0:T(8,128)(2,1)S(1)}, bf16[8,2,32,384]{3,2,1,0:T(8,128)(2,1)S(1)}, u32[]{:S(2)}, u32[]{:S(2)}) collective-permute-start(bf16[8,2,32,384]{3,2,1,0:T(8,128)(2,1)S(1)} %get-tuple-element.39.refs_1_), channel_id=1, source_target_pairs={{0,2},{2,4},{4,6},{6,8},{8,10},{10,12},{12,14},{14,0},{1,3},{3,5},... | collective-permute-start | bytes 1179656 | tf_op jit(solution)/shard_map/ppermute | solution.py:321
  34.0 15.8 %collective-permute-start.1 = (bf16[8,2,32,384]{3,2,1,0:T(8,128)(2,1)S(1)}, bf16[8,2,32,384]{3,2,1,0:T(8,128)(2,1)S(1)}, u32[]{:S(2)}, u32[]{:S(2)}) collective-permute-start(bf16[8,2,32,384]{3,2,1,0:T(8,128)(2,1)S(1)} %get-tuple-element.39.refs_1_), channel_id=1, source_target_pairs={{0,14},{2,0},{4,2},{6,4},{8,6},{10,8},{12,10},{14,12},{1,15},{3,1}... | collective-permute-start | bytes 1179656 | tf_op jit(solution)/shard_map/ppermute | solution.py:321
  40.2 17.4 %collective-permute-start.6 = (bf16[8,2,32,384]{3,2,1,0:T(8,128)(2,1)S(1)}, bf16[8,2,32,384]{3,2,1,0:T(8,128)(2,1)}, u32[]{:S(2)}, u32[]{:S(2)}) collective-permute-start(bf16[8,2,32,384]{3,2,1,0:T(8,128)(2,1)S(1)} %get-tuple-element.38.refs_2_), channel_id=1, source_target_pairs={{0,14},{2,0},{4,2},{6,4},{8,6},{10,8},{12,10},{14,12},{1,15},{3,1}... | collective-permute-start | bytes 1179656 | tf_op jit(solution)/shard_map/ppermute | solution.py:321
  49.8 13.2 %collective-permute-start.3 = (bf16[8,2,32,384]{3,2,1,0:T(8,128)(2,1)S(1)}, bf16[8,2,32,384]{3,2,1,0:T(8,128)(2,1)S(1)}, u32[]{:S(2)}, u32[]{:S(2)}) collective-permute-start(bf16[8,2,32,384]{3,2,1,0:T(8,128)(2,1)S(1)} %get-tuple-element.38.refs_2_), channel_id=1, source_target_pairs={{0,2},{2,4},{4,6},{6,8},{8,10},{10,12},{12,14},{14,0},{1,3},{3,5},... | collective-permute-start | bytes 1179656 | tf_op jit(solution)/shard_map/ppermute | solution.py:321
  50.7 20.7 %collective-permute-start.2 = (bf16[8,2,32,384]{3,2,1,0:T(8,128)(2,1)}, bf16[8,2,32,384]{3,2,1,0:T(8,128)(2,1)S(1)}, u32[]{:S(2)}, u32[]{:S(2)}) collective-permute-start(bf16[8,2,32,384]{3,2,1,0:T(8,128)(2,1)} %get-tuple-element.22.refs_3_), channel_id=1, source_target_pairs={{0,2},{2,4},{4,6},{6,8},{8,10},{10,12},{12,14},{14,0},{1,3},{3,5},... | collective-permute-start | bytes 1179656 | tf_op jit(solution)/shard_map/ppermute | solution.py:321
  57.6 13.8 %collective-permute-start.7 = (bf16[8,2,32,384]{3,2,1,0:T(8,128)(2,1)}, bf16[8,2,32,384]{3,2,1,0:T(8,128)(2,1)S(1)}, u32[]{:S(2)}, u32[]{:S(2)}) collective-permute-start(bf16[8,2,32,384]{3,2,1,0:T(8,128)(2,1)} %collective-permute-done.6.refs_8_), channel_id=1, source_target_pairs={{0,14},{2,0},{4,2},{6,4},{8,6},{10,8},{12,10},{14,12},{1,15},{3,1}... | collective-permute-start | bytes 1179656 | tf_op jit(solution)/shard_map/ppermute | solution.py:321
  61.4 18.2 %collective-permute-start.5 = (bf16[8,2,32,384]{3,2,1,0:T(8,128)(2,1)}, bf16[8,2,32,384]{3,2,1,0:T(8,128)(2,1)S(1)}, u32[]{:S(2)}, u32[]{:S(2)}) collective-permute-start(bf16[8,2,32,384]{3,2,1,0:T(8,128)(2,1)} %get-tuple-element.23.refs_7_), channel_id=1, source_target_pairs={{0,14},{2,0},{4,2},{6,4},{8,6},{10,8},{12,10},{14,12},{1,15},{3,1}... | collective-permute-start | bytes 1179656 | tf_op jit(solution)/shard_map/ppermute | solution.py:321
  63.0 20.2 %collective-permute-start.4 = (bf16[8,2,32,384]{3,2,1,0:T(8,128)(2,1)S(1)}, bf16[8,2,32,384]{3,2,1,0:T(8,128)(2,1)S(1)}, u32[]{:S(2)}, u32[]{:S(2)}) collective-permute-start(bf16[8,2,32,384]{3,2,1,0:T(8,128)(2,1)S(1)} %collective-permute-done.3.refs_4_), channel_id=1, source_target_pairs={{0,2},{2,4},{4,6},{6,8},{8,10},{10,12},{12,14},{14,0},{1,3},{3,5},... | collective-permute-start | bytes 1179656 | tf_op jit(solution)/shard_map/ppermute | solution.py:321
  71.4 17.0 %collective-permute-start.8 = (bf16[8,2,32,384]{3,2,1,0:T(8,128)(2,1)S(1)}, bf16[8,2,32,384]{3,2,1,0:T(8,128)(2,1)}, u32[]{:S(2)}, u32[]{:S(2)}) collective-permute-start(bf16[8,2,32,384]{3,2,1,0:T(8,128)(2,1)S(1)} %collective-permute-done.2.rest_0_.refs_5_), channel_id=1, source_target_pairs={{0,2},{2,4},{4,6},{6,8},{8,10},{10,12},{12,14},{14,0},{1,3},{3,5},... | collective-permute-start | bytes 1179656 | tf_op jit(solution)/shard_map/ppermute | solution.py:321
  71.5 16.9 %collective-permute-start.9 = (bf16[8,2,32,384]{3,2,1,0:T(8,128)(2,1)S(1)}, bf16[8,2,32,384]{3,2,1,0:T(8,128)(2,1)}, u32[]{:S(2)}, u32[]{:S(2)}) collective-permute-start(bf16[8,2,32,384]{3,2,1,0:T(8,128)(2,1)S(1)} %collective-permute-done.7.rest_3_.refs_6_), channel_id=1, source_target_pairs={{0,14},{2,0},{4,2},{6,4},{8,6},{10,8},{12,10},{14,12},{1,15},{3,1}... | collective-permute-start | bytes 1179656 | tf_op jit(solution)/shard_map/ppermute | solution.py:321
  79.6 28.5 %collective-permute-start.13 = (bf16[8,2,32,384]{3,2,1,0:T(8,128)(2,1)S(1)}, bf16[8,2,32,384]{3,2,1,0:T(8,128)(2,1)S(1)}, u32[]{:S(2)}, u32[]{:S(2)}) collective-permute-start(bf16[8,2,32,384]{3,2,1,0:T(8,128)(2,1)S(1)} %collective-permute-done.5.rest_2_.refs_5_), channel_id=1, source_target_pairs={{0,14},{2,0},{4,2},{6,4},{8,6},{10,8},{12,10},{14,12},{1,15},{3,1}... | collective-permute-start | bytes 1179656 | tf_op jit(solution)/shard_map/ppermute | solution.py:321
  83.2 25.0 %collective-permute-start.12 = (bf16[8,2,32,384]{3,2,1,0:T(8,128)(2,1)S(1)}, bf16[8,2,32,384]{3,2,1,0:T(8,128)(2,1)}, u32[]{:S(2)}, u32[]{:S(2)}) collective-permute-start(bf16[8,2,32,384]{3,2,1,0:T(8,128)(2,1)S(1)} %collective-permute-done.4.rest_1_.refs_6_), channel_id=1, source_target_pairs={{0,2},{2,4},{4,6},{6,8},{8,10},{10,12},{12,14},{14,0},{1,3},{3,5},... | collective-permute-start | bytes 1179656 | tf_op jit(solution)/shard_map/ppermute | solution.py:321
  88.4 19.8 %collective-permute-start.10 = (bf16[8,2,32,384]{3,2,1,0:T(8,128)(2,1)}, bf16[8,2,32,384]{3,2,1,0:T(8,128)(2,1)S(1)}, u32[]{:S(2)}, u32[]{:S(2)}) collective-permute-start(bf16[8,2,32,384]{3,2,1,0:T(8,128)(2,1)} %collective-permute-done.8.rest_4_.refs_7_), channel_id=1, source_target_pairs={{0,2},{2,4},{4,6},{6,8},{8,10},{10,12},{12,14},{14,0},{1,3},{3,5},... | collective-permute-start | bytes 1179656 | tf_op jit(solution)/shard_map/ppermute | solution.py:321
  88.4 19.8 %collective-permute-start.11 = (bf16[8,2,32,384]{3,2,1,0:T(8,128)(2,1)}, bf16[8,2,32,384]{3,2,1,0:T(8,128)(2,1)S(1)}, u32[]{:S(2)}, u32[]{:S(2)}) collective-permute-start(bf16[8,2,32,384]{3,2,1,0:T(8,128)(2,1)} %collective-permute-done.9.rest_5_.refs_4_), channel_id=1, source_target_pairs={{0,14},{2,0},{4,2},{6,4},{8,6},{10,8},{12,10},{14,12},{1,15},{3,1}... | collective-permute-start | bytes 1179656 | tf_op jit(solution)/shard_map/ppermute | solution.py:321
  109.2 57.2 %copy-start.11 = (bf16[8,2,32,384]{3,2,1,0:T(8,128)(2,1)S(1)}, bf16[8,2,32,384]{3,2,1,0:T(8,128)(2,1)}, u32[]{:S(2)}) copy-start(bf16[8,2,32,384]{3,2,1,0:T(8,128)(2,1)} %get-tuple-element.22.refs_3_) | copy-start | bytes 1179652
  109.2 57.2 %copy-start.13 = (bf16[8,2,32,384]{3,2,1,0:T(8,128)(2,1)S(1)}, bf16[8,2,32,384]{3,2,1,0:T(8,128)(2,1)}, u32[]{:S(2)}) copy-start(bf16[8,2,32,384]{3,2,1,0:T(8,128)(2,1)} %copy-done.12) | copy-start | bytes 1179652
  109.2 80.5 %reduce-scatter.5.cloned.1.call-start = ((), (), s32[]{:S(2)}) async-start(), calls=%async_computation.5 | async-start | bytes 7077888 | tf_op jit(solution)/shard_map/reduce_scatter | solution.py:402
  110.6 20.2 %all-to-all-start.1 = ((f32[16,8,256]{2,1,0:T(8,128)}), f32[16,8,256]{2,1,0:T(8,128)S(1)}, u32[]{:S(2)}, u32[]{:S(2)}) async-start(f32[16,8,256]{2,1,0:T(8,128)} %broadcast_in_dim.10), calls=%async_computation.3 | async-start | bytes 262144 | tf_op jit(solution)/shard_map/all_to_all | solution.py:341
  190.7 12.6 %collective-permute-start.14 = (bf16[512,384]{1,0:T(8,128)(2,1)S(1)}, bf16[512,384]{1,0:T(8,128)(2,1)S(1)}, u32[]{:S(2)}, u32[]{:S(2)}) collective-permute-start(bf16[512,384]{1,0:T(8,128)(2,1)S(1)} %dynamic-slice_bitcast_fusion), channel_id=1, source_target_pairs={{0,1},{1,0},{2,3},{3,2},{4,5},{5,4},{6,7},{7,6},{8,9},{9,8},{10,11... | collective-permute-start | bytes 1179656 | tf_op jit(solution)/shard_map/ppermute | solution.py:325
  (23 other events, 247.9 us)
Sparse Core Ops, SparseCore 0:
  11.3 16.3 reduce-scatter.2
  112.8 76.8 reduce-scatter.4
Sparse Core Ops, SparseCore 1:
  12.7 79.3 all-gather.4
  109.3 57.1 all-gather.6

commit v5 on v4

--- a/solution.py
+++ b/solution.py
@@ -45,6 +45,27 @@
         input_output_aliases={i: i for i in range(n)},
         cost_estimate=COST,
     )(*xs, *after)
+
+
+def pack_kernel(a_ref, b_ref, out_ref, sems):
+    copies = [pltpu.make_async_copy(a_ref.at[j], out_ref.at[j], sems.at[j]) for j in range(3)]
+    copies.append(pltpu.make_async_copy(b_ref, out_ref.at[3], sems.at[3]))
+    for copy in copies:
+        copy.start()
+    for copy in copies:
+        copy.wait()
+
+
+def pack_call(w_qkv, w_out):
+    return pl.pallas_call(
+        pack_kernel,
+        in_specs=[ANY, ANY],
+        out_specs=ANY,
+        out_shape=jax.ShapeDtypeStruct((4, SL, HW), BF),
+        scratch_shapes=[pltpu.SemaphoreType.DMA((4,))],
+        compiler_params=params(),
+        cost_estimate=COST,
+    )(w_qkv.transpose(1, 0, 2), w_out)
 
 
 def normalise(t):
@@ -374,7 +395,7 @@
             out_specs=[pl.BlockSpec((ROWS, SL), fixed)] * 2,
         ),
         out_shape=[out, out],
-        compiler_params=params(),
+        compiler_params=pltpu.CompilerParams(vmem_limit_bytes=VMEM // 4),
         cost_estimate=COST,
     )(scalars, part, recv, sums, tokens, mean, rstd, gain.reshape(1, D), *after)
 
@@ -384,7 +405,7 @@
     yh = lax.axis_index("yh")
     scalars = jnp.stack([z, yh, z * NYH + yh]).astype(jnp.int32)
 
-    w_own = jnp.concatenate([w_qkv.transpose(1, 0, 2), w_out[None]], 0)
+    w_own = pack_call(w_qkv, w_out)
     w = lax.all_gather(w_own, DP, axis=0)
     side = lax.psum_scatter(w_own, "c", scatter_dimension=0, tiled=True)
 

time: 215 us -> 215 us (level)
  local copies, waits for them, and re-layouts: 8.95 us -> 11.1 us
    unnamed x54 -> x64, local copies, waits for them, and re-layouts: 7.17 us -> 9.28 us
where the time goes in v5:
time: 215 us; the launch traced here: 214 us
  waiting for transfers between devices  92.3 us (43%)
  Pallas kernels  38.6 us (18%)
  starting transfers between devices  37.8 us (18%)
  blocking collectives  18.1 us (8%)
  between operations  15.8 us (7%)
  local copies, waits for them, and re-layouts  11.1 us (5%)
    all_gather x1, waiting for transfers between devices, local(): all_grads = lax.all_gather(grads, DP, axis=0)  34.9 us
    ppermute x14, starting transfers between devices, shift(): return lax.ppermute(a, 'z', [(i, (i + k) % NZ) for i in range(NZ)])  25.6 us
    ppermute x14, waiting for transfers between devices, shift(): return lax.ppermute(a, 'z', [(i, (i + k) % NZ) for i in range(NZ)])  24.8 us
    all_to_all x1, blocking collectives, local(): moved = ring_gather(lax.all_to_all(rows, DP, 0, 0, tiled=True), hid)  18.1 us
    pallas_call x1, Pallas kernels, core_call(): pl.pallas_call(core_kernel, in_specs=[ANY] * 3 + [full((1, HW)), full((1,...  15.6 us
    pallas_call x2, Pallas kernels, weight_call(): pl.pallas_call(lambda *refs: weight_kernel(part, *refs), grid_spec=pltpu....  12.1 us
    ppermute x1, waiting for transfers between devices, swap_yh(): return lax.ppermute(a, 'yh', [(0, 1), (1, 0)])  11.9 us
    all_to_all x1, starting transfers between devices, all_sum(): return jnp.sum(lax.all_to_all(x, MP, 0, 0, tiled=True), 0)  11.3 us
  transfers between devices with their start and end apart: 20, of which 10 were waited for; matrix products, arithmetic and copies ran while one was open for 1% of the time, Pallas kernels for 17%

profile of v5, /device:TPU:16, one launch (start us, length us, event | category | flops | bytes accessed | tf_op | source)
XLA Modules:
  0.0 214.4 jit_solution(1321472502407143790)
XLA Ops:
  12.4 2.1 shard_map.104
  14.6 18.1 %all_to_all.10 = bf16[16,2,32,384]{3,2,1,0:T(8,128)(2,1)S(1)} all-to-all(bf16[16,2,32,384]{3,2,1,0:T(8,128)(2,1)S(1)} %shard_map.104), channel_id=1, replica_groups=mesh['x'=4,'yl'=2,'c'=2,'z'=8,'yh'=2] {'x','yl','c'}, dimensions={0} | all-to-all | bytes 1572864 | tf_op jit(solution)/shard_map/all_to_all | solution.py:414
  32.8 2.0 collective-permute-start
  34.8 6.2 %collective-permute-start.1 = (bf16[8,2,32,384]{3,2,1,0:T(8,128)(2,1)S(1)}, bf16[8,2,32,384]{3,2,1,0:T(8,128)(2,1)S(1)}, u32[]{:S(2)}, u32[]{:S(2)}) collective-permute-start(bf16[8,2,32,384]{3,2,1,0:T(8,128)(2,1)S(1)} %get-tuple-element.39.refs_1_), channel_id=1, source_target_pairs={{0,14},{2,0},{4,2},{6,4},{8,6},{10,8},{12,10},{14,12},{1,15},{3,1}... | collective-permute-start | bytes 1179656 | tf_op jit(solution)/shard_map/ppermute | solution.py:342
  41.0 1.9 collective-permute-start.6
  43.0 6.3 %shard_map.102 = (bf16[272,6144]{1,0:T(8,128)(2,1)}, f32[256,1]{1,0:T(8,128)S(1)}, f32[256,1]{1,0:T(8,128)S(1)}) custom-call(bf16[256,6144]{1,0:T(8,128)(2,1)} %tok_ref.5, f32[1,6144]{1,0:T(1,128)S(1)} %bitcast.17), custom_call_target="tpu_custom_call" | custom-call | flops 1000 | bytes 1000 | tf_op jit(solution)/shard_map/pallas_call | solution.py:97
  51.6 6.8 %collective-permute-done.6.refs_8_ = bf16[8,2,32,384]{3,2,1,0:T(8,128)(2,1)} collective-permute-done((bf16[8,2,32,384]{3,2,1,0:T(8,128)(2,1)S(1)}, bf16[8,2,32,384]{3,2,1,0:T(8,128)(2,1)}, u32[]{:S(2)}, u32[]{:S(2)}) %collective-permute-start.6) | collective-permute-done | bytes 393248 | tf_op jit(solution)/shard_map/ppermute | solution.py:342
  58.4 3.8 %collective-permute-start.7 = (bf16[8,2,32,384]{3,2,1,0:T(8,128)(2,1)}, bf16[8,2,32,384]{3,2,1,0:T(8,128)(2,1)S(1)}, u32[]{:S(2)}, u32[]{:S(2)}) collective-permute-start(bf16[8,2,32,384]{3,2,1,0:T(8,128)(2,1)} %collective-permute-done.6.refs_8_), channel_id=1, source_target_pairs={{0,14},{2,0},{4,2},{6,4},{8,6},{10,8},{12,10},{14,12},{1,15},{3,1}... | collective-permute-start | bytes 1179656 | tf_op jit(solution)/shard_map/ppermute | solution.py:342
  65.0 7.2 %collective-permute-done.2.rest_0_.refs_5_ = bf16[8,2,32,384]{3,2,1,0:T(8,128)(2,1)S(1)} collective-permute-done((bf16[8,2,32,384]{3,2,1,0:T(8,128)(2,1)}, bf16[8,2,32,384]{3,2,1,0:T(8,128)(2,1)S(1)}, u32[]{:S(2)}, u32[]{:S(2)}) %collective-permute-start.2) | collective-permute-done | bytes 393248 | tf_op jit(solution)/shard_map/ppermute | solution.py:342
  72.3 3.3 %collective-permute-start.9 = (bf16[8,2,32,384]{3,2,1,0:T(8,128)(2,1)S(1)}, bf16[8,2,32,384]{3,2,1,0:T(8,128)(2,1)}, u32[]{:S(2)}, u32[]{:S(2)}) collective-permute-start(bf16[8,2,32,384]{3,2,1,0:T(8,128)(2,1)S(1)} %collective-permute-done.7.rest_3_.refs_6_), channel_id=1, source_target_pairs={{0,14},{2,0},{4,2},{6,4},{8,6},{10,8},{12,10},{14,12},{1,15},{3,1}... | collective-permute-start | bytes 1179656 | tf_op jit(solution)/shard_map/ppermute | solution.py:342
  75.6 4.8 %collective-permute-done.5.rest_2_.refs_5_ = bf16[8,2,32,384]{3,2,1,0:T(8,128)(2,1)S(1)} collective-permute-done((bf16[8,2,32,384]{3,2,1,0:T(8,128)(2,1)}, bf16[8,2,32,384]{3,2,1,0:T(8,128)(2,1)S(1)}, u32[]{:S(2)}, u32[]{:S(2)}) %collective-permute-start.5) | collective-permute-done | bytes 393248 | tf_op jit(solution)/shard_map/ppermute | solution.py:342
  80.4 3.6 %collective-permute-start.13 = (bf16[8,2,32,384]{3,2,1,0:T(8,128)(2,1)S(1)}, bf16[8,2,32,384]{3,2,1,0:T(8,128)(2,1)S(1)}, u32[]{:S(2)}, u32[]{:S(2)}) collective-permute-start(bf16[8,2,32,384]{3,2,1,0:T(8,128)(2,1)S(1)} %collective-permute-done.5.rest_2_.refs_5_), channel_id=1, source_target_pairs={{0,14},{2,0},{4,2},{6,4},{8,6},{10,8},{12,10},{14,12},{1,15},{3,1}... | collective-permute-start | bytes 1179656 | tf_op jit(solution)/shard_map/ppermute | solution.py:342
  84.0 5.2 %collective-permute-done.8.rest_4_.refs_7_ = bf16[8,2,32,384]{3,2,1,0:T(8,128)(2,1)} collective-permute-done((bf16[8,2,32,384]{3,2,1,0:T(8,128)(2,1)S(1)}, bf16[8,2,32,384]{3,2,1,0:T(8,128)(2,1)}, u32[]{:S(2)}, u32[]{:S(2)}) %collective-permute-start.8) | collective-permute-done | bytes 393248 | tf_op jit(solution)/shard_map/ppermute | solution.py:342
  89.2 3.3 %collective-permute-start.11 = (bf16[8,2,32,384]{3,2,1,0:T(8,128)(2,1)}, bf16[8,2,32,384]{3,2,1,0:T(8,128)(2,1)S(1)}, u32[]{:S(2)}, u32[]{:S(2)}) collective-permute-start(bf16[8,2,32,384]{3,2,1,0:T(8,128)(2,1)} %collective-permute-done.9.rest_5_.refs_4_), channel_id=1, source_target_pairs={{0,14},{2,0},{4,2},{6,4},{8,6},{10,8},{12,10},{14,12},{1,15},{3,1}... | collective-permute-start | bytes 1179656 | tf_op jit(solution)/shard_map/ppermute | solution.py:342
  92.8 15.6 %shard_map.106 = (bf16[256,1024]{1,0:T(8,128)(2,1)}, f32[8,256]{1,0:T(8,128)S(1)}, bf16[16,512,384]{2,1,0:T(8,128)(2,1)}) custom-call(bf16[272,6144]{1,0:T(8,128)(2,1)} %get-tuple-element.21.refs_2_.hid_in, bf16[256,6144]{1,0:T(8,128)(2,1)} %cot_in.1, bf16[16,4,384,256]{3,2,1,0:T(8,128)(2,1)} %bitcast.26, f32[1,256]{1,0:T(1,128)S(1)} %bitcast.19, ...), custom_call_target="tpu_custom_call" | custom-call | flops 1000 | bytes 1000 | tf_op jit(solution)/shard_map/pallas_call | solution.py:247
  111.5 11.3 %all-to-all-start.1 = ((f32[16,8,256]{2,1,0:T(8,128)}), f32[16,8,256]{2,1,0:T(8,128)S(1)}, u32[]{:S(2)}, u32[]{:S(2)}) async-start(f32[16,8,256]{2,1,0:T(8,128)} %broadcast_in_dim.2), calls=%async_computation.3 | async-start | bytes 262144 | tf_op jit(solution)/shard_map/all_to_all | solution.py:362
  122.8 9.0 %all-to-all-done.1 = f32[16,8,256]{2,1,0:T(8,128)S(1)} async-done(((f32[16,8,256]{2,1,0:T(8,128)}), f32[16,8,256]{2,1,0:T(8,128)S(1)}, u32[]{:S(2)}, u32[]{:S(2)}) %all-to-all-start.1) | async-done | bytes 131104 | tf_op jit(solution)/shard_map/all_to_all | solution.py:362
  132.3 34.9 %all-gather.7.cloned.1.call-done = bf16[4096,1024]{1,0:T(8,128)(2,1)} async-done(((bf16[256,1024]{1,0:T(8,128)(2,1)}), bf16[4096,1024]{1,0:T(8,128)(2,1)}) %all-gather.7.cloned.1.call-update) | async-done | bytes 8388624 | tf_op jit(solution)/shard_map/all_gather | solution.py:422
  167.3 5.7 %shard_map.108 = (f32[384,768]{1,0:T(8,128)}, f32[384,256]{1,0:T(8,128)S(1)}) custom-call(s32[3]{0:T(128)S(1)} %pad_add_fusion.z_ref.refs_0_.s_ref, bf16[8,2,32,384]{3,2,1,0:T(8,128)(2,1)S(1)} %get-tuple-element.39.refs_1_, bf16[8,2,32,384]{3,2,1,0:T(8,128)(2,1)S(1)} %get-tuple-element.38.refs_2_, bf16[8,2,32,384]{3,2,1,0:T(8,128)(2,1)S(1)} %copy-done.14, ...), custom_call_target="tpu_custom_call" | custom-call | flops 1000 | bytes 1000 | tf_op jit(solution)/shard_map/pallas_call | solution.py:324
  173.8 6.4 %shard_map.109 = (bf16[3,384,256]{2,1,0:T(8,128)(2,1)}, bf16[384,256]{1,0:T(8,128)(2,1)}) custom-call(s32[3]{0:T(128)S(1)} %pad_add_fusion.z_ref.refs_0_.s_ref, bf16[8,2,32,384]{3,2,1,0:T(8,128)(2,1)S(1)} %copy-done.5, bf16[8,2,32,384]{3,2,1,0:T(8,128)(2,1)S(1)} %copy-done.7, bf16[8,2,32,384]{3,2,1,0:T(8,128)(2,1)S(1)} %copy-done.3, ...), custom_call_target="tpu_custom_call" | custom-call | flops 1000 | bytes 1000 | tf_op jit(solution)/shard_map/pallas_call | solution.py:324
  180.3 10.3 %reduce-scatter.5.cloned.1.call-done = bf16[1024,384]{1,0:T(8,128)(2,1)} async-done(((bf16[8192,384]{1,0:T(8,128)(2,1)}), bf16[1024,384]{1,0:T(8,128)(2,1)}) %reduce-scatter.5.cloned.1.call-update) | async-done | bytes 786448 | tf_op jit(solution)/shard_map/reduce_scatter | solution.py:423
  192.2 11.9 %collective-permute-done.14.recv_ref = bf16[512,384]{1,0:T(8,128)(2,1)S(1)} collective-permute-done((bf16[512,384]{1,0:T(8,128)(2,1)S(1)}, bf16[512,384]{1,0:T(8,128)(2,1)S(1)}, u32[]{:S(2)}, u32[]{:S(2)}) %collective-permute-start.14) | collective-permute-done | bytes 393248 | tf_op jit(solution)/shard_map/ppermute | solution.py:346
  204.2 1.1 copy-done.1
  205.3 1.6 shard_map.111
  (100 shorter events, 15.9 us)
Async XLA Ops:
  8.0 84.5 %reduce-scatter.3.cloned.1.call-start = ((), (), s32[]{:S(2)}) async-start(), calls=%async_computation.4 | async-start | bytes 1179648 | tf_op jit(solution)/shard_map/reduce_scatter | solution.py:410
  11.0 81.8 %all-gather.5.cloned.1.call-start = ((), (), s32[]{:S(2)}) async-start(), calls=%async_computation.6 | async-start | bytes 13369344 | tf_op jit(solution)/shard_map/all_gather | solution.py:409
  11.6 155.7 %all-gather.7.cloned.1.call-start = ((), (), s32[]{:S(2)}) async-start(), calls=%async_computation.7 | async-start | bytes 8912896 | tf_op jit(solution)/shard_map/all_gather | solution.py:422
  14.5 78.2 %copy-start.29 = (f32[256]{0:T(256)S(1)}, f32[256]{0:T(256)}, u32[]{:S(2)}) copy-start(f32[256]{0:T(256)} %param.11) | copy-start | bytes 3076
  14.5 78.2 %copy-start.30 = (f32[256]{0:T(256)S(1)}, f32[256]{0:T(256)}, u32[]{:S(2)}) copy-start(f32[256]{0:T(256)} %param.12) | copy-start | bytes 3076
  32.8 17.9 %collective-permute-start = (bf16[8,2,32,384]{3,2,1,0:T(8,128)(2,1)S(1)}, bf16[8,2,32,384]{3,2,1,0:T(8,128)(2,1)S(1)}, u32[]{:S(2)}, u32[]{:S(2)}) collective-permute-start(bf16[8,2,32,384]{3,2,1,0:T(8,128)(2,1)S(1)} %get-tuple-element.39.refs_1_), channel_id=1, source_target_pairs={{0,2},{2,4},{4,6},{6,8},{8,10},{10,12},{12,14},{14,0},{1,3},{3,5},... | collective-permute-start | bytes 1179656 | tf_op jit(solution)/shard_map/ppermute | solution.py:342
  34.8 15.8 %collective-permute-start.1 = (bf16[8,2,32,384]{3,2,1,0:T(8,128)(2,1)S(1)}, bf16[8,2,32,384]{3,2,1,0:T(8,128)(2,1)S(1)}, u32[]{:S(2)}, u32[]{:S(2)}) collective-permute-start(bf16[8,2,32,384]{3,2,1,0:T(8,128)(2,1)S(1)} %get-tuple-element.39.refs_1_), channel_id=1, source_target_pairs={{0,14},{2,0},{4,2},{6,4},{8,6},{10,8},{12,10},{14,12},{1,15},{3,1}... | collective-permute-start | bytes 1179656 | tf_op jit(solution)/shard_map/ppermute | solution.py:342
  41.0 17.4 %collective-permute-start.6 = (bf16[8,2,32,384]{3,2,1,0:T(8,128)(2,1)S(1)}, bf16[8,2,32,384]{3,2,1,0:T(8,128)(2,1)}, u32[]{:S(2)}, u32[]{:S(2)}) collective-permute-start(bf16[8,2,32,384]{3,2,1,0:T(8,128)(2,1)S(1)} %get-tuple-element.38.refs_2_), channel_id=1, source_target_pairs={{0,14},{2,0},{4,2},{6,4},{8,6},{10,8},{12,10},{14,12},{1,15},{3,1}... | collective-permute-start | bytes 1179656 | tf_op jit(solution)/shard_map/ppermute | solution.py:342
  50.6 13.2 %collective-permute-start.3 = (bf16[8,2,32,384]{3,2,1,0:T(8,128)(2,1)S(1)}, bf16[8,2,32,384]{3,2,1,0:T(8,128)(2,1)S(1)}, u32[]{:S(2)}, u32[]{:S(2)}) collective-permute-start(bf16[8,2,32,384]{3,2,1,0:T(8,128)(2,1)S(1)} %get-tuple-element.38.refs_2_), channel_id=1, source_target_pairs={{0,2},{2,4},{4,6},{6,8},{8,10},{10,12},{12,14},{14,0},{1,3},{3,5},... | collective-permute-start | bytes 1179656 | tf_op jit(solution)/shard_map/ppermute | solution.py:342
  51.6 20.7 %collective-permute-start.2 = (bf16[8,2,32,384]{3,2,1,0:T(8,128)(2,1)}, bf16[8,2,32,384]{3,2,1,0:T(8,128)(2,1)S(1)}, u32[]{:S(2)}, u32[]{:S(2)}) collective-permute-start(bf16[8,2,32,384]{3,2,1,0:T(8,128)(2,1)} %get-tuple-element.22.refs_3_), channel_id=1, source_target_pairs={{0,2},{2,4},{4,6},{6,8},{8,10},{10,12},{12,14},{14,0},{1,3},{3,5},... | collective-permute-start | bytes 1179656 | tf_op jit(solution)/shard_map/ppermute | solution.py:342
  58.4 13.8 %collective-permute-start.7 = (bf16[8,2,32,384]{3,2,1,0:T(8,128)(2,1)}, bf16[8,2,32,384]{3,2,1,0:T(8,128)(2,1)S(1)}, u32[]{:S(2)}, u32[]{:S(2)}) collective-permute-start(bf16[8,2,32,384]{3,2,1,0:T(8,128)(2,1)} %collective-permute-done.6.refs_8_), channel_id=1, source_target_pairs={{0,14},{2,0},{4,2},{6,4},{8,6},{10,8},{12,10},{14,12},{1,15},{3,1}... | collective-permute-start | bytes 1179656 | tf_op jit(solution)/shard_map/ppermute | solution.py:342
  62.2 18.2 %collective-permute-start.5 = (bf16[8,2,32,384]{3,2,1,0:T(8,128)(2,1)}, bf16[8,2,32,384]{3,2,1,0:T(8,128)(2,1)S(1)}, u32[]{:S(2)}, u32[]{:S(2)}) collective-permute-start(bf16[8,2,32,384]{3,2,1,0:T(8,128)(2,1)} %get-tuple-element.23.refs_7_), channel_id=1, source_target_pairs={{0,14},{2,0},{4,2},{6,4},{8,6},{10,8},{12,10},{14,12},{1,15},{3,1}... | collective-permute-start | bytes 1179656 | tf_op jit(solution)/shard_map/ppermute | solution.py:342
  63.8 20.2 %collective-permute-start.4 = (bf16[8,2,32,384]{3,2,1,0:T(8,128)(2,1)S(1)}, bf16[8,2,32,384]{3,2,1,0:T(8,128)(2,1)S(1)}, u32[]{:S(2)}, u32[]{:S(2)}) collective-permute-start(bf16[8,2,32,384]{3,2,1,0:T(8,128)(2,1)S(1)} %collective-permute-done.3.refs_4_), channel_id=1, source_target_pairs={{0,2},{2,4},{4,6},{6,8},{8,10},{10,12},{12,14},{14,0},{1,3},{3,5},... | collective-permute-start | bytes 1179656 | tf_op jit(solution)/shard_map/ppermute | solution.py:342
  72.2 17.0 %collective-permute-start.8 = (bf16[8,2,32,384]{3,2,1,0:T(8,128)(2,1)S(1)}, bf16[8,2,32,384]{3,2,1,0:T(8,128)(2,1)}, u32[]{:S(2)}, u32[]{:S(2)}) collective-permute-start(bf16[8,2,32,384]{3,2,1,0:T(8,128)(2,1)S(1)} %collective-permute-done.2.rest_0_.refs_5_), channel_id=1, source_target_pairs={{0,2},{2,4},{4,6},{6,8},{8,10},{10,12},{12,14},{14,0},{1,3},{3,5},... | collective-permute-start | bytes 1179656 | tf_op jit(solution)/shard_map/ppermute | solution.py:342
  72.3 16.9 %collective-permute-start.9 = (bf16[8,2,32,384]{3,2,1,0:T(8,128)(2,1)S(1)}, bf16[8,2,32,384]{3,2,1,0:T(8,128)(2,1)}, u32[]{:S(2)}, u32[]{:S(2)}) collective-permute-start(bf16[8,2,32,384]{3,2,1,0:T(8,128)(2,1)S(1)} %collective-permute-done.7.rest_3_.refs_6_), channel_id=1, source_target_pairs={{0,14},{2,0},{4,2},{6,4},{8,6},{10,8},{12,10},{14,12},{1,15},{3,1}... | collective-permute-start | bytes 1179656 | tf_op jit(solution)/shard_map/ppermute | solution.py:342
  80.4 28.6 %collective-permute-start.13 = (bf16[8,2,32,384]{3,2,1,0:T(8,128)(2,1)S(1)}, bf16[8,2,32,384]{3,2,1,0:T(8,128)(2,1)S(1)}, u32[]{:S(2)}, u32[]{:S(2)}) collective-permute-start(bf16[8,2,32,384]{3,2,1,0:T(8,128)(2,1)S(1)} %collective-permute-done.5.rest_2_.refs_5_), channel_id=1, source_target_pairs={{0,14},{2,0},{4,2},{6,4},{8,6},{10,8},{12,10},{14,12},{1,15},{3,1}... | collective-permute-start | bytes 1179656 | tf_op jit(solution)/shard_map/ppermute | solution.py:342
  84.0 25.0 %collective-permute-start.12 = (bf16[8,2,32,384]{3,2,1,0:T(8,128)(2,1)S(1)}, bf16[8,2,32,384]{3,2,1,0:T(8,128)(2,1)}, u32[]{:S(2)}, u32[]{:S(2)}) collective-permute-start(bf16[8,2,32,384]{3,2,1,0:T(8,128)(2,1)S(1)} %collective-permute-done.4.rest_1_.refs_6_), channel_id=1, source_target_pairs={{0,2},{2,4},{4,6},{6,8},{8,10},{10,12},{12,14},{14,0},{1,3},{3,5},... | collective-permute-start | bytes 1179656 | tf_op jit(solution)/shard_map/ppermute | solution.py:342
  89.2 19.8 %collective-permute-start.10 = (bf16[8,2,32,384]{3,2,1,0:T(8,128)(2,1)}, bf16[8,2,32,384]{3,2,1,0:T(8,128)(2,1)S(1)}, u32[]{:S(2)}, u32[]{:S(2)}) collective-permute-start(bf16[8,2,32,384]{3,2,1,0:T(8,128)(2,1)} %collective-permute-done.8.rest_4_.refs_7_), channel_id=1, source_target_pairs={{0,2},{2,4},{4,6},{6,8},{8,10},{10,12},{12,14},{14,0},{1,3},{3,5},... | collective-permute-start | bytes 1179656 | tf_op jit(solution)/shard_map/ppermute | solution.py:342
  89.2 19.8 %collective-permute-start.11 = (bf16[8,2,32,384]{3,2,1,0:T(8,128)(2,1)}, bf16[8,2,32,384]{3,2,1,0:T(8,128)(2,1)S(1)}, u32[]{:S(2)}, u32[]{:S(2)}) collective-permute-start(bf16[8,2,32,384]{3,2,1,0:T(8,128)(2,1)} %collective-permute-done.9.rest_5_.refs_4_), channel_id=1, source_target_pairs={{0,14},{2,0},{4,2},{6,4},{8,6},{10,8},{12,10},{14,12},{1,15},{3,1}... | collective-permute-start | bytes 1179656 | tf_op jit(solution)/shard_map/ppermute | solution.py:342
  110.0 57.2 %copy-start.14 = (bf16[8,2,32,384]{3,2,1,0:T(8,128)(2,1)S(1)}, bf16[8,2,32,384]{3,2,1,0:T(8,128)(2,1)}, u32[]{:S(2)}) copy-start(bf16[8,2,32,384]{3,2,1,0:T(8,128)(2,1)} %get-tuple-element.22.refs_3_) | copy-start | bytes 1179652
  110.0 57.2 %copy-start.17 = (bf16[8,2,32,384]{3,2,1,0:T(8,128)(2,1)S(1)}, bf16[8,2,32,384]{3,2,1,0:T(8,128)(2,1)}, u32[]{:S(2)}) copy-start(bf16[8,2,32,384]{3,2,1,0:T(8,128)(2,1)} %copy-done.16) | copy-start | bytes 1179652
  110.1 80.5 %reduce-scatter.5.cloned.1.call-start = ((), (), s32[]{:S(2)}) async-start(), calls=%async_computation.5 | async-start | bytes 7077888 | tf_op jit(solution)/shard_map/reduce_scatter | solution.py:423
  111.5 20.2 %all-to-all-start.1 = ((f32[16,8,256]{2,1,0:T(8,128)}), f32[16,8,256]{2,1,0:T(8,128)S(1)}, u32[]{:S(2)}, u32[]{:S(2)}) async-start(f32[16,8,256]{2,1,0:T(8,128)} %broadcast_in_dim.2), calls=%async_computation.3 | async-start | bytes 262144 | tf_op jit(solution)/shard_map/all_to_all | solution.py:362
  191.6 12.6 %collective-permute-start.14 = (bf16[512,384]{1,0:T(8,128)(2,1)S(1)}, bf16[512,384]{1,0:T(8,128)(2,1)S(1)}, u32[]{:S(2)}, u32[]{:S(2)}) collective-permute-start(bf16[512,384]{1,0:T(8,128)(2,1)S(1)} %dynamic-slice_bitcast_fusion), channel_id=1, source_target_pairs={{0,1},{1,0},{2,3},{3,2},{4,5},{5,4},{6,7},{7,6},{8,9},{9,8},{10,11... | collective-permute-start | bytes 1179656 | tf_op jit(solution)/shard_map/ppermute | solution.py:346
  (28 other events, 314.8 us)
Sparse Core Ops, SparseCore 0:
  11.3 16.3 reduce-scatter.2
  113.6 76.8 reduce-scatter.4
Sparse Core Ops, SparseCore 1:
  13.5 79.3 all-gather.4
  110.1 57.1 all-gather.6

commit v6 on v4

--- a/solution.py
+++ b/solution.py
@@ -17,7 +17,7 @@
 D = 6144
 SUB = ROWS // NZ
 EXT = ROWS + 16
-KSTEP = 4
+KSTEP = 2
 COST = pl.CostEstimate(flops=1000, bytes_accessed=1000, transcendentals=0)
 VMEM = 52 * 1024 * 1024
 BF = jnp.bfloat16

time: 215 us -> 215 us (level)
  transfers between devices with their start and end apart: 20 -> 20, of which waited for: 10 -> 10; matrix products, arithmetic and copies ran while one was open for 1% -> 1% of each run, Pallas kernels for 17% -> 16%
where the time goes in v6:
time: 215 us; the launch traced here: 214 us
  waiting for transfers between devices  92.7 us (43%)
  starting transfers between devices  37.8 us (18%)
  Pallas kernels  37.8 us (18%)
  blocking collectives  18.1 us (8%)
  between operations  15.7 us (7%)
  local copies, waits for them, and re-layouts  8.95 us (4%)
  other arithmetic  2.81 us (1%)
    all_gather x1, waiting for transfers between devices, local(): all_grads = lax.all_gather(grads, DP, axis=0)  34.9 us
    ppermute x14, starting transfers between devices, shift(): return lax.ppermute(a, 'z', [(i, (i + k) % NZ) for i in range(NZ)])  25.7 us
    ppermute x14, waiting for transfers between devices, shift(): return lax.ppermute(a, 'z', [(i, (i + k) % NZ) for i in range(NZ)])  24.8 us
    all_to_all x1, blocking collectives, local(): moved = ring_gather(lax.all_to_all(rows, DP, 0, 0, tiled=True), hid)  18.1 us
    pallas_call x1, Pallas kernels, core_call(): pl.pallas_call(core_kernel, in_specs=[ANY] * 3 + [full((1, HW)), full((1,...  15.1 us
    ppermute x1, waiting for transfers between devices, swap_yh(): return lax.ppermute(a, 'yh', [(0, 1), (1, 0)])  11.9 us
    pallas_call x2, Pallas kernels, weight_call(): pl.pallas_call(lambda *refs: weight_kernel(part, *refs), grid_spec=pltpu....  11.8 us
    all_to_all x1, starting transfers between devices, all_sum(): return jnp.sum(lax.all_to_all(x, MP, 0, 0, tiled=True), 0)  11.3 us
  transfers between devices with their start and end apart: 20, of which 10 were waited for; matrix products, arithmetic and copies ran while one was open for 1% of the time, Pallas kernels for 16%

profile of v6, /device:TPU:16, one launch (start us, length us, event | category | flops | bytes accessed | tf_op | source)
XLA Modules:
  0.0 214.0 jit_solution(709028925509344436)
XLA Ops:
  8.0 2.1 pad_maximum_fusion
  11.6 2.1 shard_map.103
  13.8 18.1 %all_to_all.10 = bf16[16,2,32,384]{3,2,1,0:T(8,128)(2,1)S(1)} all-to-all(bf16[16,2,32,384]{3,2,1,0:T(8,128)(2,1)S(1)} %shard_map.103), channel_id=1, replica_groups=mesh['x'=4,'yl'=2,'c'=2,'z'=8,'yh'=2] {'x','yl','c'}, dimensions={0} | all-to-all | bytes 1572864 | tf_op jit(solution)/shard_map/all_to_all | solution.py:393
  32.0 2.0 collective-permute-start
  34.0 6.2 %collective-permute-start.1 = (bf16[8,2,32,384]{3,2,1,0:T(8,128)(2,1)S(1)}, bf16[8,2,32,384]{3,2,1,0:T(8,128)(2,1)S(1)}, u32[]{:S(2)}, u32[]{:S(2)}) collective-permute-start(bf16[8,2,32,384]{3,2,1,0:T(8,128)(2,1)S(1)} %get-tuple-element.39.refs_1_), channel_id=1, source_target_pairs={{0,14},{2,0},{4,2},{6,4},{8,6},{10,8},{12,10},{14,12},{1,15},{3,1}... | collective-permute-start | bytes 1179656 | tf_op jit(solution)/shard_map/ppermute | solution.py:321
  40.2 1.9 collective-permute-start.6
  42.2 6.3 %shard_map.102 = (bf16[272,6144]{1,0:T(8,128)(2,1)}, f32[256,1]{1,0:T(8,128)S(1)}, f32[256,1]{1,0:T(8,128)S(1)}) custom-call(bf16[256,6144]{1,0:T(8,128)(2,1)} %tok_ref.5, f32[1,6144]{1,0:T(1,128)S(1)} %bitcast.17), custom_call_target="tpu_custom_call" | custom-call | flops 1000 | bytes 1000 | tf_op jit(solution)/shard_map/pallas_call | solution.py:76
  50.7 6.9 %collective-permute-done.6.refs_8_ = bf16[8,2,32,384]{3,2,1,0:T(8,128)(2,1)} collective-permute-done((bf16[8,2,32,384]{3,2,1,0:T(8,128)(2,1)S(1)}, bf16[8,2,32,384]{3,2,1,0:T(8,128)(2,1)}, u32[]{:S(2)}, u32[]{:S(2)}) %collective-permute-start.6) | collective-permute-done | bytes 393248 | tf_op jit(solution)/shard_map/ppermute | solution.py:321
  57.6 3.8 %collective-permute-start.7 = (bf16[8,2,32,384]{3,2,1,0:T(8,128)(2,1)}, bf16[8,2,32,384]{3,2,1,0:T(8,128)(2,1)S(1)}, u32[]{:S(2)}, u32[]{:S(2)}) collective-permute-start(bf16[8,2,32,384]{3,2,1,0:T(8,128)(2,1)} %collective-permute-done.6.refs_8_), channel_id=1, source_target_pairs={{0,14},{2,0},{4,2},{6,4},{8,6},{10,8},{12,10},{14,12},{1,15},{3,1}... | collective-permute-start | bytes 1179656 | tf_op jit(solution)/shard_map/ppermute | solution.py:321
  64.2 7.2 %collective-permute-done.2.rest_0_.refs_5_ = bf16[8,2,32,384]{3,2,1,0:T(8,128)(2,1)S(1)} collective-permute-done((bf16[8,2,32,384]{3,2,1,0:T(8,128)(2,1)}, bf16[8,2,32,384]{3,2,1,0:T(8,128)(2,1)S(1)}, u32[]{:S(2)}, u32[]{:S(2)}) %collective-permute-start.2) | collective-permute-done | bytes 393248 | tf_op jit(solution)/shard_map/ppermute | solution.py:321
  71.5 3.3 %collective-permute-start.9 = (bf16[8,2,32,384]{3,2,1,0:T(8,128)(2,1)S(1)}, bf16[8,2,32,384]{3,2,1,0:T(8,128)(2,1)}, u32[]{:S(2)}, u32[]{:S(2)}) collective-permute-start(bf16[8,2,32,384]{3,2,1,0:T(8,128)(2,1)S(1)} %collective-permute-done.7.rest_3_.refs_6_), channel_id=1, source_target_pairs={{0,14},{2,0},{4,2},{6,4},{8,6},{10,8},{12,10},{14,12},{1,15},{3,1}... | collective-permute-start | bytes 1179656 | tf_op jit(solution)/shard_map/ppermute | solution.py:321
  74.8 4.8 %collective-permute-done.5.rest_2_.refs_5_ = bf16[8,2,32,384]{3,2,1,0:T(8,128)(2,1)S(1)} collective-permute-done((bf16[8,2,32,384]{3,2,1,0:T(8,128)(2,1)}, bf16[8,2,32,384]{3,2,1,0:T(8,128)(2,1)S(1)}, u32[]{:S(2)}, u32[]{:S(2)}) %collective-permute-start.5) | collective-permute-done | bytes 393248 | tf_op jit(solution)/shard_map/ppermute | solution.py:321
  79.6 3.6 %collective-permute-start.13 = (bf16[8,2,32,384]{3,2,1,0:T(8,128)(2,1)S(1)}, bf16[8,2,32,384]{3,2,1,0:T(8,128)(2,1)S(1)}, u32[]{:S(2)}, u32[]{:S(2)}) collective-permute-start(bf16[8,2,32,384]{3,2,1,0:T(8,128)(2,1)S(1)} %collective-permute-done.5.rest_2_.refs_5_), channel_id=1, source_target_pairs={{0,14},{2,0},{4,2},{6,4},{8,6},{10,8},{12,10},{14,12},{1,15},{3,1}... | collective-permute-start | bytes 1179656 | tf_op jit(solution)/shard_map/ppermute | solution.py:321
  83.2 5.2 %collective-permute-done.8.rest_4_.refs_7_ = bf16[8,2,32,384]{3,2,1,0:T(8,128)(2,1)} collective-permute-done((bf16[8,2,32,384]{3,2,1,0:T(8,128)(2,1)S(1)}, bf16[8,2,32,384]{3,2,1,0:T(8,128)(2,1)}, u32[]{:S(2)}, u32[]{:S(2)}) %collective-permute-start.8) | collective-permute-done | bytes 393248 | tf_op jit(solution)/shard_map/ppermute | solution.py:321
  88.4 3.3 %collective-permute-start.11 = (bf16[8,2,32,384]{3,2,1,0:T(8,128)(2,1)}, bf16[8,2,32,384]{3,2,1,0:T(8,128)(2,1)S(1)}, u32[]{:S(2)}, u32[]{:S(2)}) collective-permute-start(bf16[8,2,32,384]{3,2,1,0:T(8,128)(2,1)} %collective-permute-done.9.rest_5_.refs_4_), channel_id=1, source_target_pairs={{0,14},{2,0},{4,2},{6,4},{8,6},{10,8},{12,10},{14,12},{1,15},{3,1}... | collective-permute-start | bytes 1179656 | tf_op jit(solution)/shard_map/ppermute | solution.py:321
  92.0 15.1 %shard_map.105 = (bf16[256,1024]{1,0:T(8,128)(2,1)}, f32[8,256]{1,0:T(8,128)S(1)}, bf16[16,512,384]{2,1,0:T(8,128)(2,1)}) custom-call(bf16[272,6144]{1,0:T(8,128)(2,1)} %get-tuple-element.21.refs_2_.hid_in, bf16[256,6144]{1,0:T(8,128)(2,1)} %cot_in.1, bf16[16,4,384,256]{3,2,1,0:T(8,128)(2,1)} %bitcast.26, f32[1,256]{1,0:T(1,128)S(1)} %bitcast.19, ...), custom_call_target="tpu_custom_call" | custom-call | flops 1000 | bytes 1000 | tf_op jit(solution)/shard_map/pallas_call | solution.py:226
  110.2 11.3 %all-to-all-start.1 = ((f32[16,8,256]{2,1,0:T(8,128)}), f32[16,8,256]{2,1,0:T(8,128)S(1)}, u32[]{:S(2)}, u32[]{:S(2)}) async-start(f32[16,8,256]{2,1,0:T(8,128)} %broadcast_in_dim.10), calls=%async_computation.3 | async-start | bytes 262144 | tf_op jit(solution)/shard_map/all_to_all | solution.py:341
  121.4 9.0 %all-to-all-done.1 = f32[16,8,256]{2,1,0:T(8,128)S(1)} async-done(((f32[16,8,256]{2,1,0:T(8,128)}), f32[16,8,256]{2,1,0:T(8,128)S(1)}, u32[]{:S(2)}, u32[]{:S(2)}) %all-to-all-start.1) | async-done | bytes 131104 | tf_op jit(solution)/shard_map/all_to_all | solution.py:341
  131.0 34.9 %all-gather.7.cloned.1.call-done = bf16[4096,1024]{1,0:T(8,128)(2,1)} async-done(((bf16[256,1024]{1,0:T(8,128)(2,1)}), bf16[4096,1024]{1,0:T(8,128)(2,1)}) %all-gather.7.cloned.1.call-update) | async-done | bytes 8388624 | tf_op jit(solution)/shard_map/all_gather | solution.py:401
  166.0 5.7 %shard_map.107 = (f32[384,768]{1,0:T(8,128)}, f32[384,256]{1,0:T(8,128)S(1)}) custom-call(s32[3]{0:T(128)S(1)} %pad_add_fusion.z_ref.refs_0_.s_ref, bf16[8,2,32,384]{3,2,1,0:T(8,128)(2,1)S(1)} %get-tuple-element.39.refs_1_, bf16[8,2,32,384]{3,2,1,0:T(8,128)(2,1)S(1)} %get-tuple-element.38.refs_2_, bf16[8,2,32,384]{3,2,1,0:T(8,128)(2,1)S(1)} %copy-done.11, ...), custom_call_target="tpu_custom_call" | custom-call | flops 1000 | bytes 1000 | tf_op jit(solution)/shard_map/pallas_call | solution.py:303
  172.4 6.1 %shard_map.108 = (bf16[3,384,256]{2,1,0:T(8,128)(2,1)}, bf16[384,256]{1,0:T(8,128)(2,1)}) custom-call(s32[3]{0:T(128)S(1)} %pad_add_fusion.z_ref.refs_0_.s_ref, bf16[8,2,32,384]{3,2,1,0:T(8,128)(2,1)S(1)} %copy-done.4, bf16[8,2,32,384]{3,2,1,0:T(8,128)(2,1)S(1)} %copy-done.6, bf16[8,2,32,384]{3,2,1,0:T(8,128)(2,1)S(1)} %copy-done.2, ...), custom_call_target="tpu_custom_call" | custom-call | flops 1000 | bytes 1000 | tf_op jit(solution)/shard_map/pallas_call | solution.py:303
  178.5 10.7 %reduce-scatter.5.cloned.1.call-done = bf16[1024,384]{1,0:T(8,128)(2,1)} async-done(((bf16[8192,384]{1,0:T(8,128)(2,1)}), bf16[1024,384]{1,0:T(8,128)(2,1)}) %reduce-scatter.5.cloned.1.call-update) | async-done | bytes 786448 | tf_op jit(solution)/shard_map/reduce_scatter | solution.py:402
  190.9 11.9 %collective-permute-done.14.recv_ref = bf16[512,384]{1,0:T(8,128)(2,1)S(1)} collective-permute-done((bf16[512,384]{1,0:T(8,128)(2,1)S(1)}, bf16[512,384]{1,0:T(8,128)(2,1)S(1)}, u32[]{:S(2)}, u32[]{:S(2)}) %collective-permute-start.14) | collective-permute-done | bytes 393248 | tf_op jit(solution)/shard_map/ppermute | solution.py:325
  204.0 2.6 %shard_map.110 = (bf16[256,384]{1,0:T(8,128)(2,1)}, bf16[256,384]{1,0:T(8,128)(2,1)}) custom-call(s32[3]{0:T(128)S(1)} %pad_add_fusion.z_ref.refs_0_.s_ref, bf16[2,512,384]{2,1,0:T(8,128)(2,1)S(1)} %copy-done, bf16[512,384]{1,0:T(8,128)(2,1)S(1)} %collective-permute-done.14.recv_ref, f32[8,256]{1,0:T(8,128)S(1)} %copy-done.21, bf16[256,6144]{1,0:T(8,128)(2,1)} %tok_ref.5, ...), custom_call_target="tpu_custom_call" | custom-call | flops 1000 | bytes 1000 | tf_op jit(solution)/shard_map/pallas_call | solution.py:359
  (90 shorter events, 14.0 us)
Async XLA Ops:
  8.0 83.7 %reduce-scatter.3.cloned.1.call-start = ((), (), s32[]{:S(2)}) async-start(), calls=%async_computation.4 | async-start | bytes 1179648 | tf_op jit(solution)/shard_map/reduce_scatter | solution.py:389
  10.2 81.8 %all-gather.5.cloned.1.call-start = ((), (), s32[]{:S(2)}) async-start(), calls=%async_computation.6 | async-start | bytes 13369344 | tf_op jit(solution)/shard_map/all_gather | solution.py:388
  10.8 155.2 %all-gather.7.cloned.1.call-start = ((), (), s32[]{:S(2)}) async-start(), calls=%async_computation.7 | async-start | bytes 8912896 | tf_op jit(solution)/shard_map/all_gather | solution.py:401
  13.7 78.2 %copy-start.24 = (f32[256]{0:T(256)S(1)}, f32[256]{0:T(256)}, u32[]{:S(2)}) copy-start(f32[256]{0:T(256)} %param.11) | copy-start | bytes 3076
  13.7 78.2 %copy-start.25 = (f32[256]{0:T(256)S(1)}, f32[256]{0:T(256)}, u32[]{:S(2)}) copy-start(f32[256]{0:T(256)} %param.12) | copy-start | bytes 3076
  32.0 17.8 %collective-permute-start = (bf16[8,2,32,384]{3,2,1,0:T(8,128)(2,1)S(1)}, bf16[8,2,32,384]{3,2,1,0:T(8,128)(2,1)S(1)}, u32[]{:S(2)}, u32[]{:S(2)}) collective-permute-start(bf16[8,2,32,384]{3,2,1,0:T(8,128)(2,1)S(1)} %get-tuple-element.39.refs_1_), channel_id=1, source_target_pairs={{0,2},{2,4},{4,6},{6,8},{8,10},{10,12},{12,14},{14,0},{1,3},{3,5},... | collective-permute-start | bytes 1179656 | tf_op jit(solution)/shard_map/ppermute | solution.py:321
  34.0 15.8 %collective-permute-start.1 = (bf16[8,2,32,384]{3,2,1,0:T(8,128)(2,1)S(1)}, bf16[8,2,32,384]{3,2,1,0:T(8,128)(2,1)S(1)}, u32[]{:S(2)}, u32[]{:S(2)}) collective-permute-start(bf16[8,2,32,384]{3,2,1,0:T(8,128)(2,1)S(1)} %get-tuple-element.39.refs_1_), channel_id=1, source_target_pairs={{0,14},{2,0},{4,2},{6,4},{8,6},{10,8},{12,10},{14,12},{1,15},{3,1}... | collective-permute-start | bytes 1179656 | tf_op jit(solution)/shard_map/ppermute | solution.py:321
  40.2 17.4 %collective-permute-start.6 = (bf16[8,2,32,384]{3,2,1,0:T(8,128)(2,1)S(1)}, bf16[8,2,32,384]{3,2,1,0:T(8,128)(2,1)}, u32[]{:S(2)}, u32[]{:S(2)}) collective-permute-start(bf16[8,2,32,384]{3,2,1,0:T(8,128)(2,1)S(1)} %get-tuple-element.38.refs_2_), channel_id=1, source_target_pairs={{0,14},{2,0},{4,2},{6,4},{8,6},{10,8},{12,10},{14,12},{1,15},{3,1}... | collective-permute-start | bytes 1179656 | tf_op jit(solution)/shard_map/ppermute | solution.py:321
  49.8 13.2 %collective-permute-start.3 = (bf16[8,2,32,384]{3,2,1,0:T(8,128)(2,1)S(1)}, bf16[8,2,32,384]{3,2,1,0:T(8,128)(2,1)S(1)}, u32[]{:S(2)}, u32[]{:S(2)}) collective-permute-start(bf16[8,2,32,384]{3,2,1,0:T(8,128)(2,1)S(1)} %get-tuple-element.38.refs_2_), channel_id=1, source_target_pairs={{0,2},{2,4},{4,6},{6,8},{8,10},{10,12},{12,14},{14,0},{1,3},{3,5},... | collective-permute-start | bytes 1179656 | tf_op jit(solution)/shard_map/ppermute | solution.py:321
  50.7 20.7 %collective-permute-start.2 = (bf16[8,2,32,384]{3,2,1,0:T(8,128)(2,1)}, bf16[8,2,32,384]{3,2,1,0:T(8,128)(2,1)S(1)}, u32[]{:S(2)}, u32[]{:S(2)}) collective-permute-start(bf16[8,2,32,384]{3,2,1,0:T(8,128)(2,1)} %get-tuple-element.22.refs_3_), channel_id=1, source_target_pairs={{0,2},{2,4},{4,6},{6,8},{8,10},{10,12},{12,14},{14,0},{1,3},{3,5},... | collective-permute-start | bytes 1179656 | tf_op jit(solution)/shard_map/ppermute | solution.py:321
  57.6 13.8 %collective-permute-start.7 = (bf16[8,2,32,384]{3,2,1,0:T(8,128)(2,1)}, bf16[8,2,32,384]{3,2,1,0:T(8,128)(2,1)S(1)}, u32[]{:S(2)}, u32[]{:S(2)}) collective-permute-start(bf16[8,2,32,384]{3,2,1,0:T(8,128)(2,1)} %collective-permute-done.6.refs_8_), channel_id=1, source_target_pairs={{0,14},{2,0},{4,2},{6,4},{8,6},{10,8},{12,10},{14,12},{1,15},{3,1}... | collective-permute-start | bytes 1179656 | tf_op jit(solution)/shard_map/ppermute | solution.py:321
  61.4 18.2 %collective-permute-start.5 = (bf16[8,2,32,384]{3,2,1,0:T(8,128)(2,1)}, bf16[8,2,32,384]{3,2,1,0:T(8,128)(2,1)S(1)}, u32[]{:S(2)}, u32[]{:S(2)}) collective-permute-start(bf16[8,2,32,384]{3,2,1,0:T(8,128)(2,1)} %get-tuple-element.23.refs_7_), channel_id=1, source_target_pairs={{0,14},{2,0},{4,2},{6,4},{8,6},{10,8},{12,10},{14,12},{1,15},{3,1}... | collective-permute-start | bytes 1179656 | tf_op jit(solution)/shard_map/ppermute | solution.py:321
  63.0 20.2 %collective-permute-start.4 = (bf16[8,2,32,384]{3,2,1,0:T(8,128)(2,1)S(1)}, bf16[8,2,32,384]{3,2,1,0:T(8,128)(2,1)S(1)}, u32[]{:S(2)}, u32[]{:S(2)}) collective-permute-start(bf16[8,2,32,384]{3,2,1,0:T(8,128)(2,1)S(1)} %collective-permute-done.3.refs_4_), channel_id=1, source_target_pairs={{0,2},{2,4},{4,6},{6,8},{8,10},{10,12},{12,14},{14,0},{1,3},{3,5},... | collective-permute-start | bytes 1179656 | tf_op jit(solution)/shard_map/ppermute | solution.py:321
  71.4 17.0 %collective-permute-start.8 = (bf16[8,2,32,384]{3,2,1,0:T(8,128)(2,1)S(1)}, bf16[8,2,32,384]{3,2,1,0:T(8,128)(2,1)}, u32[]{:S(2)}, u32[]{:S(2)}) collective-permute-start(bf16[8,2,32,384]{3,2,1,0:T(8,128)(2,1)S(1)} %collective-permute-done.2.rest_0_.refs_5_), channel_id=1, source_target_pairs={{0,2},{2,4},{4,6},{6,8},{8,10},{10,12},{12,14},{14,0},{1,3},{3,5},... | collective-permute-start | bytes 1179656 | tf_op jit(solution)/shard_map/ppermute | solution.py:321
  71.5 16.9 %collective-permute-start.9 = (bf16[8,2,32,384]{3,2,1,0:T(8,128)(2,1)S(1)}, bf16[8,2,32,384]{3,2,1,0:T(8,128)(2,1)}, u32[]{:S(2)}, u32[]{:S(2)}) collective-permute-start(bf16[8,2,32,384]{3,2,1,0:T(8,128)(2,1)S(1)} %collective-permute-done.7.rest_3_.refs_6_), channel_id=1, source_target_pairs={{0,14},{2,0},{4,2},{6,4},{8,6},{10,8},{12,10},{14,12},{1,15},{3,1}... | collective-permute-start | bytes 1179656 | tf_op jit(solution)/shard_map/ppermute | solution.py:321
  79.6 28.1 %collective-permute-start.13 = (bf16[8,2,32,384]{3,2,1,0:T(8,128)(2,1)S(1)}, bf16[8,2,32,384]{3,2,1,0:T(8,128)(2,1)S(1)}, u32[]{:S(2)}, u32[]{:S(2)}) collective-permute-start(bf16[8,2,32,384]{3,2,1,0:T(8,128)(2,1)S(1)} %collective-permute-done.5.rest_2_.refs_5_), channel_id=1, source_target_pairs={{0,14},{2,0},{4,2},{6,4},{8,6},{10,8},{12,10},{14,12},{1,15},{3,1}... | collective-permute-start | bytes 1179656 | tf_op jit(solution)/shard_map/ppermute | solution.py:321
  83.2 24.5 %collective-permute-start.12 = (bf16[8,2,32,384]{3,2,1,0:T(8,128)(2,1)S(1)}, bf16[8,2,32,384]{3,2,1,0:T(8,128)(2,1)}, u32[]{:S(2)}, u32[]{:S(2)}) collective-permute-start(bf16[8,2,32,384]{3,2,1,0:T(8,128)(2,1)S(1)} %collective-permute-done.4.rest_1_.refs_6_), channel_id=1, source_target_pairs={{0,2},{2,4},{4,6},{6,8},{8,10},{10,12},{12,14},{14,0},{1,3},{3,5},... | collective-permute-start | bytes 1179656 | tf_op jit(solution)/shard_map/ppermute | solution.py:321
  88.4 19.3 %collective-permute-start.10 = (bf16[8,2,32,384]{3,2,1,0:T(8,128)(2,1)}, bf16[8,2,32,384]{3,2,1,0:T(8,128)(2,1)S(1)}, u32[]{:S(2)}, u32[]{:S(2)}) collective-permute-start(bf16[8,2,32,384]{3,2,1,0:T(8,128)(2,1)} %collective-permute-done.8.rest_4_.refs_7_), channel_id=1, source_target_pairs={{0,2},{2,4},{4,6},{6,8},{8,10},{10,12},{12,14},{14,0},{1,3},{3,5},... | collective-permute-start | bytes 1179656 | tf_op jit(solution)/shard_map/ppermute | solution.py:321
  88.4 19.3 %collective-permute-start.11 = (bf16[8,2,32,384]{3,2,1,0:T(8,128)(2,1)}, bf16[8,2,32,384]{3,2,1,0:T(8,128)(2,1)S(1)}, u32[]{:S(2)}, u32[]{:S(2)}) collective-permute-start(bf16[8,2,32,384]{3,2,1,0:T(8,128)(2,1)} %collective-permute-done.9.rest_5_.refs_4_), channel_id=1, source_target_pairs={{0,14},{2,0},{4,2},{6,4},{8,6},{10,8},{12,10},{14,12},{1,15},{3,1}... | collective-permute-start | bytes 1179656 | tf_op jit(solution)/shard_map/ppermute | solution.py:321
  108.7 57.2 %copy-start.11 = (bf16[8,2,32,384]{3,2,1,0:T(8,128)(2,1)S(1)}, bf16[8,2,32,384]{3,2,1,0:T(8,128)(2,1)}, u32[]{:S(2)}) copy-start(bf16[8,2,32,384]{3,2,1,0:T(8,128)(2,1)} %get-tuple-element.22.refs_3_) | copy-start | bytes 1179652
  108.7 57.2 %copy-start.13 = (bf16[8,2,32,384]{3,2,1,0:T(8,128)(2,1)S(1)}, bf16[8,2,32,384]{3,2,1,0:T(8,128)(2,1)}, u32[]{:S(2)}) copy-start(bf16[8,2,32,384]{3,2,1,0:T(8,128)(2,1)} %copy-done.12) | copy-start | bytes 1179652
  108.7 80.5 %reduce-scatter.5.cloned.1.call-start = ((), (), s32[]{:S(2)}) async-start(), calls=%async_computation.5 | async-start | bytes 7077888 | tf_op jit(solution)/shard_map/reduce_scatter | solution.py:402
  110.2 20.2 %all-to-all-start.1 = ((f32[16,8,256]{2,1,0:T(8,128)}), f32[16,8,256]{2,1,0:T(8,128)S(1)}, u32[]{:S(2)}, u32[]{:S(2)}) async-start(f32[16,8,256]{2,1,0:T(8,128)} %broadcast_in_dim.10), calls=%async_computation.3 | async-start | bytes 262144 | tf_op jit(solution)/shard_map/all_to_all | solution.py:341
  190.2 12.6 %collective-permute-start.14 = (bf16[512,384]{1,0:T(8,128)(2,1)S(1)}, bf16[512,384]{1,0:T(8,128)(2,1)S(1)}, u32[]{:S(2)}, u32[]{:S(2)}) collective-permute-start(bf16[512,384]{1,0:T(8,128)(2,1)S(1)} %dynamic-slice_bitcast_fusion), channel_id=1, source_target_pairs={{0,1},{1,0},{2,3},{3,2},{4,5},{5,4},{6,7},{7,6},{8,9},{9,8},{10,11... | collective-permute-start | bytes 1179656 | tf_op jit(solution)/shard_map/ppermute | solution.py:325
  (23 other events, 246.5 us)
Sparse Core Ops, SparseCore 0:
  11.3 16.3 reduce-scatter.2
  112.3 76.8 reduce-scatter.4
Sparse Core Ops, SparseCore 1:
  12.7 79.3 all-gather.4
  108.8 57.1 all-gather.6
